TPU v7x, 32 devices: a whole 2x2x4 slice. The times are simulated.
32 devices in a mesh: azim: 8 (over y, x, core), axial: 4 (over z).
Axes of the slice: x: 2, y: 2, z: 4, core: 2. Of those that a mesh axis runs over, the one named last changes fastest.
Arguments:
- fraction: float32 [2048, 64, 512], P('azim', 'axial'), may hold values from 0 to 1
- normals: bfloat16 [3, 2048, 64, 512], P(None, 'azim', 'axial'), may hold values from -0.63 to 0.63, as said below
- planes: bfloat16 [2048, 64, 512], P('azim', 'axial'), may hold values from 0 to 1
- cell_flags: int32 [2048, 64, 512], P('azim', 'axial'), may hold values from 0 to 2
- courant: bfloat16 [3, 2048, 64, 512], P(None, 'azim', 'axial'), may hold values from -0.29882812 to 0.29882812
- radial_basis: float32 [512, 512], replicated, may hold values from -0.25 to 0.25
- axial_basis: float32 [64, 64], replicated, may hold values from -0.75 to 0.75
- radial_rates: float32 [512], replicated, may hold values from 0.5 to 4
- axial_rates: float32 [64], replicated, may hold values from 0.2 to 2
Outputs:
- fraction_new: float32 [2048, 64, 512], P('azim', 'axial')
- pressure: float32 [2048, 64, 512], P('azim', 'axial')
Inputs may be any that keep to these rules, and one draw needn't show every extreme that they name: `normals`: every component's magnitude is 0.12 or more, and a cell's three magnitudes sum to 1 within bfloat16 rounding.
All inputs are finite; a program needn't handle non-finite values.
Results may differ from a plain program's by a relative error of at most 0.0003.
Values may be sent and summed in bfloat16 or wider, within the bound.
A program may use at most 256 MiB of HBM per device.

v0:
```python
import functools

import jax
import jax.numpy as jnp
import numpy as np
from jax import lax
from jax.experimental import pallas as pl
from jax.experimental.pallas import tpu as pltpu
from jax.sharding import PartitionSpec as P

HIGH = lax.Precision.HIGH
BUOYANCY = 0.5
CODE_TOP = 32700.0


def shifted_in(edge, axis, towards_lower):
    count = lax.axis_size(axis)
    if towards_lower:
        pairs = [((i + 1) % count, i) for i in range(count)]
    else:
        pairs = [(i, (i + 1) % count) for i in range(count)]
    return lax.ppermute(edge, axis, pairs)


def cell_parts(n0, n1, n2, code):
    m0, m1, m2 = jnp.abs(n0), jnp.abs(n1), jnp.abs(n2)
    return (n0, n1, n2, code, 1.0 / (6.0 * m0 * m1 * m2))


def cube(height):
    held = jnp.maximum(height, 0.0)
    return held * held * held


def face_flux(direction, lower, upper, speed, lower_weight=None, upper_weight=None):
    forward = speed > 0.0
    signed = jnp.where(forward, lower[direction], -upper[direction])
    first, second = [d for d in range(3) if d != direction]
    along = jnp.abs(signed)
    side_a = jnp.abs(jnp.where(forward, lower[first], upper[first]))
    side_b = jnp.abs(jnp.where(forward, lower[second], upper[second]))
    code = jnp.where(forward, lower[3], upper[3])
    inverse = jnp.where(forward, lower[4], upper[4])
    width = jnp.abs(speed)
    near = code - along * jnp.where(signed < 0.0, 0.0, 1.0 - width)
    far = near - along * width
    sides = side_a + side_b
    total = (cube(near) - cube(near - side_a)) - (cube(near - side_b) - cube(near - sides))
    total = total - ((cube(far) - cube(far - side_a)) - (cube(far - side_b) - cube(far - sides)))
    volume = jnp.where(code > 3.0, width, jnp.where(code < -0.5, 0.0, total * inverse))
    if lower_weight is not None:
        volume = volume * jnp.where(forward, lower_weight, upper_weight)
    return jnp.where(forward, volume, jnp.where(speed < 0.0, -volume, 0.0))


def advect_kernel(
    fraction_ref,
    normals_ref,
    planes_ref,
    flags_ref,
    courant_ref,
    next_ref,
    high_ref,
    low_azim_ref,
    low_axial_ref,
    updated_ref,
    source_ref,
    kept,
):
    rows, layers, cells = fraction_ref.shape
    f32 = jnp.float32

    @pl.when(pl.program_id(0) == 0)
    def _():
        kept[...] = low_azim_ref[...]

    index = lax.broadcasted_iota(jnp.int32, (1, cells), 1)
    place = index.astype(f32)
    radius = 1.0 + (place + 0.5) / cells
    next_radius = 1.0 + (place + 1.5) / cells
    face_radius = 1.0 + (place + 1.0) / cells
    inverse_radius = 1.0 / radius
    inner = lax.broadcasted_iota(jnp.int32, (layers, cells), 1) < cells - 1
    layer = lax.broadcasted_iota(jnp.int32, (layers, cells), 0)
    last_layer = layer == layers - 1
    first_layer = layer == 0

    def row_parts(row):
        flags = flags_ref[row]
        code = jnp.where(
            flags == 2, planes_ref[row].astype(f32), jnp.where(flags == 1, 4.0, -1.0)
        )
        return cell_parts(
            normals_ref[0, row].astype(f32),
            normals_ref[1, row].astype(f32),
            normals_ref[2, row].astype(f32),
            code,
        )

    def one_row(row, upper, upper_speed):
        own = row_parts(row)
        moved = [courant_ref[d, row].astype(f32) for d in range(3)]
        speed = 0.5 * (moved[0] + upper_speed)
        flux = face_flux(0, own, upper, speed)
        gained = flux - kept[0]
        divergence = speed - kept[1]
        kept[0] = flux
        kept[1] = speed
        beyond = cell_parts(*[high_ref[k, row] for k in range(4)])
        above = [
            jnp.where(last_layer, high, pltpu.roll(field, layers - 1, 0))
            for field, high in zip(own, beyond)
        ]
        speed = 0.5 * (
            moved[1]
            + jnp.where(last_layer, high_ref[4, row], pltpu.roll(moved[1], layers - 1, 0))
        )
        flux = face_flux(1, own, above, speed)
        gained = gained + (
            flux - jnp.where(first_layer, low_axial_ref[0, row], pltpu.roll(flux, 1, 0))
        )
        divergence = divergence + (
            speed - jnp.where(first_layer, low_axial_ref[1, row], pltpu.roll(speed, 1, 0))
        )
        outer = [pltpu.roll(field, cells - 1, 1) for field in own]
        speed = 0.5 * (moved[2] + pltpu.roll(moved[2], cells - 1, 1))
        speed = jnp.where(inner, speed, 0.0)
        flux = face_flux(2, own, outer, speed, radius, next_radius)
        gained = gained + (flux - pltpu.roll(flux, 1, 1)) * inverse_radius
        carried = face_radius * speed
        divergence = divergence + (carried - pltpu.roll(carried, 1, 1)) * inverse_radius
        updated = fraction_ref[row] - gained
        updated_ref[row] = updated
        source_ref[row] = divergence + BUOYANCY * updated

    def step(row, _):
        one_row(row, row_parts(row + 1), courant_ref[0, row + 1].astype(f32))
        return 0

    lax.fori_loop(0, rows - 1, step, 0)
    one_row(
        rows - 1,
        cell_parts(*[next_ref[k, 0].astype(f32) for k in range(4)]),
        next_ref[4, 0].astype(f32),
    )


def plane_codes(planes, flags):
    return jnp.where(
        flags == 2, planes.astype(jnp.float32), jnp.where(flags == 1, 4.0, -1.0)
    ).astype(jnp.bfloat16)


def packed_edge(normals, planes, flags, courant, direction, pick):
    parts = [pick(normals[d]) for d in range(3)]
    parts.append(plane_codes(pick(planes), pick(flags)))
    parts.append(pick(courant[direction]))
    return jnp.stack(parts)


def low_face(direction, lower, upper):
    lower, upper = lower.astype(jnp.float32), upper.astype(jnp.float32)
    speed = 0.5 * (lower[4] + upper[4])
    flux = face_flux(direction, cell_parts(*lower[:4]), cell_parts(*upper[:4]), speed)
    return jnp.stack([flux, speed])


def advect(fraction, normals, planes, flags, courant):
    rows, layers, cells = fraction.shape
    block = 16 if rows % 16 == 0 else 1
    blocks = rows // block
    fields = (normals, planes, flags, courant)
    top_row = packed_edge(*fields, 0, lambda x: x[rows - 1])
    bottom_row = packed_edge(*fields, 0, lambda x: x[0])
    top_layer = packed_edge(*fields, 1, lambda x: x[:, layers - 1])
    bottom_layer = packed_edge(*fields, 1, lambda x: x[:, 0])
    high_row = shifted_in(bottom_row, "azim", True)
    low_row = shifted_in(top_row, "azim", False)
    high_layer = shifted_in(bottom_layer, "axial", True)
    low_layer = shifted_in(top_layer, "axial", False)
    low_azim = low_face(0, low_row, bottom_row)
    low_axial = low_face(1, low_layer, bottom_layer)[:, :, None]
    high_axial = high_layer.astype(jnp.float32)[:, :, None]
    inside = packed_edge(*fields, 0, lambda x: x[block::block])
    following = jnp.concatenate([inside, high_row[:, None]], axis=1)
    whole = pl.BlockSpec((block, layers, cells), lambda i: (i, 0, 0))
    triple = pl.BlockSpec((3, block, layers, cells), lambda i: (0, i, 0, 0))
    return pl.pallas_call(
        advect_kernel,
        grid=(blocks,),
        in_specs=[
            whole,
            triple,
            whole,
            whole,
            triple,
            pl.BlockSpec((5, 1, layers, cells), lambda i: (0, i, 0, 0)),
            pl.BlockSpec((5, block, 1, cells), lambda i: (0, i, 0, 0)),
            pl.BlockSpec((2, layers, cells), lambda i: (0, 0, 0)),
            pl.BlockSpec((2, block, 1, cells), lambda i: (0, i, 0, 0)),
        ],
        out_specs=[whole, whole],
        out_shape=[jax.ShapeDtypeStruct(fraction.shape, jnp.float32)] * 2,
        scratch_shapes=[pltpu.VMEM((2, layers, cells), jnp.float32)],
        compiler_params=pltpu.CompilerParams(vmem_limit_bytes=40 * 2**20),
    )(
        fraction,
        normals,
        planes,
        flags,
        courant,
        following,
        high_axial,
        low_azim,
        low_axial,
    )


def coded(values):
    most = jnp.max(jnp.abs(values), axis=-1)
    exponent = jnp.clip(jnp.ceil(jnp.log2(most) * 256.0) + 1.0, -30000.0, 30000.0)
    scale = CODE_TOP * jnp.exp2(exponent * (-1.0 / 256.0))
    codes = jnp.round(values * scale[..., None])
    return jnp.clip(codes, -32767.0, 32767.0).astype(jnp.int16), exponent.astype(jnp.int16)


def exchange(values):
    modes, cells = values.shape[1], values.shape[3]
    codes, exponent = coded(values)
    extra = jnp.pad(exponent.transpose(0, 2, 1), ((0, 0), (0, 0), (0, cells - modes)))
    sent = jnp.concatenate([codes, extra[:, None]], axis=1)
    got = lax.all_to_all(sent, ("azim", "axial"), split_axis=0, concat_axis=0, tiled=True)
    exponent = got[:, modes, :, :modes].transpose(0, 2, 1).astype(jnp.float32)
    scale = jnp.exp2(exponent * (1.0 / 256.0)) * (1.0 / CODE_TOP)
    return got[:, :modes].astype(jnp.float32) * scale[..., None]


@functools.lru_cache(None)
def azimuth_tables(total):
    half, quarter = total // 2, total // 4
    place = np.arange(half)

    def table(cosines, sines):
        waves = np.concatenate([cosines, sines])
        angles = 2.0 * np.pi / total * (waves[:, None] * place[None, :] % total)
        rows = np.concatenate(
            [np.cos(angles[: len(cosines)]), np.sin(angles[len(cosines) :])]
        ).astype(np.float32)
        rates = (2.0 - 2.0 * np.cos(2.0 * np.pi * waves / total)).astype(np.float32)
        ends = (waves == 0) | (waves == half)
        return rows, rates, (np.where(ends, 1.0, 2.0) / total).astype(np.float32)

    even = 2 * np.arange(quarter + 1)
    odd = 2 * np.arange(quarter) + 1
    return table(even, even[1:-1]), table(odd, odd)


def stepwise(
    fraction,
    normals,
    planes,
    cell_flags,
    courant,
    radial_basis,
    axial_basis,
    radial_rates,
    axial_rates,
):
    rows, layers, cells = fraction.shape
    around, along = lax.axis_size("azim"), lax.axis_size("axial")
    devices = around * along
    modes = cells // devices
    total = rows * around
    half = total // 2
    updated, source = advect(fraction, normals, planes, cell_flags, courant)
    radial_modes = jnp.einsum("azr,rj->jza", source, radial_basis, precision=HIGH)
    got = exchange(radial_modes.reshape(devices, modes, layers, rows))
    got = got.reshape(around, along, modes, layers, rows).transpose(2, 1, 3, 0, 4)
    got = got.reshape(modes, along * layers, total)
    both = jnp.einsum("jza,zn->jna", got, axial_basis, precision=HIGH)
    first = (lax.axis_index("azim") * along + lax.axis_index("axial")) * modes
    shifts = lax.dynamic_slice_in_dim(radial_rates, first, modes)[:, None] + axial_rates[None, :]
    low, high = both[..., :half], both[..., half:]
    solved = []
    for folded, (table, rates, weight) in zip((low + high, low - high), azimuth_tables(total)):
        coefficients = jnp.einsum("jna,ka->jnk", folded, table, precision=HIGH)
        scaled = coefficients / (rates + shifts[..., None]) * weight
        solved.append(jnp.einsum("jnk,ka->jna", scaled, table, precision=HIGH))
    physical = jnp.concatenate([solved[0] + solved[1], solved[0] - solved[1]], axis=-1)
    physical = jnp.einsum("jna,zn->jza", physical, axial_basis, precision=HIGH)
    physical = physical.reshape(modes, along, layers, around, rows).transpose(3, 1, 0, 2, 4)
    returned = exchange(physical.reshape(devices, modes, layers, rows))
    returned = returned.reshape(cells, layers, rows)
    pressure = jnp.einsum("jza,rj->azr", returned, radial_basis, precision=HIGH)
    return (updated, pressure)


CHUNK = 128
BLOCK = 16
FLUX_SCALE = 32767.0 / 0.3
F32 = jnp.float32
BF16 = jnp.bfloat16


def split(values):
    high = values.astype(BF16)
    return high, (values - high.astype(F32)).astype(BF16)


def dot(a, b, contract):
    return lax.dot_general(a, b, (contract, ((), ())), preferred_element_type=F32)


def dot3(a, b, contract=((1,), (0,))):
    return dot(a[0], b[0], contract) + (dot(a[0], b[1], contract) + dot(a[1], b[0], contract))


def donor_volume(signed, side_a, side_b, plane, inverse, width):
    along = jnp.abs(signed)
    slab = along * width
    near = plane - jnp.maximum(signed, 0.0) * (1.0 - width)
    other = (slab + (side_a + side_b)) - near
    folded = near > other
    held = jnp.maximum(jnp.minimum(near, other), 0.0)
    low, high = jnp.minimum(side_a, side_b), jnp.maximum(side_a, side_b)
    corner = low + slab
    by_low = jnp.maximum(held - low, 0.0)
    by_slab = jnp.maximum(held - slab, 0.0)
    last = jnp.maximum(held - jnp.minimum(high, corner), 0.0)
    last_cube = last * last * last
    last_cube = jnp.where(high < corner, -last_cube, last_cube)
    total = held * held * held - by_slab * by_slab * by_slab
    total = total - (by_low * by_low * by_low - last_cube)
    volume = total * inverse
    return jnp.where(folded, width - volume, volume)


def upwind_flux(direction, lower, upper, speed, lower_weight=None, upper_weight=None):
    forward = speed > 0.0
    first, second = [d for d in range(3) if d != direction]
    signed = jnp.where(forward, lower[direction], -upper[direction])
    side_a = jnp.abs(jnp.where(forward, lower[first], upper[first]))
    side_b = jnp.abs(jnp.where(forward, lower[second], upper[second]))
    plane = jnp.where(forward, lower[3], upper[3])
    inverse = jnp.where(forward, lower[4], upper[4])
    volume = donor_volume(signed, side_a, side_b, plane, inverse, jnp.abs(speed))
    if lower_weight is not None:
        volume = volume * jnp.where(forward, lower_weight, upper_weight)
    return jnp.where(forward, volume, -volume)


def inverse_of(n0, n1, n2):
    return 1.0 / (6.0 * jnp.abs(n0 * n1 * n2))


def plane_value(planes, flags):
    return jnp.where(flags == 2, planes.astype(F32), jnp.where(flags == 1, 4.0, -4.0))


def strided_rows(work, layer, rows, layers, cells):
    parts = []
    for lane in range(0, cells, 128):
        parts.append(work[lane // 128, pl.ds(layer, rows, stride=layers), :])
    return parts


def speeds_kernel(courant_ref, edge_ref, work):
    rows, layers, cells = courant_ref.shape[1:]
    for lane in range(0, cells, 128):
        work[lane // 128] = courant_ref[0, :, :, pl.ds(lane, 128)].astype(F32).reshape(rows * layers, 128)
    for side, layer in ((0, 0), (1, layers - 1)):
        for tile, got in enumerate(strided_rows(work, layer, rows, layers, cells)):
            edge_ref[side, :, pl.ds(tile * 128, 128)] = got.astype(BF16)


def edge_speeds(courant):
    _, rows, layers, cells = courant.shape
    step = 64
    return pl.pallas_call(
        speeds_kernel,
        grid=(rows // step,),
        in_specs=[pl.BlockSpec((1, step, layers, cells), lambda i: (1, i, 0, 0))],
        out_specs=pl.BlockSpec((2, step, cells), lambda i: (0, i, 0)),
        out_shape=jax.ShapeDtypeStruct((2, rows, cells), BF16),
        scratch_shapes=[pltpu.VMEM((cells // 128, step * layers, 128), F32)],
        name="edge_speeds",
    )(courant)


def fields_kernel(normals_ref, planes_ref, flags_ref, fields_ref, work):
    rows, layers, cells = planes_ref.shape
    for k in range(4):
        for lane in range(0, cells, 128):
            at = pl.ds(lane, 128)
            if k < 3:
                field = normals_ref[k, :, :, at].astype(F32)
            else:
                field = plane_value(planes_ref[:, :, at], flags_ref[:, :, at])
            work[lane // 128] = field.reshape(rows * layers, 128)
        for side, layer in ((0, 0), (1, layers - 1)):
            for tile, got in enumerate(strided_rows(work, layer, rows, layers, cells)):
                fields_ref[side, k, :, pl.ds(tile * 128, 128)] = got


def edge_fields(normals, planes, flags):
    rows, layers, cells = planes.shape
    step = 32
    whole = pl.BlockSpec((step, layers, cells), lambda i: (i, 0, 0))
    return pl.pallas_call(
        fields_kernel,
        grid=(rows // step,),
        in_specs=[
            pl.BlockSpec((3, step, layers, cells), lambda i: (0, i, 0, 0)),
            whole,
            whole,
        ],
        out_specs=pl.BlockSpec((2, 4, step, cells), lambda i: (0, 0, i, 0)),
        out_shape=jax.ShapeDtypeStruct((2, 4, rows, cells), F32),
        scratch_shapes=[pltpu.VMEM((cells // 128, step * layers, 128), F32)],
        name="edge_fields",
    )(normals, planes, flags)


def donors_kernel(fields_ref, edge_ref, below_ref, above_ref, own_ref, code_ref, speed_ref):
    for side in range(2):
        n = [fields_ref[side, k] for k in range(3)]
        beyond = (below_ref if side == 0 else above_ref)[...].astype(F32)
        speed = 0.5 * (edge_ref[side].astype(F32) + beyond)
        inverse = inverse_of(*n)
        signed = n[1] if side == 1 else -n[1]
        volume = donor_volume(
            signed, jnp.abs(n[0]), jnp.abs(n[2]), fields_ref[side, 3], inverse, jnp.abs(speed)
        )
        if side == 1:
            flux = jnp.where(speed > 0.0, volume, 0.0)
        else:
            flux = jnp.where(speed < 0.0, -volume, 0.0)
        own_ref[side] = flux
        code_ref[side] = jnp.round(flux * FLUX_SCALE).astype(jnp.int32).astype(jnp.int16)
        speed_ref[side] = speed


def donors(fields, edge, below, above):
    rows, cells = below.shape
    step = 64
    pair = pl.BlockSpec((2, step, cells), lambda i: (0, i, 0))
    one = pl.BlockSpec((step, cells), lambda i: (i, 0))
    shape = (2, rows, cells)
    return pl.pallas_call(
        donors_kernel,
        grid=(rows // step,),
        in_specs=[pl.BlockSpec((2, 4, step, cells), lambda i: (0, 0, i, 0)), pair, one, one],
        out_specs=[pair, pair, pair],
        out_shape=[
            jax.ShapeDtypeStruct(shape, F32),
            jax.ShapeDtypeStruct(shape, jnp.int16),
            jax.ShapeDtypeStruct(shape, F32),
        ],
        name="edge_donors",
    )(fields, edge, below, above)


def rows_kernel(normals_ref, planes_ref, flags_ref, courant_ref, out_ref):
    for k in range(3):
        out_ref[0, k] = normals_ref[k, 0]
    out_ref[0, 3] = plane_value(planes_ref[0], flags_ref[0]).astype(BF16)
    out_ref[0, 4] = courant_ref[0, 0]


def packed_rows(normals, planes, flags, courant, chunk):
    rows, layers, cells = planes.shape

    def place(i):
        return (i // 2) * chunk + (i % 2) * (chunk - 1)

    return pl.pallas_call(
        rows_kernel,
        grid=(2 * (rows // chunk),),
        in_specs=[
            pl.BlockSpec((3, 1, layers, cells), lambda i: (0, place(i), 0, 0)),
            pl.BlockSpec((1, layers, cells), lambda i: (place(i), 0, 0)),
            pl.BlockSpec((1, layers, cells), lambda i: (place(i), 0, 0)),
            pl.BlockSpec((1, 1, layers, cells), lambda i: (0, place(i), 0, 0)),
        ],
        out_specs=pl.BlockSpec((1, 5, layers, cells), lambda i: (i, 0, 0, 0)),
        out_shape=jax.ShapeDtypeStruct((2 * (rows // chunk), 5, layers, cells), BF16),
        name="packed_rows",
    )(normals, planes, flags, courant)


def exponent_of(most):
    return jnp.clip(jnp.ceil(jnp.log2(jnp.maximum(most, 1e-29)) * 256.0) + 1.0, -25000.0, 30000.0)


def to_codes(values):
    return jnp.round(values).astype(jnp.int32).astype(jnp.int16)


def chunk_kernel(
    around,
    has_base,
    fraction_ref,
    normals_ref,
    planes_ref,
    flags_ref,
    courant_ref,
    next_normals_ref,
    next_planes_ref,
    next_flags_ref,
    next_courant_ref,
    low_ref,
    high_ref,
    axial_flux_ref,
    axial_speed_ref,
    basis_ref,
    *rest,
):
    if has_base:
        rest = rest[1:]
    updated_ref, sent_ref, parts, kept, source, wide, scales = rest
    block, layers, cells = fraction_ref.shape
    steps = pl.num_programs(0)
    step = pl.program_id(0)
    chunk = source.shape[1] // layers
    lane_tiles = cells // 128
    backwards = lax.rem(lax.axis_index("azim"), around // 2) >= around // 4

    def put_parts(slot, normals, plane, speed):
        for k in range(3):
            parts[slot, k] = normals[k]
        parts[slot, 3] = plane
        parts[slot, 4] = inverse_of(*normals)
        parts[slot, 5] = 0.5 * speed

    def put_packed(slot, ref):
        values = [ref[0, k].astype(F32) for k in range(5)]
        put_parts(slot, values[:3], values[3], values[4])

    def own_parts(row, _):
        put_parts(
            row,
            [normals_ref[k, row].astype(F32) for k in range(3)],
            plane_value(planes_ref[row], flags_ref[row]),
            courant_ref[0, row].astype(F32),
        )
        return 0

    lax.fori_loop(0, block, own_parts, 0)

    @pl.when(step < steps - 1)
    def _():
        put_parts(
            block,
            [next_normals_ref[k, 0].astype(F32) for k in range(3)],
            plane_value(next_planes_ref[0], next_flags_ref[0]),
            next_courant_ref[0, 0].astype(F32),
        )

    @pl.when(step == steps - 1)
    def _():
        put_packed(block, high_ref)

    def read_parts(slot):
        return [parts[slot, k] for k in range(5)]

    @pl.when(step == 0)
    def _():
        put_packed(block + 1, low_ref)
        speed = parts[block + 1, 5] + parts[0, 5]
        kept[0] = upwind_flux(0, read_parts(block + 1), read_parts(0), speed)
        kept[1] = speed

    index = lax.broadcasted_iota(jnp.int32, (1, cells), 1)
    place = index.astype(F32)
    radius = 1.0 + (place + 0.5) / cells
    next_radius = 1.0 + (place + 1.5) / cells
    face_radius = 1.0 + (place + 1.0) / cells
    inverse_radius = 1.0 / radius
    inner = lax.broadcasted_iota(jnp.int32, (layers, cells), 1) < cells - 1
    layer = lax.broadcasted_iota(jnp.int32, (layers, cells), 0)
    last_layer = layer == layers - 1
    first_layer = layer == 0

    def one_row(row, _):
        own = read_parts(row)
        speed = parts[row, 5] + parts[row + 1, 5]
        flux = upwind_flux(0, own, read_parts(row + 1), speed)
        gained = flux - kept[0]
        divergence = speed - kept[1]
        kept[0] = flux
        kept[1] = speed

        half = 0.5 * courant_ref[1, row].astype(F32)
        above = [pltpu.roll(field, layers - 1, 0) for field in own]
        speed = half + pltpu.roll(half, layers - 1, 0)
        flux = upwind_flux(1, own, above, speed)
        flux = jnp.where(last_layer, axial_flux_ref[1, row], flux)
        speed = jnp.where(last_layer, axial_speed_ref[1, row], speed)
        gained = gained + (
            flux - jnp.where(first_layer, axial_flux_ref[0, row], pltpu.roll(flux, 1, 0))
        )
        divergence = divergence + (
            speed - jnp.where(first_layer, axial_speed_ref[0, row], pltpu.roll(speed, 1, 0))
        )

        half = 0.5 * courant_ref[2, row].astype(F32)
        outer = [pltpu.roll(field, cells - 1, 1) for field in own]
        speed = jnp.where(inner, half + pltpu.roll(half, cells - 1, 1), 0.0)
        flux = upwind_flux(2, own, outer, speed, radius, next_radius)
        gained = gained + (flux - pltpu.roll(flux, 1, 1)) * inverse_radius
        carried = face_radius * speed
        divergence = divergence + (carried - pltpu.roll(carried, 1, 1)) * inverse_radius
        updated = fraction_ref[row] - gained
        updated_ref[row] = updated
        result = divergence + BUOYANCY * updated
        at = step * block + row
        at = jnp.where(backwards, chunk - 1 - at, at)
        for tile in range(lane_tiles):
            source[tile, pl.ds(at, layers, stride=chunk), :] = result[
                :, tile * 128 : (tile + 1) * 128
            ]
        return 0

    lax.fori_loop(0, block, one_row, 0)

    @pl.when(step == steps - 1)
    def _():
        modes = basis_ref.shape[1]
        scales[...] = jnp.zeros_like(scales)

        def radial(z, _):
            at = pl.ds(pl.multiple_of(z * chunk, chunk), chunk)
            rows = jnp.concatenate([source[tile, at, :] for tile in range(lane_tiles)], axis=1)
            got = dot3((basis_ref[0], basis_ref[1]), split(rows), ((1,), (1,)))
            scales[...] = jnp.maximum(scales[...], jnp.abs(got))
            wide[pl.ds(z, modes, stride=layers), :] = got
            return 0

        lax.fori_loop(0, layers, radial, 0)
        exponent = exponent_of(scales[...])
        devices, _, height, lanes = sent_ref.shape
        share = modes // devices
        codes = exponent.astype(jnp.int32).astype(jnp.int16)
        sent_ref[:, share] = codes.reshape(devices, share, lanes)
        scales[...] = CODE_TOP / jnp.exp2(exponent * (1.0 / 256.0))

        def coding(device, _):
            for mode in range(share):
                row = device * share + mode
                values = wide[pl.ds(pl.multiple_of(row * layers, layers), layers), :]
                sent_ref[device, mode] = to_codes(values * scales[pl.ds(row, 1), :])
            return 0

        lax.fori_loop(0, devices, coding, 0)


def advect_chunk(arrays, low, high, axial_flux, axial_speed, basis, chunk_index, chunk, around, devices, base):
    fraction, normals, planes, flags, courant = arrays
    rows, layers, cells = fraction.shape
    block = BLOCK
    steps = chunk // block
    first = chunk_index * steps
    share = cells // devices

    def here(i):
        return first + i

    def after(i):
        return jnp.minimum((first + i + 1) * block, rows - 1)

    whole = pl.BlockSpec((block, layers, cells), lambda i: (here(i), 0, 0))
    triple = pl.BlockSpec((3, block, layers, cells), lambda i: (0, here(i), 0, 0))
    row = pl.BlockSpec((1, layers, cells), lambda i: (after(i), 0, 0))
    pack = pl.BlockSpec((1, 5, layers, cells), lambda i: (0, 0, 0, 0))
    edge = pl.BlockSpec((2, block, 1, cells), lambda i: (0, here(i), 0, 0))
    in_specs = [
        whole,
        triple,
        whole,
        whole,
        triple,
        pl.BlockSpec((3, 1, layers, cells), lambda i: (0, after(i), 0, 0)),
        row,
        row,
        pl.BlockSpec((1, 1, layers, cells), lambda i: (0, after(i), 0, 0)),
        pack,
        pack,
        edge,
        edge,
        pl.BlockSpec((2, cells, cells), lambda i: (0, 0, 0)),
    ]
    operands = [
        fraction, normals, planes, flags, courant,
        normals, planes, flags, courant,
        low, high, axial_flux, axial_speed, basis,
    ]
    aliases = {}
    if base is not None:
        in_specs.append(pl.BlockSpec(memory_space=pl.ANY))
        operands.append(base)
        aliases = {len(operands) - 1: 0}
    return pl.pallas_call(
        functools.partial(chunk_kernel, around, base is not None),
        grid=(steps,),
        in_specs=in_specs,
        out_specs=[
            whole,
            pl.BlockSpec((devices, share + 1, layers, chunk), lambda i: (0, 0, 0, 0)),
        ],
        out_shape=[
            jax.ShapeDtypeStruct(fraction.shape, F32),
            jax.ShapeDtypeStruct((devices, share + 1, layers, chunk), jnp.int16),
        ],
        scratch_shapes=[
            pltpu.VMEM((block + 2, 6, layers, cells), F32),
            pltpu.VMEM((2, layers, cells), F32),
            pltpu.VMEM((cells // 128, layers * chunk, 128), F32),
            pltpu.VMEM((cells * layers, chunk), F32),
            pltpu.VMEM((cells, chunk), F32),
        ],
        input_output_aliases=aliases,
        compiler_params=pltpu.CompilerParams(vmem_limit_bytes=48 * 2**20),
        cost_estimate=pl.CostEstimate(
            flops=40000 * chunk * layers * cells, bytes_accessed=30 * chunk * layers * cells, transcendentals=0
        ),
        name="advect_chunk",
    )(*operands)


@functools.lru_cache(None)
def folded_tables(total):
    quarter = total // 4
    place = np.arange(quarter) + 0.5

    def halves(x):
        high = x.astype(jnp.bfloat16)
        return np.stack([high, (x - high.astype(np.float64)).astype(jnp.bfloat16)])

    tables, rates, weights = [], [], []
    for waves, wave in (
        (2 * np.arange(quarter), np.cos),
        (2 * np.arange(quarter) + 2, np.sin),
        (2 * np.arange(quarter) + 1, np.cos),
        (2 * np.arange(quarter) + 1, np.sin),
    ):
        doubled = waves[:, None] * (2 * np.arange(quarter) + 1)[None, :] % (2 * total)
        tables.append(wave(np.pi * doubled / total))
        rates.append(2.0 - 2.0 * np.cos(2.0 * np.pi * waves / total))
        weights.append(np.where((waves == 0) | (waves == total // 2), 1.0, 2.0) / total)
    tables = np.stack(tables)
    back = np.stack([halves(t) for t in tables])
    forth = np.stack([halves(t.T) for t in tables])
    return forth, back, np.stack(rates)[:, None].astype(np.float32), np.stack(weights)[:, None].astype(np.float32)


def decoded(values):
    return values.astype(jnp.int32).astype(F32)


def scale_of(codes):
    return jnp.exp2(decoded(codes) * (1.0 / 256.0)) * (1.0 / CODE_TOP)


def solve_kernel(around, along, chunks, group, *refs):
    got = refs[:chunks]
    extra = refs[chunks : 2 * chunks]
    mix, unmix, forth, back, rates, weights, shifts = refs[2 * chunks : 2 * chunks + 7]
    sent, high, low, result, scale, exponents = refs[2 * chunks + 7 :]
    devices, count, layers, lanes = got[0].shape
    share = (sent.shape[1] - 1) // chunks
    pairs = around // 4
    step = pl.program_id(0)
    first = group * share + step * count
    for chunk in range(chunks):
        scale[chunk] = scale_of(extra[chunk][:, 0])

    def spots():
        for pair in range(pairs):
            for chunk in range(chunks):
                mirror = chunks - 1 - chunk
                at = pl.ds((pair * chunks + chunk) * lanes, lanes)
                yield at, (
                    (pair, chunk),
                    (pair + 2 * pairs, chunk),
                    (2 * pairs - 1 - pair, mirror),
                    (4 * pairs - 1 - pair, mirror),
                )

    def fold(index, _):
        mode, axial = index // along, index % along
        rows = pl.ds(pl.multiple_of(index * layers, layers), layers)
        row = pl.ds(first + mode, 1)
        for at, places in spots():
            u0, u1, r0, r1 = [
                decoded(got[chunk][azim * along + axial, mode])
                * scale[chunk, azim * along + axial, row, :]
                for azim, chunk in places
            ]
            e0, o0, e1, o1 = u0 + u1, u0 - u1, r0 + r1, r0 - r1
            for k, folded in enumerate((e0 + e1, e0 - e1, o0 - o1, o0 + o1)):
                high[k, rows, at], low[k, rows, at] = split(folded)
        return 0

    lax.fori_loop(0, count * along, fold, 0)

    def waves(k, _):
        mixed = dot3((mix[0], mix[1]), (high[k], low[k]))
        spectrum = dot3(split(mixed), (forth[k, 0], forth[k, 1]))
        solved = spectrum * weights[k] / (rates[k] + shifts[...])
        physical = dot3(split(solved), (back[k, 0], back[k, 1]))
        result[k] = dot3((unmix[0], unmix[1]), split(physical))
        return 0

    lax.fori_loop(0, 4, waves, 0)

    def unfold(index, _):
        mode, axial = index // along, index % along
        rows = pl.ds(pl.multiple_of(index * layers, layers), layers)
        for at, places in spots():
            ec, es, oc, os = [result[k, rows, at] for k in range(4)]
            e0, e1, o0, o1 = ec + es, ec - es, oc + os, os - oc
            for (azim, chunk), values in zip(places, (e0 + o0, e0 - o0, e1 + o1, e1 - o1)):
                device = azim * along + axial
                slot = chunk * share + step * count + mode
                exponent = exponent_of(jnp.max(jnp.abs(values), axis=0, keepdims=True))
                exponents[device, pl.ds(slot, 1), :] = exponent
                factor = CODE_TOP / jnp.exp2(exponent * (1.0 / 256.0))
                sent[device, slot] = to_codes(values * factor)
        return 0

    lax.fori_loop(0, count * along, unfold, 0)

    @pl.when(step == pl.num_programs(0) - 1)
    def _():
        sent[:, chunks * share] = exponents[...].astype(jnp.int32).astype(jnp.int16)


def solve_group(got, mix, unmix, tables, shifts, group, groups, around, along):
    chunks = len(got)
    devices, slots, layers, lanes = got[0].shape
    modes = slots - 1
    share = modes // groups
    count = 4
    steps = share // count
    rows = count * along * layers
    forth, back, rates, weights = tables
    width = forth.shape[-1]

    def fixed(array):
        return pl.BlockSpec(array.shape, lambda i: (0,) * array.ndim, pipeline_mode=pl.Buffered(1))

    return pl.pallas_call(
        functools.partial(solve_kernel, around, along, chunks, group),
        grid=(steps,),
        in_specs=[
            pl.BlockSpec((devices, count, layers, lanes), lambda i: (0, group * steps + i, 0, 0))
        ]
        * chunks
        + [pl.BlockSpec((devices, 1, layers, lanes), lambda i: (0, modes, 0, 0))] * chunks
        + [fixed(x) for x in (mix, unmix, forth, back, rates, weights)]
        + [pl.BlockSpec((rows, 1), lambda i: (group * steps + i, 0))],
        out_specs=pl.BlockSpec((devices, slots, layers, lanes), lambda i: (0, 0, 0, 0)),
        out_shape=jax.ShapeDtypeStruct((devices, chunks * share + 1, layers, lanes), jnp.int16),
        scratch_shapes=[
            pltpu.VMEM((4, rows, width), BF16),
            pltpu.VMEM((4, rows, width), BF16),
            pltpu.VMEM((4, rows, width), F32),
            pltpu.VMEM((chunks, devices, layers, lanes), F32),
            pltpu.VMEM((devices, layers, lanes), F32),
        ],
        compiler_params=pltpu.CompilerParams(vmem_limit_bytes=48 * 2**20),
        cost_estimate=pl.CostEstimate(
            flops=60 * rows * width * width * steps, bytes_accessed=20 * 2**20, transcendentals=0
        ),
        name="solve_group",
    )(*got, *got, mix, unmix, forth, back, rates, weights, shifts)


def pressure_kernel(around, groups, *refs):
    got = refs[:groups]
    extra = refs[groups : 2 * groups]
    basis, out, flat, wide, scale = refs[2 * groups :]
    devices, share, layers, lanes = got[0].shape
    lane_tiles = out.shape[2] // 128
    chunk = pl.program_id(0)
    backwards = lax.rem(lax.axis_index("azim"), around // 2) >= around // 4
    i = lax.broadcasted_iota(jnp.int32, (lanes, lanes), 0)
    j = lax.broadcasted_iota(jnp.int32, (lanes, lanes), 1)
    turned_place = jnp.where(backwards, lanes - 1, 0) + jnp.where(backwards, -1, 1) * i
    turn = jnp.where(j == turned_place, 1.0, 0.0).astype(BF16)
    for group in range(groups):
        scale[group] = scale_of(extra[group][:, 0])

        def unpack(device, _, group=group):
            for mode in range(share):
                at = pl.multiple_of((device * share + mode) * layers, layers)
                flat[group, pl.ds(at, layers), :] = (
                    decoded(got[group][device, mode])
                    * scale[group, device, pl.ds(chunk * share + mode, 1), :]
                )
            return 0

        lax.fori_loop(0, devices, unpack, 0)

    def radial(z, _):
        total = jnp.zeros((lanes, out.shape[2]), F32)
        for group in range(groups):
            values = split(flat[group, pl.ds(z, devices * share, stride=layers), :])
            turned = [dot(turn, part, ((1,), (1,))).astype(BF16) for part in values]
            total = total + dot3(turned, (basis[0, group], basis[1, group]))
        for tile in range(lane_tiles):
            wide[tile, pl.ds(z, lanes, stride=layers), :] = total[:, tile * 128 : (tile + 1) * 128]
        return 0

    lax.fori_loop(0, layers, radial, 0)
    for tile in range(lane_tiles):
        out[:, :, tile * 128 : (tile + 1) * 128] = wide[tile].reshape(lanes, layers, 128)


def pressure_of(got, basis, around, chunks):
    groups = len(got)
    devices, slots, layers, lanes = got[0].shape
    share = (slots - 1) // chunks
    cells = basis.shape[-1]
    return pl.pallas_call(
        functools.partial(pressure_kernel, around, groups),
        grid=(chunks,),
        in_specs=[pl.BlockSpec((devices, share, layers, lanes), lambda i: (0, i, 0, 0))] * groups
        + [pl.BlockSpec((devices, 1, layers, lanes), lambda i: (0, chunks * share, 0, 0))] * groups
        + [
            pl.BlockSpec(
                basis.shape, lambda i: (0,) * basis.ndim, pipeline_mode=pl.Buffered(1)
            )
        ],
        out_specs=pl.BlockSpec((lanes, layers, cells), lambda i: (i, 0, 0)),
        out_shape=jax.ShapeDtypeStruct((lanes * chunks, layers, cells), F32),
        scratch_shapes=[
            pltpu.VMEM((groups, devices * share * layers, lanes), F32),
            pltpu.VMEM((cells // 128, lanes * layers, 128), F32),
            pltpu.VMEM((groups, devices, layers, lanes), F32),
        ],
        compiler_params=pltpu.CompilerParams(vmem_limit_bytes=48 * 2**20),
        name="pressure_of",
    )(*got, *got, basis)


def halves(values):
    high = lax.reduce_precision(values, 8, 7)
    return jnp.stack([high.astype(BF16), (values - high).astype(BF16)])


def exchanged(sent):
    return lax.all_to_all(sent, ("azim", "axial"), split_axis=0, concat_axis=0, tiled=True)


def following_kernel(values_ref, earlier_ref, out_ref):
    del values_ref, earlier_ref, out_ref


def following(values, earlier):
    anywhere = pl.BlockSpec(memory_space=pl.ANY)
    return pl.pallas_call(
        following_kernel,
        in_specs=[anywhere, anywhere],
        out_specs=anywhere,
        out_shape=jax.ShapeDtypeStruct(values.shape, values.dtype),
        input_output_aliases={0: 0},
        name="following",
    )(values, earlier)


def overlapped(
    fraction,
    normals,
    planes,
    cell_flags,
    courant,
    radial_basis,
    axial_basis,
    radial_rates,
    axial_rates,
):
    rows, layers, cells = fraction.shape
    around, along = lax.axis_size("azim"), lax.axis_size("axial")
    devices = around * along
    modes = cells // devices
    chunks, groups = rows // CHUNK, 2
    edge = edge_speeds(courant)
    below = shifted_in(edge[1], "axial", False)
    above = shifted_in(edge[0], "axial", True)
    packs = packed_rows(normals, planes, cell_flags, courant, CHUNK)
    low_row = shifted_in(packs[-1:], "azim", False)
    high_row = shifted_in(packs[:1], "azim", True)
    fields = edge_fields(normals, planes, cell_flags)
    own, code, speed = donors(fields, edge, below, above)
    from_below = shifted_in(code[1], "axial", False)
    from_above = shifted_in(code[0], "axial", True)
    axial_flux = own + jnp.stack([from_below, from_above]).astype(F32) * (1.0 / FLUX_SCALE)
    axial_flux, axial_speed = axial_flux[:, :, None], speed[:, :, None]
    forward_basis = halves(radial_basis.T)
    arrays = (fraction, normals, planes, cell_flags, courant)
    updated, got = None, []
    for chunk in range(chunks):
        low = low_row if chunk == 0 else packs[2 * chunk - 1 : 2 * chunk]
        high = high_row if chunk == chunks - 1 else packs[2 * chunk + 2 : 2 * chunk + 3]
        updated, sent = advect_chunk(
            arrays, low, high, axial_flux, axial_speed, forward_basis, chunk, CHUNK, around, devices, updated
        )
        got.append(exchanged(following(sent, got[-1]) if got else sent))
    count = jnp.eye(4, dtype=F32)
    mix, unmix = halves(jnp.kron(count, axial_basis.T)), halves(jnp.kron(count, axial_basis))
    first = (lax.axis_index("azim") * along + lax.axis_index("axial")) * modes
    shifts = lax.dynamic_slice_in_dim(radial_rates, first, modes)[:, None] + axial_rates[None, :]
    shifts = shifts.reshape(modes * along * layers, 1)
    tables = [jnp.asarray(x) for x in folded_tables(rows * around)]
    returned = []
    for group in range(groups):
        sent = solve_group(got, mix, unmix, tables, shifts, group, groups, around, along)
        returned.append(exchanged(sent))
    back_basis = radial_basis.T.reshape(devices, groups, modes // groups, cells)
    back_basis = halves(back_basis.transpose(1, 0, 2, 3).reshape(groups, -1, cells))
    pressure = pressure_of(returned, back_basis, around, chunks)
    return (updated, pressure)


def fits(fraction):
    rows, layers, cells = fraction.shape
    around, along = lax.axis_size("azim"), lax.axis_size("axial")
    modes = cells // (around * along)
    chunks = rows // CHUNK
    return (
        rows % CHUNK == 0
        and layers == 16
        and modes == 16
        and modes // 2 * chunks == layers
        and cells % 128 == 0
        and around % 4 == 0
    )


def local(*arguments):
    return overlapped(*arguments) if fits(arguments[0]) else stepwise(*arguments)


def solution(mesh):
    placed = (
        P("azim", "axial", None),
        P(None, "azim", "axial", None),
        P("azim", "axial", None),
        P("azim", "axial", None),
        P(None, "azim", "axial", None),
        P(),
        P(),
        P(),
        P(),
    )
    return jax.shard_map(
        local,
        mesh=mesh,
        in_specs=placed,
        out_specs=(P("azim", "axial", None), P("azim", "axial", None)),
        check_vma=False,
    )
```

profile of v0, /device:TPU:1, one launch (start us, length us, event | category | flops | bytes accessed | tf_op | source)
XLA Modules:
  0.0 410.1 jit_solution(5903277645403288060)
XLA Ops:
  0.6 4.4 %edge_speeds.1.edge_ref = bf16[2,256,512]{2,1,0:T(8,128)(2,1)} custom-call(bf16[3,256,16,512]{3,2,1,0:T(8,128)(2,1)} %next_courant_ref.3), custom_call_target="tpu_custom_call" | custom-call | tf_op jit(solution)/shard_map/edge_speeds/pallas_call | solution.py:379
  5.0 1.8 slice_bitcast_fusion
  6.8 2.1 collective-permute-start.1
  8.9 2.0 collective-permute-start.2
  10.9 2.9 packed_rows.1
  14.9 2.3 collective-permute-start.5
  17.2 13.2 %edge_fields.1.fields_ref = f32[2,4,256,512]{3,2,1,0:T(8,128)} custom-call(bf16[3,256,16,512]{3,2,1,0:T(8,128)(2,1)} %next_normals_ref.3, bf16[256,16,512]{2,1,0:T(8,128)(2,1)} %next_planes_ref.3, s32[256,16,512]{2,1,0:T(8,128)} %next_flags_ref.3), custom_call_target="tpu_custom_call" | custom-call | tf_op jit(solution)/shard_map/edge_fields/pallas_call | solution.py:409
  32.2 5.3 %edge_donors.1 = (f32[2,256,512]{2,1,0:T(8,128)}, s16[2,256,512]{2,1,0:T(8,128)(2,1)}, f32[2,256,512]{2,1,0:T(8,128)}) custom-call(f32[2,4,256,512]{3,2,1,0:T(8,128)} %edge_fields.1.fields_ref, bf16[2,256,512]{2,1,0:T(8,128)(2,1)} %edge_speeds.1.edge_ref, bf16[256,512]{1,0:T(8,128)(2,1)} %copy-done.18, bf16[256,512]{1,0:T(8,128)(2,1)} %copy-done.19), custom_call_target="tpu_custom_call" | custom-call | tf_op jit(solution)/shard_map/edge_donors/pallas_call | solution.py:449
  38.8 3.3 collective-permute-start.4
  43.1 5.5 %collective-permute-done.3 = s16[256,512]{1,0:T(8,128)(2,1)S(1)} collective-permute-done((s16[256,512]{1,0:T(8,128)(2,1)S(1)}, s16[256,512]{1,0:T(8,128)(2,1)S(1)}, u32[]{:S(2)}, u32[]{:S(2)}) %collective-permute-start.3) | collective-permute-done | bytes 262176 | tf_op jit(solution)/shard_map/ppermute | solution.py:22
  48.6 3.1 collective-permute-done.4
  52.7 53.6 %advect_chunk.2 = (f32[256,16,512]{2,1,0:T(8,128)}, s16[32,17,16,128]{3,2,1,0:T(8,128)(2,1)S(1)}) custom-call(f32[256,16,512]{2,1,0:T(8,128)} %fraction_ref.3, bf16[3,256,16,512]{3,2,1,0:T(8,128)(2,1)} %next_normals_ref.3, bf16[256,16,512]{2,1,0:T(8,128)(2,1)} %next_planes_ref.3, s32[256,16,512]{2,1,0:T(8,128)} %next_flags_ref.3, ...), custom_call_target="tpu_custom_call" | custom-call | flops 41943040000 | bytes 31457280 | tf_op jit(solution)/shard_map/advect_chunk/pallas_call | solution.py:702
  106.3 1.4 copy-done.5
  107.7 4.5 %all-to-all-start = ((s16[32,17,16,128]{3,2,1,0:T(8,128)(2,1)}), s16[32,17,16,128]{3,2,1,0:T(8,128)(2,1)S(1)}, u32[]{:S(2)}, u32[]{:S(2)}) async-start(s16[32,17,16,128]{3,2,1,0:T(8,128)(2,1)} %copy-done.5), calls=%async_computation | async-start | bytes 4456448 | tf_op jit(solution)/shard_map/all_to_all | solution.py:953
  112.5 15.7 %collective-permute-done.high_ref = bf16[1,5,16,512]{3,2,1,0:T(8,128)(2,1)S(1)} collective-permute-done((bf16[1,5,16,512]{3,2,1,0:T(8,128)(2,1)S(1)}, bf16[1,5,16,512]{3,2,1,0:T(8,128)(2,1)S(1)}, u32[]{:S(2)}, u32[]{:S(2)}) %collective-permute-start) | collective-permute-done | bytes 81952 | tf_op jit(solution)/shard_map/ppermute | solution.py:22
  128.3 1.2 copy-done.8
  130.7 53.5 %advect_chunk.3 = (f32[256,16,512]{2,1,0:T(8,128)}, s16[32,17,16,128]{3,2,1,0:T(8,128)(2,1)S(1)}) custom-call(f32[256,16,512]{2,1,0:T(8,128)} %fraction_ref.3, bf16[3,256,16,512]{3,2,1,0:T(8,128)(2,1)} %next_normals_ref.3, bf16[256,16,512]{2,1,0:T(8,128)(2,1)} %next_planes_ref.3, s32[256,16,512]{2,1,0:T(8,128)} %next_flags_ref.3, ...), custom_call_target="tpu_custom_call", output_to_operand_aliasing={{0}: (14, {})} | custom-call | flops 41943040000 | bytes 31457280 | tf_op jit(solution)/shard_map/advect_chunk/pallas_call | solution.py:702
  184.2 1.4 copy-done.3
  185.6 1.4 copy-done
  187.0 7.1 %all-to-all-start.1 = ((s16[32,17,16,128]{3,2,1,0:T(8,128)(2,1)}), s16[32,17,16,128]{3,2,1,0:T(8,128)(2,1)}, u32[]{:S(2)}, u32[]{:S(2)}) async-start(s16[32,17,16,128]{3,2,1,0:T(8,128)(2,1)} %following.1), calls=%async_computation.1 | async-start | bytes 4456448 | tf_op jit(solution)/shard_map/all_to_all | solution.py:953
  196.5 2.1 mul.83
  200.0 45.1 %all-to-all-done.1.refs_1_.refs_3_ = s16[32,17,16,128]{3,2,1,0:T(8,128)(2,1)} async-done(((s16[32,17,16,128]{3,2,1,0:T(8,128)(2,1)}), s16[32,17,16,128]{3,2,1,0:T(8,128)(2,1)}, u32[]{:S(2)}, u32[]{:S(2)}) %all-to-all-start.1) | async-done | bytes 2228256 | tf_op jit(solution)/shard_map/all_to_all | solution.py:953
  245.2 22.1 %solve_group.3 = s16[32,17,16,128]{3,2,1,0:T(8,128)(2,1)S(1)} custom-call(s16[32,17,16,128]{3,2,1,0:T(8,128)(2,1)S(1)} %copy-done.1, s16[32,17,16,128]{3,2,1,0:T(8,128)(2,1)} %all-to-all-done.1.refs_1_.refs_3_, s16[32,17,16,128]{3,2,1,0:T(8,128)(2,1)S(1)} %copy-done.1, s16[32,17,16,128]{3,2,1,0:T(8,128)(2,1)} %all-to-all-done.1.refs_1_.refs_3_, ...), custom_call_target="tpu_custom_call" | custom-call | flops 8053063680 | bytes 20971520 | tf_op jit(solution)/shard_map/solve_group/pallas_call | solution.py:852
  267.3 1.4 copy-done.6
  268.7 3.7 all-to-all-start.3
  272.4 1.6 copy-done.2
  274.0 22.1 %solve_group.2 = s16[32,17,16,128]{3,2,1,0:T(8,128)(2,1)S(1)} custom-call(s16[32,17,16,128]{3,2,1,0:T(8,128)(2,1)S(1)} %copy-done.2, s16[32,17,16,128]{3,2,1,0:T(8,128)(2,1)} %all-to-all-done.1.refs_1_.refs_3_, s16[32,17,16,128]{3,2,1,0:T(8,128)(2,1)S(1)} %copy-done.2, s16[32,17,16,128]{3,2,1,0:T(8,128)(2,1)} %all-to-all-done.1.refs_1_.refs_3_, ...), custom_call_target="tpu_custom_call" | custom-call | flops 8053063680 | bytes 20971520 | tf_op jit(solution)/shard_map/solve_group/pallas_call | solution.py:852
  296.2 1.4 copy-done.4
  297.5 25.9 %all-to-all-done.3.refs_1_.refs_3_ = s16[32,17,16,128]{3,2,1,0:T(8,128)(2,1)S(1)} async-done(((s16[32,17,16,128]{3,2,1,0:T(8,128)(2,1)}), s16[32,17,16,128]{3,2,1,0:T(8,128)(2,1)S(1)}, u32[]{:S(2)}, u32[]{:S(2)}) %all-to-all-start.3) | async-done | bytes 2228256 | tf_op jit(solution)/shard_map/all_to_all | solution.py:953
  323.4 3.7 all-to-all-start.2
  327.4 50.8 %all-to-all-done.2.refs_0_.refs_2_ = s16[32,17,16,128]{3,2,1,0:T(8,128)(2,1)} async-done(((s16[32,17,16,128]{3,2,1,0:T(8,128)(2,1)}), s16[32,17,16,128]{3,2,1,0:T(8,128)(2,1)}, u32[]{:S(2)}, u32[]{:S(2)}) %all-to-all-start.2) | async-done | bytes 2228256 | tf_op jit(solution)/shard_map/all_to_all | solution.py:953
  378.2 31.9 %pressure_of.1 = f32[256,16,512]{2,1,0:T(8,128)} custom-call(s16[32,17,16,128]{3,2,1,0:T(8,128)(2,1)} %all-to-all-done.2.refs_0_.refs_2_, s16[32,17,16,128]{3,2,1,0:T(8,128)(2,1)S(1)} %all-to-all-done.3.refs_1_.refs_3_, s16[32,17,16,128]{3,2,1,0:T(8,128)(2,1)} %all-to-all-done.2.refs_0_.refs_2_, s16[32,17,16,128]{3,2,1,0:T(8,128)(2,1)S(1)} %all-to-all-done.3.refs_1_.refs_3_, ...), custom_call_target="tpu_custom_call" | custom-call | tf_op jit(solution)/shard_map/pressure_of/pallas_call | solution.py:925
  (64 shorter events, 11.7 us)
Async XLA Ops:
  6.8 24.0 %collective-permute-start.1 = (bf16[256,512]{1,0:T(8,128)(2,1)}, bf16[256,512]{1,0:T(8,128)(2,1)S(1)}, u32[]{:S(2)}, u32[]{:S(2)}) collective-permute-start(bf16[256,512]{1,0:T(8,128)(2,1)} %get-tuple-element.23), channel_id=1, source_target_pairs={{0,1},{1,2},{2,3},{3,0},{4,5},{5,6},{6,7},{7,4},{8,9},{9,10},{10,1... | collective-permute-start | bytes 786440 | tf_op jit(solution)/shard_map/ppermute | solution.py:22
  8.9 21.9 %collective-permute-start.2 = (bf16[256,512]{1,0:T(8,128)(2,1)S(1)}, bf16[256,512]{1,0:T(8,128)(2,1)S(1)}, u32[]{:S(2)}, u32[]{:S(2)}) collective-permute-start(bf16[256,512]{1,0:T(8,128)(2,1)S(1)} %get-tuple-element.22), channel_id=1, source_target_pairs={{1,0},{2,1},{3,2},{0,3},{5,4},{6,5},{7,6},{4,7},{9,8},{10,9},{11,1... | collective-permute-start | bytes 786440 | tf_op jit(solution)/shard_map/ppermute | solution.py:22
  14.8 15.6 %copy-start.15 = (f32[512,512]{1,0:T(8,128)S(1)}, f32[512,512]{1,0:T(8,128)}, u32[]{:S(2)}) copy-start(f32[512,512]{1,0:T(8,128)} %param.18) | copy-start | bytes 3145732
  14.9 37.9 %collective-permute-start.5 = (bf16[1,5,16,512]{3,2,1,0:T(8,128)(2,1)S(1)}, bf16[1,5,16,512]{3,2,1,0:T(8,128)(2,1)S(1)}, u32[]{:S(2)}, u32[]{:S(2)}) collective-permute-start(bf16[1,5,16,512]{3,2,1,0:T(8,128)(2,1)S(1)} %get-tuple-element.25), channel_id=1, source_target_pairs={{0,4},{4,8},{8,12},{12,16},{16,20},{20,24},{24,28},{28,0},{1,5},{5... | collective-permute-start | bytes 245768 | tf_op jit(solution)/shard_map/ppermute | solution.py:22
  30.8 11.5 %copy-start.13 = (f32[512,512]{0,1:T(8,128)}, f32[512,512]{0,1:T(8,128)S(1)}, u32[]{:S(2)}) copy-start(f32[512,512]{0,1:T(8,128)S(1)} %copy.20) | copy-start | bytes 3145732
  30.8 0.7 copy-start.18
  31.5 0.7 copy-start.19
  37.5 4.8 %copy-start.17 = (f32[2,256,512]{2,1,0:T(8,128)S(1)}, f32[2,256,512]{2,1,0:T(8,128)}, u32[]{:S(2)}) copy-start(f32[2,256,512]{2,1,0:T(8,128)} %get-tuple-element.11) | copy-start | bytes 3145732
  37.5 14.2 %copy-start.16 = (f32[2,256,512]{2,1,0:T(8,128)S(1)}, f32[2,256,512]{2,1,0:T(8,128)}, u32[]{:S(2)}) copy-start(f32[2,256,512]{2,1,0:T(8,128)} %get-tuple-element.9) | copy-start | bytes 3145732
  38.8 9.9 %collective-permute-start.3 = (s16[256,512]{1,0:T(8,128)(2,1)S(1)}, s16[256,512]{1,0:T(8,128)(2,1)S(1)}, u32[]{:S(2)}, u32[]{:S(2)}) collective-permute-start(s16[256,512]{1,0:T(8,128)(2,1)S(1)} %get-tuple-element.20), channel_id=1, source_target_pairs={{0,1},{1,2},{2,3},{3,0},{4,5},{5,6},{6,7},{7,4},{8,9},{9,10},{10,1... | collective-permute-start | bytes 786440 | tf_op jit(solution)/shard_map/ppermute | solution.py:22
  38.8 13.0 %collective-permute-start.4 = (s16[256,512]{1,0:T(8,128)(2,1)S(1)}, s16[256,512]{1,0:T(8,128)(2,1)S(1)}, u32[]{:S(2)}, u32[]{:S(2)}) collective-permute-start(s16[256,512]{1,0:T(8,128)(2,1)S(1)} %get-tuple-element.21), channel_id=1, source_target_pairs={{1,0},{2,1},{3,2},{0,3},{5,4},{6,5},{7,6},{4,7},{9,8},{10,9},{11,1... | collective-permute-start | bytes 786440 | tf_op jit(solution)/shard_map/ppermute | solution.py:22
  43.1 63.2 %copy-start.7 = (f32[2,256,1,512]{3,2,1,0:T(1,128)}, f32[2,256,1,512]{3,2,1,0:T(1,128)S(1)}, u32[]{:S(2)}) copy-start(f32[2,256,1,512]{3,2,1,0:T(1,128)S(1)} %broadcast_in_dim.15.axial_speed_ref) | copy-start | bytes 3145732
  52.7 53.6 %copy-start.9 = (f32[2,256,1,512]{3,2,1,0:T(1,128)}, f32[2,256,1,512]{3,2,1,0:T(1,128)S(1)}, u32[]{:S(2)}) copy-start(f32[2,256,1,512]{3,2,1,0:T(1,128)S(1)} %broadcast_in_dim.14.axial_flux_ref) | copy-start | bytes 3145732
  106.3 1.4 copy-start.5
  107.7 77.9 %all-to-all-start = ((s16[32,17,16,128]{3,2,1,0:T(8,128)(2,1)}), s16[32,17,16,128]{3,2,1,0:T(8,128)(2,1)S(1)}, u32[]{:S(2)}, u32[]{:S(2)}) async-start(s16[32,17,16,128]{3,2,1,0:T(8,128)(2,1)} %copy-done.5), calls=%async_computation | async-start | bytes 4456448 | tf_op jit(solution)/shard_map/all_to_all | solution.py:953
  112.2 16.0 %collective-permute-start = (bf16[1,5,16,512]{3,2,1,0:T(8,128)(2,1)S(1)}, bf16[1,5,16,512]{3,2,1,0:T(8,128)(2,1)S(1)}, u32[]{:S(2)}, u32[]{:S(2)}) collective-permute-start(bf16[1,5,16,512]{3,2,1,0:T(8,128)(2,1)S(1)} %get-tuple-element.26), channel_id=1, source_target_pairs={{4,0},{8,4},{12,8},{16,12},{20,16},{24,20},{28,24},{0,28},{5,1},{9... | collective-permute-start | bytes 245768 | tf_op jit(solution)/shard_map/ppermute | solution.py:22
  128.3 1.2 copy-start.8
  129.5 1.2 copy-start.10
  184.2 1.4 copy-start.3
  185.6 1.4 copy-start
  187.0 7.9 %copy-start.21 = (f32[64]{0:T(128)S(1)}, f32[64]{0:T(128)}, u32[]{:S(2)}) copy-start(f32[64]{0:T(128)} %param.21) | copy-start | bytes 772
  187.0 8.5 %copy-start.20 = (f32[64,64]{1,0:T(8,128)S(1)}, f32[64,64]{1,0:T(8,128)}, u32[]{:S(2)}) copy-start(f32[64,64]{1,0:T(8,128)} %param.19) | copy-start | bytes 49156
  187.0 58.2 %copy-start.1 = (s16[32,17,16,128]{3,2,1,0:T(8,128)(2,1)S(1)}, s16[32,17,16,128]{3,2,1,0:T(8,128)(2,1)}, u32[]{:S(2)}) copy-start(s16[32,17,16,128]{3,2,1,0:T(8,128)(2,1)} %copy-done) | copy-start | bytes 6684676
  187.0 58.2 %copy-start.11 = (f32[4,1,512]{2,1,0:T(1,128)S(1)}, f32[4,1,512]{2,1,0:T(1,128)}, u32[]{:S(2)}) copy-start(f32[4,1,512]{2,1,0:T(1,128)} %constant.29.clone.refs_8_) | copy-start | bytes 24580
  187.0 58.2 %copy-start.12 = (f32[4,1,512]{2,1,0:T(1,128)S(1)}, f32[4,1,512]{2,1,0:T(1,128)}, u32[]{:S(2)}) copy-start(f32[4,1,512]{2,1,0:T(1,128)} %constant.30.clone.refs_9_) | copy-start | bytes 24580
  187.0 58.2 %all-to-all-start.1 = ((s16[32,17,16,128]{3,2,1,0:T(8,128)(2,1)}), s16[32,17,16,128]{3,2,1,0:T(8,128)(2,1)}, u32[]{:S(2)}, u32[]{:S(2)}) async-start(s16[32,17,16,128]{3,2,1,0:T(8,128)(2,1)} %following.1), calls=%async_computation.1 | async-start | bytes 4456448 | tf_op jit(solution)/shard_map/all_to_all | solution.py:953
  267.3 1.4 copy-start.6
  268.7 54.7 %all-to-all-start.3 = ((s16[32,17,16,128]{3,2,1,0:T(8,128)(2,1)}), s16[32,17,16,128]{3,2,1,0:T(8,128)(2,1)S(1)}, u32[]{:S(2)}, u32[]{:S(2)}) async-start(s16[32,17,16,128]{3,2,1,0:T(8,128)(2,1)} %copy-done.6), calls=%async_computation.3 | async-start | bytes 4456448 | tf_op jit(solution)/shard_map/all_to_all | solution.py:953
  272.4 1.6 copy-start.2
  296.2 1.4 copy-start.4
  297.5 29.6 %copy-start.14 = (f32[512,512]{0,1:T(8,128)S(1)}, f32[512,512]{0,1:T(8,128)}, u32[]{:S(2)}) copy-start(f32[512,512]{0,1:T(8,128)} %copy-done.13) | copy-start | bytes 3145732
  323.4 54.8 %all-to-all-start.2 = ((s16[32,17,16,128]{3,2,1,0:T(8,128)(2,1)}), s16[32,17,16,128]{3,2,1,0:T(8,128)(2,1)}, u32[]{:S(2)}, u32[]{:S(2)}) async-start(s16[32,17,16,128]{3,2,1,0:T(8,128)(2,1)} %copy-done.4), calls=%async_computation.2 | async-start | bytes 4456448 | tf_op jit(solution)/shard_map/all_to_all | solution.py:953
where the time goes:
time: 411 us; the launch traced here: 410 us
  Pallas kernels  209 us (51%)
  waiting for transfers between devices  146 us (36%)
  starting transfers between devices  29.1 us (7%)
  local copies, waits for them, and re-layouts  22 us (5%)
    all_to_all x4, waiting for transfers between devices, exchanged(): lax.all_to_all(sent, ('azim', 'axial'), split_axis=0, concat_axis=0, tile...  122 us
    pallas_call x2, Pallas kernels, advect_chunk(): pl.pallas_call(functools.partial(chunk_kernel, around, base is not None),...  107 us
    pallas_call x2, Pallas kernels, solve_group(): pl.pallas_call(functools.partial(solve_kernel, around, along, chunks, gro...  44.3 us
    pallas_call x1, Pallas kernels, pressure_of(): pl.pallas_call(functools.partial(pressure_kernel, around, groups), grid=(...  31.9 us
    ppermute x6, waiting for transfers between devices, shifted_in(): return lax.ppermute(edge, axis, pairs)  24.4 us
    all_to_all x4, starting transfers between devices, exchanged(): lax.all_to_all(sent, ('azim', 'axial'), split_axis=0, concat_axis=0, tile...  19 us
    pallas_call x1, Pallas kernels, edge_fields(): pl.pallas_call(fields_kernel, grid=(rows // step,), in_specs=[pl.BlockSpe...  13.2 us
    unnamed x45, local copies, waits for them, and re-layouts  12.8 us
  transfers between devices with their start and end apart: 10, of which 6 were waited for; matrix products, arithmetic and copies ran while one was open for 3% of the time, Pallas kernels for 24%

commit v1 on v0

--- a/solution.py
+++ b/solution.py
@@ -315,38 +315,36 @@
     return dot(a[0], b[0], contract) + (dot(a[0], b[1], contract) + dot(a[1], b[0], contract))
 
 
-def donor_volume(signed, side_a, side_b, plane, inverse, width):
-    along = jnp.abs(signed)
-    slab = along * width
-    near = plane - jnp.maximum(signed, 0.0) * (1.0 - width)
+def slab_flux(normal, side_a, side_b, plane, inverse, speed):
+    along = jnp.abs(normal)
+    reach = normal * speed
+    slab = jnp.abs(reach)
+    near = plane - jnp.where(reach > 0.0, along - slab, 0.0)
     other = (slab + (side_a + side_b)) - near
     folded = near > other
     held = jnp.maximum(jnp.minimum(near, other), 0.0)
     low, high = jnp.minimum(side_a, side_b), jnp.maximum(side_a, side_b)
-    corner = low + slab
     by_low = jnp.maximum(held - low, 0.0)
     by_slab = jnp.maximum(held - slab, 0.0)
-    last = jnp.maximum(held - jnp.minimum(high, corner), 0.0)
-    last_cube = last * last * last
-    last_cube = jnp.where(high < corner, -last_cube, last_cube)
+    last = jnp.maximum(held - (low + slab), 0.0) - jnp.maximum(held - high, 0.0)
     total = held * held * held - by_slab * by_slab * by_slab
-    total = total - (by_low * by_low * by_low - last_cube)
-    volume = total * inverse
-    return jnp.where(folded, width - volume, volume)
+    total = total - (by_low * by_low * by_low - last * last * last)
+    flux = total * inverse
+    return jnp.where(folded, speed - flux, flux)
 
 
 def upwind_flux(direction, lower, upper, speed, lower_weight=None, upper_weight=None):
     forward = speed > 0.0
     first, second = [d for d in range(3) if d != direction]
-    signed = jnp.where(forward, lower[direction], -upper[direction])
+    normal = jnp.where(forward, lower[direction], upper[direction])
     side_a = jnp.abs(jnp.where(forward, lower[first], upper[first]))
     side_b = jnp.abs(jnp.where(forward, lower[second], upper[second]))
     plane = jnp.where(forward, lower[3], upper[3])
-    inverse = jnp.where(forward, lower[4], upper[4])
-    volume = donor_volume(signed, side_a, side_b, plane, inverse, jnp.abs(speed))
+    inverse = jnp.where(forward, lower[4], upper[5])
+    flux = slab_flux(normal, side_a, side_b, plane, inverse, speed)
     if lower_weight is not None:
-        volume = volume * jnp.where(forward, lower_weight, upper_weight)
-    return jnp.where(forward, volume, -volume)
+        flux = flux * jnp.where(forward, lower_weight, upper_weight)
+    return flux
 
 
 def inverse_of(n0, n1, n2):
@@ -427,14 +425,9 @@
         beyond = (below_ref if side == 0 else above_ref)[...].astype(F32)
         speed = 0.5 * (edge_ref[side].astype(F32) + beyond)
         inverse = inverse_of(*n)
-        signed = n[1] if side == 1 else -n[1]
-        volume = donor_volume(
-            signed, jnp.abs(n[0]), jnp.abs(n[2]), fields_ref[side, 3], inverse, jnp.abs(speed)
-        )
-        if side == 1:
-            flux = jnp.where(speed > 0.0, volume, 0.0)
-        else:
-            flux = jnp.where(speed < 0.0, -volume, 0.0)
+        inverse = inverse if side == 1 else -inverse
+        flux = slab_flux(n[1], jnp.abs(n[0]), jnp.abs(n[2]), fields_ref[side, 3], inverse, speed)
+        flux = jnp.where(speed > 0.0 if side == 1 else speed < 0.0, flux, 0.0)
         own_ref[side] = flux
         code_ref[side] = jnp.round(flux * FLUX_SCALE).astype(jnp.int32).astype(jnp.int16)
         speed_ref[side] = speed
@@ -529,8 +522,10 @@
         for k in range(3):
             parts[slot, k] = normals[k]
         parts[slot, 3] = plane
-        parts[slot, 4] = inverse_of(*normals)
-        parts[slot, 5] = 0.5 * speed
+        inverse = inverse_of(*normals)
+        parts[slot, 4] = inverse
+        parts[slot, 5] = -inverse
+        parts[slot, 6] = 0.5 * speed
 
     def put_packed(slot, ref):
         values = [ref[0, k].astype(F32) for k in range(5)]
@@ -561,12 +556,12 @@
         put_packed(block, high_ref)
 
     def read_parts(slot):
-        return [parts[slot, k] for k in range(5)]
+        return [parts[slot, k] for k in range(6)]
 
     @pl.when(step == 0)
     def _():
         put_packed(block + 1, low_ref)
-        speed = parts[block + 1, 5] + parts[0, 5]
+        speed = parts[block + 1, 6] + parts[0, 6]
         kept[0] = upwind_flux(0, read_parts(block + 1), read_parts(0), speed)
         kept[1] = speed
 
@@ -583,7 +578,7 @@
 
     def one_row(row, _):
         own = read_parts(row)
-        speed = parts[row, 5] + parts[row + 1, 5]
+        speed = parts[row, 6] + parts[row + 1, 6]
         flux = upwind_flux(0, own, read_parts(row + 1), speed)
         gained = flux - kept[0]
         divergence = speed - kept[1]
@@ -591,7 +586,7 @@
         kept[1] = speed
 
         half = 0.5 * courant_ref[1, row].astype(F32)
-        above = [pltpu.roll(field, layers - 1, 0) for field in own]
+        above = [None if k == 4 else pltpu.roll(field, layers - 1, 0) for k, field in enumerate(own)]
         speed = half + pltpu.roll(half, layers - 1, 0)
         flux = upwind_flux(1, own, above, speed)
         flux = jnp.where(last_layer, axial_flux_ref[1, row], flux)
@@ -604,7 +599,7 @@
         )
 
         half = 0.5 * courant_ref[2, row].astype(F32)
-        outer = [pltpu.roll(field, cells - 1, 1) for field in own]
+        outer = [None if k == 4 else pltpu.roll(field, cells - 1, 1) for k, field in enumerate(own)]
         speed = jnp.where(inner, half + pltpu.roll(half, cells - 1, 1), 0.0)
         flux = upwind_flux(2, own, outer, speed, radius, next_radius)
         gained = gained + (flux - pltpu.roll(flux, 1, 1)) * inverse_radius
@@ -629,14 +624,16 @@
         scales[...] = jnp.zeros_like(scales)
 
         def radial(z, _):
-            at = pl.ds(pl.multiple_of(z * chunk, chunk), chunk)
+            at = pl.ds(pl.multiple_of(z * 2 * chunk, 2 * chunk), 2 * chunk)
             rows = jnp.concatenate([source[tile, at, :] for tile in range(lane_tiles)], axis=1)
-            got = dot3((basis_ref[0], basis_ref[1]), split(rows), ((1,), (1,)))
-            scales[...] = jnp.maximum(scales[...], jnp.abs(got))
-            wide[pl.ds(z, modes, stride=layers), :] = got
+            both = dot3((basis_ref[0], basis_ref[1]), split(rows), ((1,), (1,)))
+            for half in range(2):
+                got = both[:, half * chunk : (half + 1) * chunk]
+                scales[...] = jnp.maximum(scales[...], jnp.abs(got))
+                wide[pl.ds(z * 2 + half, modes, stride=layers), :] = got
             return 0
 
-        lax.fori_loop(0, layers, radial, 0)
+        lax.fori_loop(0, layers // 2, radial, 0)
         exponent = exponent_of(scales[...])
         devices, _, height, lanes = sent_ref.shape
         share = modes // devices
@@ -654,7 +651,7 @@
         lax.fori_loop(0, devices, coding, 0)
 
 
-def advect_chunk(arrays, low, high, axial_flux, axial_speed, basis, chunk_index, chunk, around, devices, base):
+def advect_chunk(arrays, ends, axial_flux, axial_speed, basis, chunk_index, chunk, around, devices, base):
     fraction, normals, planes, flags, courant = arrays
     rows, layers, cells = fraction.shape
     block = BLOCK
@@ -671,7 +668,8 @@
     whole = pl.BlockSpec((block, layers, cells), lambda i: (here(i), 0, 0))
     triple = pl.BlockSpec((3, block, layers, cells), lambda i: (0, here(i), 0, 0))
     row = pl.BlockSpec((1, layers, cells), lambda i: (after(i), 0, 0))
-    pack = pl.BlockSpec((1, 5, layers, cells), lambda i: (0, 0, 0, 0))
+    low = pl.BlockSpec((1, 5, layers, cells), lambda i: (2 * chunk_index, 0, 0, 0))
+    high = pl.BlockSpec((1, 5, layers, cells), lambda i: (2 * chunk_index + 3, 0, 0, 0))
     edge = pl.BlockSpec((2, block, 1, cells), lambda i: (0, here(i), 0, 0))
     in_specs = [
         whole,
@@ -683,8 +681,8 @@
         row,
         row,
         pl.BlockSpec((1, 1, layers, cells), lambda i: (0, after(i), 0, 0)),
-        pack,
-        pack,
+        low,
+        high,
         edge,
         edge,
         pl.BlockSpec((2, cells, cells), lambda i: (0, 0, 0)),
@@ -692,7 +690,7 @@
     operands = [
         fraction, normals, planes, flags, courant,
         normals, planes, flags, courant,
-        low, high, axial_flux, axial_speed, basis,
+        ends, ends, axial_flux, axial_speed, basis,
     ]
     aliases = {}
     if base is not None:
@@ -712,7 +710,7 @@
             jax.ShapeDtypeStruct((devices, share + 1, layers, chunk), jnp.int16),
         ],
         scratch_shapes=[
-            pltpu.VMEM((block + 2, 6, layers, cells), F32),
+            pltpu.VMEM((block + 2, 7, layers, cells), F32),
             pltpu.VMEM((2, layers, cells), F32),
             pltpu.VMEM((cells // 128, layers * chunk, 128), F32),
             pltpu.VMEM((cells * layers, chunk), F32),
@@ -764,8 +762,18 @@
 def solve_kernel(around, along, chunks, group, *refs):
     got = refs[:chunks]
     extra = refs[chunks : 2 * chunks]
-    mix, unmix, forth, back, rates, weights, shifts = refs[2 * chunks : 2 * chunks + 7]
-    sent, high, low, result, scale, exponents = refs[2 * chunks + 7 :]
+    mix, unmix, forth_ref, back_ref, rates, weights, shifts = refs[2 * chunks : 2 * chunks + 7]
+    sent, high, low, result, scale, exponents, forth, back, arrived = refs[2 * chunks + 7 :]
+    copies = [
+        pltpu.make_async_copy(forth_ref, forth, arrived.at[0]),
+        pltpu.make_async_copy(back_ref, back, arrived.at[1]),
+    ]
+
+    @pl.when(pl.program_id(0) == 0)
+    def _():
+        for copy in copies:
+            copy.start()
+
     devices, count, layers, lanes = got[0].shape
     share = (sent.shape[1] - 1) // chunks
     pairs = around // 4
@@ -803,12 +811,24 @@
 
     lax.fori_loop(0, count * along, fold, 0)
 
+    @pl.when(pl.program_id(0) == 0)
+    def _():
+        for copy in copies:
+            copy.wait()
+
+    height = mix.shape[1]
+    parts = [pl.ds(at, height) for at in range(0, high.shape[1], height)]
+
     def waves(k, _):
-        mixed = dot3((mix[0], mix[1]), (high[k], low[k]))
-        spectrum = dot3(split(mixed), (forth[k, 0], forth[k, 1]))
-        solved = spectrum * weights[k] / (rates[k] + shifts[...])
-        physical = dot3(split(solved), (back[k, 0], back[k, 1]))
-        result[k] = dot3((unmix[0], unmix[1]), split(physical))
+        for at in parts:
+            high[k, at], low[k, at] = split(
+                dot3((mix[0], mix[1]), (high[k, at], low[k, at]))
+            )
+        spectrum = dot3((high[k], low[k]), (forth[k, 0], forth[k, 1]))
+        high[k], low[k] = split(spectrum * weights[k] / (rates[k] + shifts[...]))
+        high[k], low[k] = split(dot3((high[k], low[k]), (back[k, 0], back[k, 1])))
+        for at in parts:
+            result[k, at] = dot3((unmix[0], unmix[1]), (high[k, at], low[k, at]))
         return 0
 
     lax.fori_loop(0, 4, waves, 0)
@@ -840,7 +860,7 @@
     devices, slots, layers, lanes = got[0].shape
     modes = slots - 1
     share = modes // groups
-    count = 4
+    count = share
     steps = share // count
     rows = count * along * layers
     forth, back, rates, weights = tables
@@ -857,7 +877,9 @@
         ]
         * chunks
         + [pl.BlockSpec((devices, 1, layers, lanes), lambda i: (0, modes, 0, 0))] * chunks
-        + [fixed(x) for x in (mix, unmix, forth, back, rates, weights)]
+        + [fixed(mix), fixed(unmix)]
+        + [pl.BlockSpec(memory_space=pl.ANY)] * 2
+        + [fixed(rates), fixed(weights)]
         + [pl.BlockSpec((rows, 1), lambda i: (group * steps + i, 0))],
         out_specs=pl.BlockSpec((devices, slots, layers, lanes), lambda i: (0, 0, 0, 0)),
         out_shape=jax.ShapeDtypeStruct((devices, chunks * share + 1, layers, lanes), jnp.int16),
@@ -867,6 +889,9 @@
             pltpu.VMEM((4, rows, width), F32),
             pltpu.VMEM((chunks, devices, layers, lanes), F32),
             pltpu.VMEM((devices, layers, lanes), F32),
+            pltpu.VMEM(forth.shape, BF16),
+            pltpu.VMEM(back.shape, BF16),
+            pltpu.SemaphoreType.DMA((2,)),
         ],
         compiler_params=pltpu.CompilerParams(vmem_limit_bytes=48 * 2**20),
         cost_estimate=pl.CostEstimate(
@@ -879,7 +904,7 @@
 def pressure_kernel(around, groups, *refs):
     got = refs[:groups]
     extra = refs[groups : 2 * groups]
-    basis, out, flat, wide, scale = refs[2 * groups :]
+    basis, out, flat, wide, scale, high, low = refs[2 * groups :]
     devices, share, layers, lanes = got[0].shape
     lane_tiles = out.shape[2] // 128
     chunk = pl.program_id(0)
@@ -902,17 +927,27 @@
 
         lax.fori_loop(0, devices, unpack, 0)
 
-    def radial(z, _):
-        total = jnp.zeros((lanes, out.shape[2]), F32)
-        for group in range(groups):
-            values = split(flat[group, pl.ds(z, devices * share, stride=layers), :])
-            turned = [dot(turn, part, ((1,), (1,))).astype(BF16) for part in values]
-            total = total + dot3(turned, (basis[0, group], basis[1, group]))
-        for tile in range(lane_tiles):
-            wide[tile, pl.ds(z, lanes, stride=layers), :] = total[:, tile * 128 : (tile + 1) * 128]
+    together = high.shape[0] // lanes
+
+    def radial(batch, _):
+        for part in range(together):
+            for group in range(groups):
+                z = batch * together + part
+                values = split(flat[group, pl.ds(z, devices * share, stride=layers), :])
+                at = pl.ds(group * devices * share, devices * share)
+                for target, value in zip((high, low), values):
+                    target[part * lanes : (part + 1) * lanes, at] = dot(
+                        turn, value, ((1,), (1,))
+                    ).astype(BF16)
+        total = dot3((high[...], low[...]), (basis[0], basis[1]))
+        for part in range(together):
+            for tile in range(lane_tiles):
+                wide[tile, pl.ds(batch * together + part, lanes, stride=layers), :] = total[
+                    part * lanes : (part + 1) * lanes, tile * 128 : (tile + 1) * 128
+                ]
         return 0
 
-    lax.fori_loop(0, layers, radial, 0)
+    lax.fori_loop(0, layers // together, radial, 0)
     for tile in range(lane_tiles):
         out[:, :, tile * 128 : (tile + 1) * 128] = wide[tile].reshape(lanes, layers, 128)
 
@@ -938,6 +973,8 @@
             pltpu.VMEM((groups, devices * share * layers, lanes), F32),
             pltpu.VMEM((cells // 128, lanes * layers, 128), F32),
             pltpu.VMEM((groups, devices, layers, lanes), F32),
+            pltpu.VMEM((4 * lanes, groups * devices * share), BF16),
+            pltpu.VMEM((4 * lanes, groups * devices * share), BF16),
         ],
         compiler_params=pltpu.CompilerParams(vmem_limit_bytes=48 * 2**20),
         name="pressure_of",
@@ -1000,11 +1037,10 @@
     forward_basis = halves(radial_basis.T)
     arrays = (fraction, normals, planes, cell_flags, courant)
     updated, got = None, []
+    ends = jnp.concatenate([low_row, packs, high_row])
     for chunk in range(chunks):
-        low = low_row if chunk == 0 else packs[2 * chunk - 1 : 2 * chunk]
-        high = high_row if chunk == chunks - 1 else packs[2 * chunk + 2 : 2 * chunk + 3]
         updated, sent = advect_chunk(
-            arrays, low, high, axial_flux, axial_speed, forward_basis, chunk, CHUNK, around, devices, updated
+            arrays, ends, axial_flux, axial_speed, forward_basis, chunk, CHUNK, around, devices, updated
         )
         got.append(exchanged(following(sent, got[-1]) if got else sent))
     count = jnp.eye(4, dtype=F32)
@@ -1018,7 +1054,7 @@
         sent = solve_group(got, mix, unmix, tables, shifts, group, groups, around, along)
         returned.append(exchanged(sent))
     back_basis = radial_basis.T.reshape(devices, groups, modes // groups, cells)
-    back_basis = halves(back_basis.transpose(1, 0, 2, 3).reshape(groups, -1, cells))
+    back_basis = halves(back_basis.transpose(1, 0, 2, 3).reshape(-1, cells))
     pressure = pressure_of(returned, back_basis, around, chunks)
     return (updated, pressure)
 

time: 411 us -> 376 us (0.915)
  Pallas kernels: 209 us -> 186 us
  waiting for transfers between devices: 146 us -> 132 us
    ppermute x6, waiting for transfers between devices: 24.4 us -> 6.99 us  [shifted_in(): return lax.ppermute(edge, axis, pairs)]
    pallas_call x1, Pallas kernels: 31.9 us -> 22.5 us  [pressure_of(): pl.pallas_call(functools.partial(pressure_kernel, around, groups), grid=(...]
    pallas_call x2, Pallas kernels: 44.3 us -> 37.2 us  [solve_group(): pl.pallas_call(functools.partial(solve_kernel, around, along, chunks, gro...]
    pallas_call x2, Pallas kernels: 107 us -> 101 us  [advect_chunk(): pl.pallas_call(functools.partial(chunk_kernel, around, base is not None),...]
    unnamed x45 -> x49, local copies, waits for them, and re-layouts: 12.8 us -> 13.9 us
  transfers between devices with their start and end apart: 10 -> 10, of which waited for: 6 -> 5; matrix products, arithmetic and copies ran while one was open for 3% -> 3% of each run, Pallas kernels for 24% -> 24%
where the time goes in v1:
time: 376 us; the launch traced here: 375 us
  Pallas kernels  186 us (49%)
  waiting for transfers between devices  132 us (35%)
  starting transfers between devices  28.7 us (8%)
  local copies, waits for them, and re-layouts  22.4 us (6%)
  other arithmetic  3.96 us (1%)
    all_to_all x4, waiting for transfers between devices, exchanged(): lax.all_to_all(sent, ('azim', 'axial'), split_axis=0, concat_axis=0, tile...  125 us
    pallas_call x2, Pallas kernels, advect_chunk(): pl.pallas_call(functools.partial(chunk_kernel, around, base is not None),...  101 us
    pallas_call x2, Pallas kernels, solve_group(): pl.pallas_call(functools.partial(solve_kernel, around, along, chunks, gro...  37.2 us
    pallas_call x1, Pallas kernels, pressure_of(): pl.pallas_call(functools.partial(pressure_kernel, around, groups), grid=(...  22.5 us
    all_to_all x4, starting transfers between devices, exchanged(): lax.all_to_all(sent, ('azim', 'axial'), split_axis=0, concat_axis=0, tile...  18.9 us
    unnamed x49, local copies, waits for them, and re-layouts  13.9 us
    pallas_call x1, Pallas kernels, edge_fields(): pl.pallas_call(fields_kernel, grid=(rows // step,), in_specs=[pl.BlockSpe...  13.3 us
    ppermute x6, starting transfers between devices, shifted_in(): return lax.ppermute(edge, axis, pairs)  9.84 us
  transfers between devices with their start and end apart: 10, of which 5 were waited for; matrix products, arithmetic and copies ran while one was open for 3% of the time, Pallas kernels for 24%

profile of v1, /device:TPU:1, one launch (start us, length us, event | category | flops | bytes accessed | tf_op | source)
XLA Modules:
  0.0 374.8 jit_solution(11252899985014603101)
XLA Ops:
  0.6 4.3 %edge_speeds.1.edge_ref = bf16[2,256,512]{2,1,0:T(8,128)(2,1)} custom-call(bf16[3,256,16,512]{3,2,1,0:T(8,128)(2,1)} %next_courant_ref.3), custom_call_target="tpu_custom_call" | custom-call | tf_op jit(solution)/shard_map/edge_speeds/pallas_call | solution.py:377
  6.0 2.2 collective-permute-start.2
  8.2 2.1 collective-permute-start.3
  10.3 2.9 packed_rows.1
  14.1 2.3 collective-permute-start
  16.4 13.3 %edge_fields.1.fields_ref = f32[2,4,256,512]{3,2,1,0:T(8,128)} custom-call(bf16[3,256,16,512]{3,2,1,0:T(8,128)(2,1)} %next_normals_ref.3, bf16[256,16,512]{2,1,0:T(8,128)(2,1)} %next_planes_ref.3, s32[256,16,512]{2,1,0:T(8,128)} %next_flags_ref.3), custom_call_target="tpu_custom_call" | custom-call | tf_op jit(solution)/shard_map/edge_fields/pallas_call | solution.py:407
  31.9 5.3 %edge_donors.1 = (f32[2,256,512]{2,1,0:T(8,128)}, s16[2,256,512]{2,1,0:T(8,128)(2,1)}, f32[2,256,512]{2,1,0:T(8,128)}) custom-call(f32[2,4,256,512]{3,2,1,0:T(8,128)} %edge_fields.1.fields_ref, bf16[2,256,512]{2,1,0:T(8,128)(2,1)} %edge_speeds.1.edge_ref, bf16[256,512]{1,0:T(8,128)(2,1)} %copy-done.20, bf16[256,512]{1,0:T(8,128)(2,1)} %copy-done.21), custom_call_target="tpu_custom_call" | custom-call | tf_op jit(solution)/shard_map/edge_donors/pallas_call | solution.py:442
  37.1 1.2 slice_bitcast_fusion.3
  38.4 3.3 collective-permute-start.5
  43.6 3.2 collective-permute-done.4
  46.8 3.8 %collective-permute-done.5 = s16[256,512]{1,0:T(8,128)(2,1)S(1)} collective-permute-done((s16[256,512]{1,0:T(8,128)(2,1)S(1)}, s16[256,512]{1,0:T(8,128)(2,1)S(1)}, u32[]{:S(2)}, u32[]{:S(2)}) %collective-permute-start.5) | collective-permute-done | bytes 262176 | tf_op jit(solution)/shard_map/ppermute | solution.py:22
  51.6 50.5 %advect_chunk.2 = (f32[256,16,512]{2,1,0:T(8,128)}, s16[32,17,16,128]{3,2,1,0:T(8,128)(2,1)S(1)}) custom-call(f32[256,16,512]{2,1,0:T(8,128)} %fraction_ref.3, bf16[3,256,16,512]{3,2,1,0:T(8,128)(2,1)} %next_normals_ref.3, bf16[256,16,512]{2,1,0:T(8,128)(2,1)} %next_planes_ref.3, s32[256,16,512]{2,1,0:T(8,128)} %next_flags_ref.3, ...), custom_call_target="tpu_custom_call" | custom-call | flops 41943040000 | bytes 31457280 | tf_op jit(solution)/shard_map/advect_chunk/pallas_call | solution.py:700
  102.1 1.4 copy-done.6
  103.4 5.6 %all-to-all-start = ((s16[32,17,16,128]{3,2,1,0:T(8,128)(2,1)}), s16[32,17,16,128]{3,2,1,0:T(8,128)(2,1)S(1)}, u32[]{:S(2)}, u32[]{:S(2)}) async-start(s16[32,17,16,128]{3,2,1,0:T(8,128)(2,1)} %copy-done.6), calls=%async_computation | async-start | bytes 4456448 | tf_op jit(solution)/shard_map/all_to_all | solution.py:990
  109.0 1.2 copy-done.8
  110.3 1.2 copy-done.10
  112.5 50.4 %advect_chunk.3 = (f32[256,16,512]{2,1,0:T(8,128)}, s16[32,17,16,128]{3,2,1,0:T(8,128)(2,1)S(1)}) custom-call(f32[256,16,512]{2,1,0:T(8,128)} %fraction_ref.3, bf16[3,256,16,512]{3,2,1,0:T(8,128)(2,1)} %next_normals_ref.3, bf16[256,16,512]{2,1,0:T(8,128)(2,1)} %next_planes_ref.3, s32[256,16,512]{2,1,0:T(8,128)} %next_flags_ref.3, ...), custom_call_target="tpu_custom_call", output_to_operand_aliasing={{0}: (14, {})} | custom-call | flops 41943040000 | bytes 31457280 | tf_op jit(solution)/shard_map/advect_chunk/pallas_call | solution.py:700
  162.9 1.4 copy-done.3
  164.3 1.4 copy-done
  165.7 5.9 %all-to-all-start.1 = ((s16[32,17,16,128]{3,2,1,0:T(8,128)(2,1)}), s16[32,17,16,128]{3,2,1,0:T(8,128)(2,1)}, u32[]{:S(2)}, u32[]{:S(2)}) async-start(s16[32,17,16,128]{3,2,1,0:T(8,128)(2,1)} %following.1), calls=%async_computation.1 | async-start | bytes 4456448 | tf_op jit(solution)/shard_map/all_to_all | solution.py:990
  174.0 2.1 mul.83
  177.5 45.1 %all-to-all-done.1.refs_1_.refs_3_ = s16[32,17,16,128]{3,2,1,0:T(8,128)(2,1)} async-done(((s16[32,17,16,128]{3,2,1,0:T(8,128)(2,1)}), s16[32,17,16,128]{3,2,1,0:T(8,128)(2,1)}, u32[]{:S(2)}, u32[]{:S(2)}) %all-to-all-start.1) | async-done | bytes 2228256 | tf_op jit(solution)/shard_map/all_to_all | solution.py:990
  222.7 18.7 %solve_group.3 = s16[32,17,16,128]{3,2,1,0:T(8,128)(2,1)S(1)} custom-call(s16[32,17,16,128]{3,2,1,0:T(8,128)(2,1)S(1)} %copy-done.1, s16[32,17,16,128]{3,2,1,0:T(8,128)(2,1)} %all-to-all-done.1.refs_1_.refs_3_, s16[32,17,16,128]{3,2,1,0:T(8,128)(2,1)S(1)} %copy-done.1, s16[32,17,16,128]{3,2,1,0:T(8,128)(2,1)} %all-to-all-done.1.refs_1_.refs_3_, ...), custom_call_target="tpu_custom_call" | custom-call | flops 8053063680 | bytes 20971520 | tf_op jit(solution)/shard_map/solve_group/pallas_call | solution.py:872
  241.4 1.4 copy-done.5
  242.8 3.7 all-to-all-start.3
  246.5 1.6 copy-done.2
  248.1 18.5 %solve_group.2 = s16[32,17,16,128]{3,2,1,0:T(8,128)(2,1)S(1)} custom-call(s16[32,17,16,128]{3,2,1,0:T(8,128)(2,1)S(1)} %copy-done.2, s16[32,17,16,128]{3,2,1,0:T(8,128)(2,1)} %all-to-all-done.1.refs_1_.refs_3_, s16[32,17,16,128]{3,2,1,0:T(8,128)(2,1)S(1)} %copy-done.2, s16[32,17,16,128]{3,2,1,0:T(8,128)(2,1)} %all-to-all-done.1.refs_1_.refs_3_, ...), custom_call_target="tpu_custom_call" | custom-call | flops 8053063680 | bytes 20971520 | tf_op jit(solution)/shard_map/solve_group/pallas_call | solution.py:872
  266.7 1.4 copy-done.4
  268.0 29.5 %all-to-all-done.3.refs_1_.refs_3_ = s16[32,17,16,128]{3,2,1,0:T(8,128)(2,1)S(1)} async-done(((s16[32,17,16,128]{3,2,1,0:T(8,128)(2,1)}), s16[32,17,16,128]{3,2,1,0:T(8,128)(2,1)S(1)}, u32[]{:S(2)}, u32[]{:S(2)}) %all-to-all-start.3) | async-done | bytes 2228256 | tf_op jit(solution)/shard_map/all_to_all | solution.py:990
  297.5 3.7 all-to-all-start.2
  301.5 50.7 %all-to-all-done.2.refs_0_.refs_2_ = s16[32,17,16,128]{3,2,1,0:T(8,128)(2,1)} async-done(((s16[32,17,16,128]{3,2,1,0:T(8,128)(2,1)}), s16[32,17,16,128]{3,2,1,0:T(8,128)(2,1)}, u32[]{:S(2)}, u32[]{:S(2)}) %all-to-all-start.2) | async-done | bytes 2228256 | tf_op jit(solution)/shard_map/all_to_all | solution.py:990
  352.2 22.5 %pressure_of.1 = f32[256,16,512]{2,1,0:T(8,128)} custom-call(s16[32,17,16,128]{3,2,1,0:T(8,128)(2,1)} %all-to-all-done.2.refs_0_.refs_2_, s16[32,17,16,128]{3,2,1,0:T(8,128)(2,1)S(1)} %all-to-all-done.3.refs_1_.refs_3_, s16[32,17,16,128]{3,2,1,0:T(8,128)(2,1)} %all-to-all-done.2.refs_0_.refs_2_, s16[32,17,16,128]{3,2,1,0:T(8,128)(2,1)S(1)} %all-to-all-done.3.refs_1_.refs_3_, ...), custom_call_target="tpu_custom_call" | custom-call | tf_op jit(solution)/shard_map/pressure_of/pallas_call | solution.py:960
  (70 shorter events, 12.2 us)
Async XLA Ops:
  6.0 24.2 %collective-permute-start.2 = (bf16[256,512]{1,0:T(8,128)(2,1)S(1)}, bf16[256,512]{1,0:T(8,128)(2,1)S(1)}, u32[]{:S(2)}, u32[]{:S(2)}) collective-permute-start(bf16[256,512]{1,0:T(8,128)(2,1)S(1)} %get-tuple-element.23), channel_id=1, source_target_pairs={{0,1},{1,2},{2,3},{3,0},{4,5},{5,6},{6,7},{7,4},{8,9},{9,10},{10,1... | collective-permute-start | bytes 786440 | tf_op jit(solution)/shard_map/ppermute | solution.py:22
  8.2 22.1 %collective-permute-start.3 = (bf16[256,512]{1,0:T(8,128)(2,1)S(1)}, bf16[256,512]{1,0:T(8,128)(2,1)S(1)}, u32[]{:S(2)}, u32[]{:S(2)}) collective-permute-start(bf16[256,512]{1,0:T(8,128)(2,1)S(1)} %get-tuple-element.22), channel_id=1, source_target_pairs={{1,0},{2,1},{3,2},{0,3},{5,4},{6,5},{7,6},{4,7},{9,8},{10,9},{11,1... | collective-permute-start | bytes 786440 | tf_op jit(solution)/shard_map/ppermute | solution.py:22
  14.1 27.6 %collective-permute-start = (bf16[1,5,16,512]{3,2,1,0:T(8,128)(2,1)S(1)}, bf16[1,5,16,512]{3,2,1,0:T(8,128)(2,1)S(1)}, u32[]{:S(2)}, u32[]{:S(2)}) collective-permute-start(bf16[1,5,16,512]{3,2,1,0:T(8,128)(2,1)S(1)} %get-tuple-element.24), channel_id=1, source_target_pairs={{0,4},{4,8},{8,12},{12,16},{16,20},{20,24},{24,28},{28,0},{1,5},{5... | collective-permute-start | bytes 245768 | tf_op jit(solution)/shard_map/ppermute | solution.py:22
  16.4 13.3 %copy-start.17 = (f32[512,512]{1,0:T(8,128)S(1)}, f32[512,512]{1,0:T(8,128)}, u32[]{:S(2)}) copy-start(f32[512,512]{1,0:T(8,128)} %param.18) | copy-start | bytes 3145732
  16.4 25.4 %collective-permute-start.1 = (bf16[1,5,16,512]{3,2,1,0:T(8,128)(2,1)S(1)}, bf16[1,5,16,512]{3,2,1,0:T(8,128)(2,1)}, u32[]{:S(2)}, u32[]{:S(2)}) collective-permute-start(bf16[1,5,16,512]{3,2,1,0:T(8,128)(2,1)S(1)} %get-tuple-element.25), channel_id=1, source_target_pairs={{4,0},{8,4},{12,8},{16,12},{20,16},{24,20},{28,24},{0,28},{5,1},{9... | collective-permute-start | bytes 245768 | tf_op jit(solution)/shard_map/ppermute | solution.py:22
  30.1 8.3 %copy-start.15 = (f32[512,512]{0,1:T(8,128)}, f32[512,512]{0,1:T(8,128)S(1)}, u32[]{:S(2)}) copy-start(f32[512,512]{0,1:T(8,128)S(1)} %copy.20) | copy-start | bytes 3145732
  37.1 5.8 %copy-start.19 = (f32[2,256,512]{2,1,0:T(8,128)S(1)}, f32[2,256,512]{2,1,0:T(8,128)}, u32[]{:S(2)}) copy-start(f32[2,256,512]{2,1,0:T(8,128)} %get-tuple-element.11) | copy-start | bytes 3145732
  37.1 13.5 %copy-start.18 = (f32[2,256,512]{2,1,0:T(8,128)S(1)}, f32[2,256,512]{2,1,0:T(8,128)}, u32[]{:S(2)}) copy-start(f32[2,256,512]{2,1,0:T(8,128)} %get-tuple-element.9) | copy-start | bytes 3145732
  38.4 8.5 %collective-permute-start.4 = (s16[256,512]{1,0:T(8,128)(2,1)S(1)}, s16[256,512]{1,0:T(8,128)(2,1)S(1)}, u32[]{:S(2)}, u32[]{:S(2)}) collective-permute-start(s16[256,512]{1,0:T(8,128)(2,1)S(1)} %get-tuple-element.20), channel_id=1, source_target_pairs={{0,1},{1,2},{2,3},{3,0},{4,5},{5,6},{6,7},{7,4},{8,9},{9,10},{10,1... | collective-permute-start | bytes 786440 | tf_op jit(solution)/shard_map/ppermute | solution.py:22
  38.4 12.2 %collective-permute-start.5 = (s16[256,512]{1,0:T(8,128)(2,1)S(1)}, s16[256,512]{1,0:T(8,128)(2,1)S(1)}, u32[]{:S(2)}, u32[]{:S(2)}) collective-permute-start(s16[256,512]{1,0:T(8,128)(2,1)S(1)} %get-tuple-element.21), channel_id=1, source_target_pairs={{1,0},{2,1},{3,2},{0,3},{5,4},{6,5},{7,6},{4,7},{9,8},{10,9},{11,1... | collective-permute-start | bytes 786440 | tf_op jit(solution)/shard_map/ppermute | solution.py:22
  42.9 59.2 %copy-start.11 = (bf16[6,5,16,512]{3,2,1,0:T(8,128)(2,1)}, bf16[6,5,16,512]{3,2,1,0:T(8,128)(2,1)S(1)}, u32[]{:S(2)}) copy-start(bf16[6,5,16,512]{3,2,1,0:T(8,128)(2,1)S(1)} %pad_maximum_fusion.2.low_ref.high_ref) | copy-start | bytes 1474564
  43.6 58.4 %copy-start.7 = (f32[2,256,1,512]{3,2,1,0:T(1,128)}, f32[2,256,1,512]{3,2,1,0:T(1,128)S(1)}, u32[]{:S(2)}) copy-start(f32[2,256,1,512]{3,2,1,0:T(1,128)S(1)} %broadcast_in_dim.15.axial_speed_ref) | copy-start | bytes 3145732
  51.6 50.5 %copy-start.9 = (f32[2,256,1,512]{3,2,1,0:T(1,128)}, f32[2,256,1,512]{3,2,1,0:T(1,128)S(1)}, u32[]{:S(2)}) copy-start(f32[2,256,1,512]{3,2,1,0:T(1,128)S(1)} %broadcast_in_dim.14.axial_flux_ref) | copy-start | bytes 3145732
  102.1 1.4 copy-start.6
  103.4 60.9 %all-to-all-start = ((s16[32,17,16,128]{3,2,1,0:T(8,128)(2,1)}), s16[32,17,16,128]{3,2,1,0:T(8,128)(2,1)S(1)}, u32[]{:S(2)}, u32[]{:S(2)}) async-start(s16[32,17,16,128]{3,2,1,0:T(8,128)(2,1)} %copy-done.6), calls=%async_computation | async-start | bytes 4456448 | tf_op jit(solution)/shard_map/all_to_all | solution.py:990
  109.0 1.2 copy-start.8
  110.3 1.2 copy-start.10
  111.5 1.0 copy-start.12
  162.9 1.4 copy-start.3
  164.3 1.4 copy-start
  165.7 6.7 %copy-start.23 = (f32[64]{0:T(128)S(1)}, f32[64]{0:T(128)}, u32[]{:S(2)}) copy-start(f32[64]{0:T(128)} %param.21) | copy-start | bytes 772
  165.7 7.2 %copy-start.22 = (f32[64,64]{1,0:T(8,128)S(1)}, f32[64,64]{1,0:T(8,128)}, u32[]{:S(2)}) copy-start(f32[64,64]{1,0:T(8,128)} %param.19) | copy-start | bytes 49156
  165.7 57.0 %copy-start.1 = (s16[32,17,16,128]{3,2,1,0:T(8,128)(2,1)S(1)}, s16[32,17,16,128]{3,2,1,0:T(8,128)(2,1)}, u32[]{:S(2)}) copy-start(s16[32,17,16,128]{3,2,1,0:T(8,128)(2,1)} %copy-done) | copy-start | bytes 6684676
  165.7 57.0 %copy-start.13 = (f32[4,1,512]{2,1,0:T(1,128)S(1)}, f32[4,1,512]{2,1,0:T(1,128)}, u32[]{:S(2)}) copy-start(f32[4,1,512]{2,1,0:T(1,128)} %constant.29.clone.refs_8_) | copy-start | bytes 24580
  165.7 57.0 %copy-start.14 = (f32[4,1,512]{2,1,0:T(1,128)S(1)}, f32[4,1,512]{2,1,0:T(1,128)}, u32[]{:S(2)}) copy-start(f32[4,1,512]{2,1,0:T(1,128)} %constant.30.clone.refs_9_) | copy-start | bytes 24580
  165.7 57.0 %all-to-all-start.1 = ((s16[32,17,16,128]{3,2,1,0:T(8,128)(2,1)}), s16[32,17,16,128]{3,2,1,0:T(8,128)(2,1)}, u32[]{:S(2)}, u32[]{:S(2)}) async-start(s16[32,17,16,128]{3,2,1,0:T(8,128)(2,1)} %following.1), calls=%async_computation.1 | async-start | bytes 4456448 | tf_op jit(solution)/shard_map/all_to_all | solution.py:990
  241.4 1.4 copy-start.5
  242.8 54.7 %all-to-all-start.3 = ((s16[32,17,16,128]{3,2,1,0:T(8,128)(2,1)}), s16[32,17,16,128]{3,2,1,0:T(8,128)(2,1)S(1)}, u32[]{:S(2)}, u32[]{:S(2)}) async-start(s16[32,17,16,128]{3,2,1,0:T(8,128)(2,1)} %copy-done.5), calls=%async_computation.3 | async-start | bytes 4456448 | tf_op jit(solution)/shard_map/all_to_all | solution.py:990
  246.5 1.6 copy-start.2
  266.6 1.4 copy-start.4
  268.0 33.2 %copy-start.16 = (f32[512,512]{0,1:T(8,128)S(1)}, f32[512,512]{0,1:T(8,128)}, u32[]{:S(2)}) copy-start(f32[512,512]{0,1:T(8,128)} %copy-done.15) | copy-start | bytes 3145732
  297.5 54.8 %all-to-all-start.2 = ((s16[32,17,16,128]{3,2,1,0:T(8,128)(2,1)}), s16[32,17,16,128]{3,2,1,0:T(8,128)(2,1)}, u32[]{:S(2)}, u32[]{:S(2)}) async-start(s16[32,17,16,128]{3,2,1,0:T(8,128)(2,1)} %copy-done.4), calls=%async_computation.2 | async-start | bytes 4456448 | tf_op jit(solution)/shard_map/all_to_all | solution.py:990
  (2 other events, 1.6 us)

commit v2 on v1

--- a/solution.py
+++ b/solution.py
@@ -355,130 +355,229 @@
     return jnp.where(flags == 2, planes.astype(F32), jnp.where(flags == 1, 4.0, -4.0))
 
 
-def strided_rows(work, layer, rows, layers, cells):
-    parts = []
-    for lane in range(0, cells, 128):
-        parts.append(work[lane // 128, pl.ds(layer, rows, stride=layers), :])
-    return parts
-
-
-def speeds_kernel(courant_ref, edge_ref, work):
-    rows, layers, cells = courant_ref.shape[1:]
-    for lane in range(0, cells, 128):
-        work[lane // 128] = courant_ref[0, :, :, pl.ds(lane, 128)].astype(F32).reshape(rows * layers, 128)
-    for side, layer in ((0, 0), (1, layers - 1)):
-        for tile, got in enumerate(strided_rows(work, layer, rows, layers, cells)):
-            edge_ref[side, :, pl.ds(tile * 128, 128)] = got.astype(BF16)
-
-
-def edge_speeds(courant):
-    _, rows, layers, cells = courant.shape
-    step = 64
+def halo_kernel(
+    courant_ref,
+    normals_ref,
+    planes_ref,
+    flags_ref,
+    first_normals_ref,
+    first_planes_ref,
+    first_flags_ref,
+    first_courant_ref,
+    last_normals_ref,
+    last_planes_ref,
+    last_flags_ref,
+    last_courant_ref,
+    flux_ref,
+    speed_ref,
+    ends_ref,
+    work,
+    edge,
+    edge_in,
+    fields,
+    code,
+    code_in,
+    packs,
+    packs_in,
+    row_send,
+    row_recv,
+    edge_send,
+    edge_recv,
+    code_send,
+    code_recv,
+):
+    step = pl.program_id(0)
+    half = pl.num_programs(0) // 2
+    span, layers, cells = planes_ref.shape
+    groups, group = code_send.shape[1], code.shape[2]
+    tiles = cells // 128
+    neighbours = []
+    for axis in ("azim", "axial"):
+        count, me = lax.axis_size(axis), lax.axis_index(axis)
+        neighbours.append(
+            ({axis: lax.rem(me + count - 1, count)}, {axis: lax.rem(me + 1, count)})
+        )
+
+    def remote(source, target, send, recv, device):
+        return pltpu.make_async_remote_copy(
+            src_ref=source,
+            dst_ref=target,
+            send_sem=send,
+            recv_sem=recv,
+            device_id=device,
+            device_id_type=pl.DeviceIdType.MESH,
+        )
+
+    row_copies = [
+        remote(packs.at[s], packs_in.at[1 - s], row_send.at[s], row_recv.at[1 - s], neighbours[0][s])
+        for s in range(2)
+    ]
+    edge_copies = [
+        remote(edge.at[s], edge_in.at[1 - s], edge_send.at[s], edge_recv.at[1 - s], neighbours[1][s])
+        for s in range(2)
+    ]
+
+    def code_copy(s, g):
+        return remote(
+            code.at[s, g],
+            code_in.at[1 - s, g],
+            code_send.at[s, g],
+            code_recv.at[1 - s, g],
+            neighbours[1][s],
+        )
+
+    @pl.when(step == 0)
+    def _():
+        barrier = pltpu.get_barrier_semaphore()
+        for pair in neighbours:
+            for device in pair:
+                pl.semaphore_signal(
+                    barrier, inc=1, device_id=device, device_id_type=pl.DeviceIdType.MESH
+                )
+        pl.semaphore_wait(barrier, 4)
+        for s, (normals, planes, flags, courant) in enumerate(
+            (
+                (first_normals_ref, first_planes_ref, first_flags_ref, first_courant_ref),
+                (last_normals_ref, last_planes_ref, last_flags_ref, last_courant_ref),
+            )
+        ):
+            for k in range(3):
+                packs[s, k] = normals[k, 0]
+            packs[s, 3] = plane_value(planes[0], flags[0]).astype(BF16)
+            packs[s, 4] = courant[0, 0]
+        for copy in row_copies:
+            copy.start()
+
+    def layer_rows(tile, layer):
+        return work[tile, pl.ds(layer, span, stride=layers), :]
+
+    @pl.when(step < half)
+    def _():
+        at = pl.ds(pl.multiple_of(step * span, span), span)
+        for tile in range(tiles):
+            lanes = pl.ds(tile * 128, 128)
+            work[tile] = courant_ref[0, :, :, lanes].astype(F32).reshape(span * layers, 128)
+            for s, layer in ((0, 0), (1, layers - 1)):
+                edge[s, at, lanes] = layer_rows(tile, layer).astype(BF16)
+
+    @pl.when(step == half - 1)
+    def _():
+        for copy in edge_copies:
+            copy.start()
+
+    @pl.when(step >= half)
+    def _():
+        at = pl.ds(pl.multiple_of((step - half) * span, span), span)
+        for k in range(4):
+            for tile in range(tiles):
+                lanes = pl.ds(tile * 128, 128)
+                if k < 3:
+                    field = normals_ref[k, :, :, lanes].astype(F32)
+                else:
+                    field = plane_value(planes_ref[:, :, lanes], flags_ref[:, :, lanes])
+                work[tile] = field.reshape(span * layers, 128)
+                for s, layer in ((0, 0), (1, layers - 1)):
+                    fields[s, k, at, lanes] = layer_rows(tile, layer)
+
+    @pl.when(step == 2 * half - 1)
+    def _():
+        for copy in edge_copies:
+            copy.wait()
+        for g in range(groups):
+            for s in range(2):
+
+                def donate(piece, _, g=g, s=s):
+                    inside = pl.ds(pl.multiple_of(piece * 16, 16), 16)
+                    at = pl.ds(pl.multiple_of(g * group + piece * 16, 16), 16)
+                    normals = [fields[s, k, at, :] for k in range(3)]
+                    speed = 0.5 * (edge[s, at, :].astype(F32) + edge_in[s, at, :].astype(F32))
+                    inverse = inverse_of(*normals)
+                    flux = slab_flux(
+                        normals[1],
+                        jnp.abs(normals[0]),
+                        jnp.abs(normals[2]),
+                        fields[s, 3, at, :],
+                        inverse if s == 1 else -inverse,
+                        speed,
+                    )
+                    flux = jnp.where(speed > 0.0 if s == 1 else speed < 0.0, flux, 0.0)
+                    flux_ref[s, at, :] = flux
+                    speed_ref[s, at, :] = speed
+                    code[s, g, inside, :] = to_codes(flux * FLUX_SCALE)
+                    return 0
+
+                lax.fori_loop(0, group // 16, donate, 0)
+                code_copy(s, g).start()
+        for copy in row_copies:
+            copy.wait()
+        ends_ref[...] = packs_in[...]
+        for g in range(groups):
+            for s in range(2):
+                code_copy(s, g).wait()
+            for s in range(2):
+                at = pl.ds(g * group, group)
+                received = code_in[s, g].astype(jnp.int32).astype(F32)
+                flux_ref[s, at, :] += received * (1.0 / FLUX_SCALE)
+
+
+def halos(normals, planes, flags, courant):
+    rows, layers, cells = planes.shape
+    span, groups = 32, 4
+    half = rows // span
+
+    def later(i):
+        return jnp.maximum(i - half, 0)
+
+    whole = pl.BlockSpec((span, layers, cells), lambda i: (later(i), 0, 0))
+    in_specs = [
+        pl.BlockSpec((1, span, layers, cells), lambda i: (1, jnp.minimum(i, half - 1), 0, 0)),
+        pl.BlockSpec((3, span, layers, cells), lambda i: (0, later(i), 0, 0)),
+        whole,
+        whole,
+    ]
+    for row in (0, rows - 1):
+        one = pl.BlockSpec((1, layers, cells), lambda i, row=row: (row, 0, 0))
+        in_specs += [
+            pl.BlockSpec((3, 1, layers, cells), lambda i, row=row: (0, row, 0, 0)),
+            one,
+            one,
+            pl.BlockSpec((1, 1, layers, cells), lambda i, row=row: (0, row, 0, 0)),
+        ]
+    pair = pl.BlockSpec((2, rows, cells), lambda i: (0, 0, 0))
+    ends = (2, 5, layers, cells)
+    split_shape = (2, groups, rows // groups, cells)
+    dma = pltpu.SemaphoreType.DMA
     return pl.pallas_call(
-        speeds_kernel,
-        grid=(rows // step,),
-        in_specs=[pl.BlockSpec((1, step, layers, cells), lambda i: (1, i, 0, 0))],
-        out_specs=pl.BlockSpec((2, step, cells), lambda i: (0, i, 0)),
-        out_shape=jax.ShapeDtypeStruct((2, rows, cells), BF16),
-        scratch_shapes=[pltpu.VMEM((cells // 128, step * layers, 128), F32)],
-        name="edge_speeds",
-    )(courant)
-
-
-def fields_kernel(normals_ref, planes_ref, flags_ref, fields_ref, work):
-    rows, layers, cells = planes_ref.shape
-    for k in range(4):
-        for lane in range(0, cells, 128):
-            at = pl.ds(lane, 128)
-            if k < 3:
-                field = normals_ref[k, :, :, at].astype(F32)
-            else:
-                field = plane_value(planes_ref[:, :, at], flags_ref[:, :, at])
-            work[lane // 128] = field.reshape(rows * layers, 128)
-        for side, layer in ((0, 0), (1, layers - 1)):
-            for tile, got in enumerate(strided_rows(work, layer, rows, layers, cells)):
-                fields_ref[side, k, :, pl.ds(tile * 128, 128)] = got
-
-
-def edge_fields(normals, planes, flags):
-    rows, layers, cells = planes.shape
-    step = 32
-    whole = pl.BlockSpec((step, layers, cells), lambda i: (i, 0, 0))
-    return pl.pallas_call(
-        fields_kernel,
-        grid=(rows // step,),
-        in_specs=[
-            pl.BlockSpec((3, step, layers, cells), lambda i: (0, i, 0, 0)),
-            whole,
-            whole,
+        halo_kernel,
+        grid=(2 * half,),
+        in_specs=in_specs,
+        out_specs=[pair, pair, pl.BlockSpec(ends, lambda i: (0, 0, 0, 0))],
+        out_shape=[
+            jax.ShapeDtypeStruct((2, rows, cells), F32),
+            jax.ShapeDtypeStruct((2, rows, cells), F32),
+            jax.ShapeDtypeStruct(ends, BF16),
         ],
-        out_specs=pl.BlockSpec((2, 4, step, cells), lambda i: (0, 0, i, 0)),
-        out_shape=jax.ShapeDtypeStruct((2, 4, rows, cells), F32),
-        scratch_shapes=[pltpu.VMEM((cells // 128, step * layers, 128), F32)],
-        name="edge_fields",
-    )(normals, planes, flags)
-
-
-def donors_kernel(fields_ref, edge_ref, below_ref, above_ref, own_ref, code_ref, speed_ref):
-    for side in range(2):
-        n = [fields_ref[side, k] for k in range(3)]
-        beyond = (below_ref if side == 0 else above_ref)[...].astype(F32)
-        speed = 0.5 * (edge_ref[side].astype(F32) + beyond)
-        inverse = inverse_of(*n)
-        inverse = inverse if side == 1 else -inverse
-        flux = slab_flux(n[1], jnp.abs(n[0]), jnp.abs(n[2]), fields_ref[side, 3], inverse, speed)
-        flux = jnp.where(speed > 0.0 if side == 1 else speed < 0.0, flux, 0.0)
-        own_ref[side] = flux
-        code_ref[side] = jnp.round(flux * FLUX_SCALE).astype(jnp.int32).astype(jnp.int16)
-        speed_ref[side] = speed
-
-
-def donors(fields, edge, below, above):
-    rows, cells = below.shape
-    step = 64
-    pair = pl.BlockSpec((2, step, cells), lambda i: (0, i, 0))
-    one = pl.BlockSpec((step, cells), lambda i: (i, 0))
-    shape = (2, rows, cells)
-    return pl.pallas_call(
-        donors_kernel,
-        grid=(rows // step,),
-        in_specs=[pl.BlockSpec((2, 4, step, cells), lambda i: (0, 0, i, 0)), pair, one, one],
-        out_specs=[pair, pair, pair],
-        out_shape=[
-            jax.ShapeDtypeStruct(shape, F32),
-            jax.ShapeDtypeStruct(shape, jnp.int16),
-            jax.ShapeDtypeStruct(shape, F32),
+        scratch_shapes=[
+            pltpu.VMEM((cells // 128, span * layers, 128), F32),
+            pltpu.VMEM((2, rows, cells), BF16),
+            pltpu.VMEM((2, rows, cells), BF16),
+            pltpu.VMEM((2, 4, rows, cells), F32),
+            pltpu.VMEM(split_shape, jnp.int16),
+            pltpu.VMEM(split_shape, jnp.int16),
+            pltpu.VMEM(ends, BF16),
+            pltpu.VMEM(ends, BF16),
+            dma((2,)),
+            dma((2,)),
+            dma((2,)),
+            dma((2,)),
+            dma((2, groups)),
+            dma((2, groups)),
         ],
-        name="edge_donors",
-    )(fields, edge, below, above)
-
-
-def rows_kernel(normals_ref, planes_ref, flags_ref, courant_ref, out_ref):
-    for k in range(3):
-        out_ref[0, k] = normals_ref[k, 0]
-    out_ref[0, 3] = plane_value(planes_ref[0], flags_ref[0]).astype(BF16)
-    out_ref[0, 4] = courant_ref[0, 0]
-
-
-def packed_rows(normals, planes, flags, courant, chunk):
-    rows, layers, cells = planes.shape
-
-    def place(i):
-        return (i // 2) * chunk + (i % 2) * (chunk - 1)
-
-    return pl.pallas_call(
-        rows_kernel,
-        grid=(2 * (rows // chunk),),
-        in_specs=[
-            pl.BlockSpec((3, 1, layers, cells), lambda i: (0, place(i), 0, 0)),
-            pl.BlockSpec((1, layers, cells), lambda i: (place(i), 0, 0)),
-            pl.BlockSpec((1, layers, cells), lambda i: (place(i), 0, 0)),
-            pl.BlockSpec((1, 1, layers, cells), lambda i: (0, place(i), 0, 0)),
-        ],
-        out_specs=pl.BlockSpec((1, 5, layers, cells), lambda i: (i, 0, 0, 0)),
-        out_shape=jax.ShapeDtypeStruct((2 * (rows // chunk), 5, layers, cells), BF16),
-        name="packed_rows",
-    )(normals, planes, flags, courant)
+        compiler_params=pltpu.CompilerParams(
+            collective_id=0, has_side_effects=True, vmem_limit_bytes=60 * 2**20
+        ),
+        name="halos",
+    )(courant, normals, planes, flags, *(normals, planes, flags, courant) * 2)
 
 
 def exponent_of(most):
@@ -491,7 +590,8 @@
 
 def chunk_kernel(
     around,
-    has_base,
+    chunk_index,
+    chunks,
     fraction_ref,
     normals_ref,
     planes_ref,
@@ -501,14 +601,17 @@
     next_planes_ref,
     next_flags_ref,
     next_courant_ref,
-    low_ref,
-    high_ref,
+    last_normals_ref,
+    last_planes_ref,
+    last_flags_ref,
+    last_courant_ref,
+    ends_ref,
     axial_flux_ref,
     axial_speed_ref,
     basis_ref,
     *rest,
 ):
-    if has_base:
+    if chunk_index:
         rest = rest[1:]
     updated_ref, sent_ref, parts, kept, source, wide, scales = rest
     block, layers, cells = fraction_ref.shape
@@ -518,17 +621,22 @@
     lane_tiles = cells // 128
     backwards = lax.rem(lax.axis_index("azim"), around // 2) >= around // 4
 
+    def put_field(slot, k, value):
+        at = pl.ds(pl.multiple_of(slot * layers, layers), layers)
+        for tile in range(lane_tiles):
+            parts[k, tile, at, :] = value[:, tile * 128 : (tile + 1) * 128]
+
+    def get_field(slot, k, shift=0):
+        at = pl.ds(slot * layers + shift, layers)
+        return jnp.concatenate([parts[k, tile, at, :] for tile in range(lane_tiles)], axis=1)
+
     def put_parts(slot, normals, plane, speed):
-        for k in range(3):
-            parts[slot, k] = normals[k]
-        parts[slot, 3] = plane
         inverse = inverse_of(*normals)
-        parts[slot, 4] = inverse
-        parts[slot, 5] = -inverse
-        parts[slot, 6] = 0.5 * speed
-
-    def put_packed(slot, ref):
-        values = [ref[0, k].astype(F32) for k in range(5)]
+        for k, value in enumerate((*normals, plane, inverse, -inverse, 0.5 * speed)):
+            put_field(slot, k, value)
+
+    def put_packed(slot, side):
+        values = [ends_ref[side, k].astype(F32) for k in range(5)]
         put_parts(slot, values[:3], values[3], values[4])
 
     def own_parts(row, _):
@@ -538,30 +646,43 @@
             plane_value(planes_ref[row], flags_ref[row]),
             courant_ref[0, row].astype(F32),
         )
+        put_field(row, 7, 0.5 * courant_ref[1, row].astype(F32))
         return 0
 
-    lax.fori_loop(0, block, own_parts, 0)
-
-    @pl.when(step < steps - 1)
-    def _():
+    lax.fori_loop(0, block, own_parts, 0, unroll=2)
+
+    def put_row(slot, normals, planes, flags, courant):
         put_parts(
-            block,
-            [next_normals_ref[k, 0].astype(F32) for k in range(3)],
-            plane_value(next_planes_ref[0], next_flags_ref[0]),
-            next_courant_ref[0, 0].astype(F32),
+            slot,
+            [normals[k, 0].astype(F32) for k in range(3)],
+            plane_value(planes[0], flags[0]),
+            courant[0, 0].astype(F32),
         )
 
-    @pl.when(step == steps - 1)
-    def _():
-        put_packed(block, high_ref)
+    def put_next():
+        put_row(block, next_normals_ref, next_planes_ref, next_flags_ref, next_courant_ref)
+
+    if chunk_index < chunks - 1:
+        put_next()
+    else:
+        pl.when(step < steps - 1)(put_next)
+
+        @pl.when(step == steps - 1)
+        def _():
+            put_packed(block, 1)
 
     def read_parts(slot):
-        return [parts[slot, k] for k in range(6)]
+        return [get_field(slot, k) for k in range(6)]
 
     @pl.when(step == 0)
     def _():
-        put_packed(block + 1, low_ref)
-        speed = parts[block + 1, 6] + parts[0, 6]
+        if chunk_index == 0:
+            put_packed(block + 1, 0)
+        else:
+            put_row(
+                block + 1, last_normals_ref, last_planes_ref, last_flags_ref, last_courant_ref
+            )
+        speed = get_field(block + 1, 6) + get_field(0, 6)
         kept[0] = upwind_flux(0, read_parts(block + 1), read_parts(0), speed)
         kept[1] = speed
 
@@ -578,24 +699,23 @@
 
     def one_row(row, _):
         own = read_parts(row)
-        speed = parts[row, 6] + parts[row + 1, 6]
+        speed = get_field(row, 6) + get_field(row + 1, 6)
         flux = upwind_flux(0, own, read_parts(row + 1), speed)
         gained = flux - kept[0]
         divergence = speed - kept[1]
         kept[0] = flux
         kept[1] = speed
 
-        half = 0.5 * courant_ref[1, row].astype(F32)
-        above = [None if k == 4 else pltpu.roll(field, layers - 1, 0) for k, field in enumerate(own)]
-        speed = half + pltpu.roll(half, layers - 1, 0)
+        above = [None if k == 4 else get_field(row, k, 1) for k in range(6)]
+        speed = get_field(row, 7) + get_field(row, 7, 1)
         flux = upwind_flux(1, own, above, speed)
-        flux = jnp.where(last_layer, axial_flux_ref[1, row], flux)
-        speed = jnp.where(last_layer, axial_speed_ref[1, row], speed)
+        flux = jnp.where(last_layer, axial_flux_ref[1, pl.ds(row, 1), :], flux)
+        speed = jnp.where(last_layer, axial_speed_ref[1, pl.ds(row, 1), :], speed)
         gained = gained + (
-            flux - jnp.where(first_layer, axial_flux_ref[0, row], pltpu.roll(flux, 1, 0))
+            flux - jnp.where(first_layer, axial_flux_ref[0, pl.ds(row, 1), :], pltpu.roll(flux, 1, 0))
         )
         divergence = divergence + (
-            speed - jnp.where(first_layer, axial_speed_ref[0, row], pltpu.roll(speed, 1, 0))
+            speed - jnp.where(first_layer, axial_speed_ref[0, pl.ds(row, 1), :], pltpu.roll(speed, 1, 0))
         )
 
         half = 0.5 * courant_ref[2, row].astype(F32)
@@ -616,7 +736,7 @@
             ]
         return 0
 
-    lax.fori_loop(0, block, one_row, 0)
+    lax.fori_loop(0, block, one_row, 0, unroll=2)
 
     @pl.when(step == steps - 1)
     def _():
@@ -668,9 +788,9 @@
     whole = pl.BlockSpec((block, layers, cells), lambda i: (here(i), 0, 0))
     triple = pl.BlockSpec((3, block, layers, cells), lambda i: (0, here(i), 0, 0))
     row = pl.BlockSpec((1, layers, cells), lambda i: (after(i), 0, 0))
-    low = pl.BlockSpec((1, 5, layers, cells), lambda i: (2 * chunk_index, 0, 0, 0))
-    high = pl.BlockSpec((1, 5, layers, cells), lambda i: (2 * chunk_index + 3, 0, 0, 0))
-    edge = pl.BlockSpec((2, block, 1, cells), lambda i: (0, here(i), 0, 0))
+    before = max(first * block - 1, 0)
+    last_row = pl.BlockSpec((1, layers, cells), lambda i: (before, 0, 0))
+    edge = pl.BlockSpec((2, block, cells), lambda i: (0, here(i), 0))
     in_specs = [
         whole,
         triple,
@@ -681,8 +801,11 @@
         row,
         row,
         pl.BlockSpec((1, 1, layers, cells), lambda i: (0, after(i), 0, 0)),
-        low,
-        high,
+        pl.BlockSpec((3, 1, layers, cells), lambda i: (0, before, 0, 0)),
+        last_row,
+        last_row,
+        pl.BlockSpec((1, 1, layers, cells), lambda i: (0, before, 0, 0)),
+        pl.BlockSpec(ends.shape, lambda i: (0, 0, 0, 0)),
         edge,
         edge,
         pl.BlockSpec((2, cells, cells), lambda i: (0, 0, 0)),
@@ -690,7 +813,8 @@
     operands = [
         fraction, normals, planes, flags, courant,
         normals, planes, flags, courant,
-        ends, ends, axial_flux, axial_speed, basis,
+        normals, planes, flags, courant,
+        ends, axial_flux, axial_speed, basis,
     ]
     aliases = {}
     if base is not None:
@@ -698,7 +822,7 @@
         operands.append(base)
         aliases = {len(operands) - 1: 0}
     return pl.pallas_call(
-        functools.partial(chunk_kernel, around, base is not None),
+        functools.partial(chunk_kernel, around, chunk_index, rows // chunk),
         grid=(steps,),
         in_specs=in_specs,
         out_specs=[
@@ -710,14 +834,14 @@
             jax.ShapeDtypeStruct((devices, share + 1, layers, chunk), jnp.int16),
         ],
         scratch_shapes=[
-            pltpu.VMEM((block + 2, 7, layers, cells), F32),
+            pltpu.VMEM((8, cells // 128, (block + 2) * layers, 128), F32),
             pltpu.VMEM((2, layers, cells), F32),
             pltpu.VMEM((cells // 128, layers * chunk, 128), F32),
             pltpu.VMEM((cells * layers, chunk), F32),
             pltpu.VMEM((cells, chunk), F32),
         ],
         input_output_aliases=aliases,
-        compiler_params=pltpu.CompilerParams(vmem_limit_bytes=48 * 2**20),
+        compiler_params=pltpu.CompilerParams(vmem_limit_bytes=60 * 2**20),
         cost_estimate=pl.CostEstimate(
             flops=40000 * chunk * layers * cells, bytes_accessed=30 * chunk * layers * cells, transcendentals=0
         ),
@@ -893,7 +1017,7 @@
             pltpu.VMEM(back.shape, BF16),
             pltpu.SemaphoreType.DMA((2,)),
         ],
-        compiler_params=pltpu.CompilerParams(vmem_limit_bytes=48 * 2**20),
+        compiler_params=pltpu.CompilerParams(vmem_limit_bytes=60 * 2**20),
         cost_estimate=pl.CostEstimate(
             flops=60 * rows * width * width * steps, bytes_accessed=20 * 2**20, transcendentals=0
         ),
@@ -976,7 +1100,7 @@
             pltpu.VMEM((4 * lanes, groups * devices * share), BF16),
             pltpu.VMEM((4 * lanes, groups * devices * share), BF16),
         ],
-        compiler_params=pltpu.CompilerParams(vmem_limit_bytes=48 * 2**20),
+        compiler_params=pltpu.CompilerParams(vmem_limit_bytes=60 * 2**20),
         name="pressure_of",
     )(*got, *got, basis)
 
@@ -1022,22 +1146,10 @@
     devices = around * along
     modes = cells // devices
     chunks, groups = rows // CHUNK, 2
-    edge = edge_speeds(courant)
-    below = shifted_in(edge[1], "axial", False)
-    above = shifted_in(edge[0], "axial", True)
-    packs = packed_rows(normals, planes, cell_flags, courant, CHUNK)
-    low_row = shifted_in(packs[-1:], "azim", False)
-    high_row = shifted_in(packs[:1], "azim", True)
-    fields = edge_fields(normals, planes, cell_flags)
-    own, code, speed = donors(fields, edge, below, above)
-    from_below = shifted_in(code[1], "axial", False)
-    from_above = shifted_in(code[0], "axial", True)
-    axial_flux = own + jnp.stack([from_below, from_above]).astype(F32) * (1.0 / FLUX_SCALE)
-    axial_flux, axial_speed = axial_flux[:, :, None], speed[:, :, None]
+    axial_flux, axial_speed, ends = halos(normals, planes, cell_flags, courant)
     forward_basis = halves(radial_basis.T)
     arrays = (fraction, normals, planes, cell_flags, courant)
     updated, got = None, []
-    ends = jnp.concatenate([low_row, packs, high_row])
     for chunk in range(chunks):
         updated, sent = advect_chunk(
             arrays, ends, axial_flux, axial_speed, forward_basis, chunk, CHUNK, around, devices, updated
@@ -1071,6 +1183,7 @@
         and modes // 2 * chunks == layers
         and cells % 128 == 0
         and around % 4 == 0
+        and along > 2
     )
 
 

time: 376 us -> 355 us (0.944)
  local copies, waits for them, and re-layouts: 22.4 us -> 9.93 us
  starting transfers between devices: 28.7 us -> 17.4 us
  Pallas kernels: 186 us -> 193 us
  waiting for transfers between devices: 132 us -> 128 us
    ppermute x6 -> x0, starting transfers between devices: 9.84 us -> none  [shifted_in(): return lax.ppermute(edge, axis, pairs)]
    unnamed x49 -> x11, local copies, waits for them, and re-layouts: 13.9 us -> 4.3 us
    ppermute x6 -> x0, waiting for transfers between devices: 6.99 us -> none  [shifted_in(): return lax.ppermute(edge, axis, pairs)]
    pallas_call x2, Pallas kernels: 37.2 us -> 41 us  [solve_group(): pl.pallas_call(functools.partial(solve_kernel, around, along, chunks, gro...]
    pallas_call x6 -> x3, Pallas kernels: 127 us -> 128 us  [the longest x2 91.6 us: advect_chunk(): pl.pallas_call(functools.partial(chunk_kernel, around, chunk_index, rows...]
  transfers between devices with their start and end apart: 10 -> 4, of which waited for: 5 -> 4; matrix products, arithmetic and copies ran while one was open for 3% -> 3% of each run, Pallas kernels for 24% -> 19%
where the time goes in v2:
time: 355 us; the launch traced here: 354 us
  Pallas kernels  193 us (54%)
  waiting for transfers between devices  128 us (36%)
  starting transfers between devices  17.4 us (5%)
  local copies, waits for them, and re-layouts  9.93 us (3%)
  other arithmetic  5.61 us (2%)
    all_to_all x4, waiting for transfers between devices, exchanged(): lax.all_to_all(sent, ('azim', 'axial'), split_axis=0, concat_axis=0, tile...  128 us
    pallas_call x2, Pallas kernels, advect_chunk(): pl.pallas_call(functools.partial(chunk_kernel, around, chunk_index, rows...  91.6 us
    pallas_call x2, Pallas kernels, solve_group(): pl.pallas_call(functools.partial(solve_kernel, around, along, chunks, gro...  41 us
    pallas_call x1, Pallas kernels, halos(): pl.pallas_call(halo_kernel, grid=(2 * half,), in_specs=in_specs, out_spec...  36.7 us
    pallas_call x1, Pallas kernels, pressure_of(): pl.pallas_call(functools.partial(pressure_kernel, around, groups), grid=(...  23.2 us
    all_to_all x4, starting transfers between devices, exchanged(): lax.all_to_all(sent, ('azim', 'axial'), split_axis=0, concat_axis=0, tile...  17.4 us
  transfers between devices with their start and end apart: 4, of which 4 were waited for; matrix products, arithmetic and copies ran while one was open for 3% of the time, Pallas kernels for 19%

profile of v2, /device:TPU:1, one launch (start us, length us, event | category | flops | bytes accessed | tf_op | source)
XLA Modules:
  0.0 354.0 jit_solution(16141483281359607724)
XLA Ops:
  0.6 1.6 copy.20
  2.2 0.2 fusion.3
  2.4 1.1 pad_maximum_fusion.basis_ref
  3.5 36.7 %halos.1 = (f32[2,256,512]{2,1,0:T(8,128)}, f32[2,256,512]{2,1,0:T(8,128)}, bf16[2,5,16,512]{3,2,1,0:T(8,128)(2,1)}) custom-call(bf16[3,256,16,512]{3,2,1,0:T(8,128)(2,1)} %last_courant_ref.5, bf16[3,256,16,512]{3,2,1,0:T(8,128)(2,1)} %last_normals_ref.5, bf16[256,16,512]{2,1,0:T(8,128)(2,1)} %last_planes_ref.5, s32[256,16,512]{2,1,0:T(8,128)} %last_flags_ref.5, ...), custom_call_target="tpu_custom_call" | custom-call | tf_op jit(solution)/shard_map/halos/pallas_call | solution.py:550
  40.2 45.9 %advect_chunk.2 = (f32[256,16,512]{2,1,0:T(8,128)}, s16[32,17,16,128]{3,2,1,0:T(8,128)(2,1)}) custom-call(f32[256,16,512]{2,1,0:T(8,128)} %fraction_ref.3, bf16[3,256,16,512]{3,2,1,0:T(8,128)(2,1)} %last_normals_ref.5, bf16[256,16,512]{2,1,0:T(8,128)(2,1)} %last_planes_ref.5, s32[256,16,512]{2,1,0:T(8,128)} %last_flags_ref.5, ...), custom_call_target="tpu_custom_call" | custom-call | flops 41943040000 | bytes 31457280 | tf_op jit(solution)/shard_map/advect_chunk/pallas_call | solution.py:824
  86.0 6.3 %all-to-all-start = ((s16[32,17,16,128]{3,2,1,0:T(8,128)(2,1)}), s16[32,17,16,128]{3,2,1,0:T(8,128)(2,1)S(1)}, u32[]{:S(2)}, u32[]{:S(2)}) async-start(s16[32,17,16,128]{3,2,1,0:T(8,128)(2,1)} %get-tuple-element.14), calls=%async_computation | async-start | bytes 4456448 | tf_op jit(solution)/shard_map/all_to_all | solution.py:1114
  92.4 45.8 %advect_chunk.3 = (f32[256,16,512]{2,1,0:T(8,128)}, s16[32,17,16,128]{3,2,1,0:T(8,128)(2,1)}) custom-call(f32[256,16,512]{2,1,0:T(8,128)} %fraction_ref.3, bf16[3,256,16,512]{3,2,1,0:T(8,128)(2,1)} %last_normals_ref.5, bf16[256,16,512]{2,1,0:T(8,128)(2,1)} %last_planes_ref.5, s32[256,16,512]{2,1,0:T(8,128)} %last_flags_ref.5, ...), custom_call_target="tpu_custom_call", output_to_operand_aliasing={{0}: (17, {})} | custom-call | flops 41943040000 | bytes 31457280 | tf_op jit(solution)/shard_map/advect_chunk/pallas_call | solution.py:824
  138.1 5.2 %all-to-all-done.earlier_ref.refs_0_.refs_2_ = s16[32,17,16,128]{3,2,1,0:T(8,128)(2,1)S(1)} async-done(((s16[32,17,16,128]{3,2,1,0:T(8,128)(2,1)}), s16[32,17,16,128]{3,2,1,0:T(8,128)(2,1)S(1)}, u32[]{:S(2)}, u32[]{:S(2)}) %all-to-all-start) | async-done | bytes 2228256 | tf_op jit(solution)/shard_map/all_to_all | solution.py:1114
  143.4 1.4 copy-done.1
  144.7 3.7 %all-to-all-start.1 = ((s16[32,17,16,128]{3,2,1,0:T(8,128)(2,1)}), s16[32,17,16,128]{3,2,1,0:T(8,128)(2,1)S(1)}, u32[]{:S(2)}, u32[]{:S(2)}) async-start(s16[32,17,16,128]{3,2,1,0:T(8,128)(2,1)} %following.1), calls=%async_computation.1 | async-start | bytes 4456448 | tf_op jit(solution)/shard_map/all_to_all | solution.py:1114
  148.4 0.8 dynamic_slice.3
  149.2 0.0 copy-done.4
  149.2 0.1 broadcast_add_fusion
  149.2 1.3 add.35.refs_10_
  150.5 0.1 copy.21
  150.6 1.2 broadcast_multiply_fusion
  151.8 2.1 mul.75
  153.9 1.4 mul.72
  155.2 1.0 reduce-precision_convert_fusion.2
  156.3 0.8 pad_maximum_fusion.2
  157.1 42.3 %all-to-all-done.1.refs_1_.refs_3_ = s16[32,17,16,128]{3,2,1,0:T(8,128)(2,1)S(1)} async-done(((s16[32,17,16,128]{3,2,1,0:T(8,128)(2,1)}), s16[32,17,16,128]{3,2,1,0:T(8,128)(2,1)S(1)}, u32[]{:S(2)}, u32[]{:S(2)}) %all-to-all-start.1) | async-done | bytes 2228256 | tf_op jit(solution)/shard_map/all_to_all | solution.py:1114
  199.4 1.4 copy-done.2
  200.8 20.5 %solve_group.3 = s16[32,17,16,128]{3,2,1,0:T(8,128)(2,1)} custom-call(s16[32,17,16,128]{3,2,1,0:T(8,128)(2,1)} %copy-done.1, s16[32,17,16,128]{3,2,1,0:T(8,128)(2,1)} %copy-done.2, s16[32,17,16,128]{3,2,1,0:T(8,128)(2,1)} %copy-done.1, s16[32,17,16,128]{3,2,1,0:T(8,128)(2,1)} %copy-done.2, bf16[2,256,256]{2,1,0:T(8,128)(2,1)} %get-tuple-element.26.refs_4_, ...), custom_call_target="tpu_custom_call" | custom-call | flops 8053063680 | bytes 20971520 | tf_op jit(solution)/shard_map/solve_group/pallas_call | solution.py:996
  221.3 3.7 %all-to-all-start.3 = ((s16[32,17,16,128]{3,2,1,0:T(8,128)(2,1)}), s16[32,17,16,128]{3,2,1,0:T(8,128)(2,1)S(1)}, u32[]{:S(2)}, u32[]{:S(2)}) async-start(s16[32,17,16,128]{3,2,1,0:T(8,128)(2,1)} %solve_group.3), calls=%async_computation.3 | async-start | bytes 4456448 | tf_op jit(solution)/shard_map/all_to_all | solution.py:1114
  225.0 20.5 %solve_group.2 = s16[32,17,16,128]{3,2,1,0:T(8,128)(2,1)} custom-call(s16[32,17,16,128]{3,2,1,0:T(8,128)(2,1)} %copy-done.1, s16[32,17,16,128]{3,2,1,0:T(8,128)(2,1)} %copy-done.2, s16[32,17,16,128]{3,2,1,0:T(8,128)(2,1)} %copy-done.1, s16[32,17,16,128]{3,2,1,0:T(8,128)(2,1)} %copy-done.2, bf16[2,256,256]{2,1,0:T(8,128)(2,1)} %get-tuple-element.26.refs_4_, ...), custom_call_target="tpu_custom_call" | custom-call | flops 8053063680 | bytes 20971520 | tf_op jit(solution)/shard_map/solve_group/pallas_call | solution.py:996
  245.5 30.5 %all-to-all-done.3.refs_1_.refs_3_ = s16[32,17,16,128]{3,2,1,0:T(8,128)(2,1)S(1)} async-done(((s16[32,17,16,128]{3,2,1,0:T(8,128)(2,1)}), s16[32,17,16,128]{3,2,1,0:T(8,128)(2,1)S(1)}, u32[]{:S(2)}, u32[]{:S(2)}) %all-to-all-start.3) | async-done | bytes 2228256 | tf_op jit(solution)/shard_map/all_to_all | solution.py:1114
  276.0 3.7 %all-to-all-start.2 = ((s16[32,17,16,128]{3,2,1,0:T(8,128)(2,1)}), s16[32,17,16,128]{3,2,1,0:T(8,128)(2,1)}, u32[]{:S(2)}, u32[]{:S(2)}) async-start(s16[32,17,16,128]{3,2,1,0:T(8,128)(2,1)} %solve_group.2), calls=%async_computation.2 | async-start | bytes 4456448 | tf_op jit(solution)/shard_map/all_to_all | solution.py:1114
  279.7 0.1 copy.24
  279.8 0.2 reduce-precision_convert_fusion
  280.0 1.1 pad_maximum_fusion.1.refs_4_
  281.1 49.7 %all-to-all-done.2.refs_0_.refs_2_ = s16[32,17,16,128]{3,2,1,0:T(8,128)(2,1)} async-done(((s16[32,17,16,128]{3,2,1,0:T(8,128)(2,1)}), s16[32,17,16,128]{3,2,1,0:T(8,128)(2,1)}, u32[]{:S(2)}, u32[]{:S(2)}) %all-to-all-start.2) | async-done | bytes 2228256 | tf_op jit(solution)/shard_map/all_to_all | solution.py:1114
  330.8 23.2 %pressure_of.1 = f32[256,16,512]{2,1,0:T(8,128)} custom-call(s16[32,17,16,128]{3,2,1,0:T(8,128)(2,1)} %all-to-all-done.2.refs_0_.refs_2_, s16[32,17,16,128]{3,2,1,0:T(8,128)(2,1)} %copy-done, s16[32,17,16,128]{3,2,1,0:T(8,128)(2,1)} %all-to-all-done.2.refs_0_.refs_2_, s16[32,17,16,128]{3,2,1,0:T(8,128)(2,1)} %copy-done, ...), custom_call_target="tpu_custom_call" | custom-call | tf_op jit(solution)/shard_map/pressure_of/pallas_call | solution.py:1084
  (10 shorter events, 0.1 us)
Async XLA Ops:
  86.0 57.3 %all-to-all-start = ((s16[32,17,16,128]{3,2,1,0:T(8,128)(2,1)}), s16[32,17,16,128]{3,2,1,0:T(8,128)(2,1)S(1)}, u32[]{:S(2)}, u32[]{:S(2)}) async-start(s16[32,17,16,128]{3,2,1,0:T(8,128)(2,1)} %get-tuple-element.14), calls=%async_computation | async-start | bytes 4456448 | tf_op jit(solution)/shard_map/all_to_all | solution.py:1114
  143.4 1.4 copy-start.1
  144.7 4.4 %copy-start.4 = (f32[64]{0:T(128)S(1)}, f32[64]{0:T(128)}, u32[]{:S(2)}) copy-start(f32[64]{0:T(128)} %param.21) | copy-start | bytes 772
  144.7 5.8 %copy-start.3 = (f32[64,64]{1,0:T(8,128)S(1)}, f32[64,64]{1,0:T(8,128)}, u32[]{:S(2)}) copy-start(f32[64,64]{1,0:T(8,128)} %param.19) | copy-start | bytes 49156
  144.7 54.7 %all-to-all-start.1 = ((s16[32,17,16,128]{3,2,1,0:T(8,128)(2,1)}), s16[32,17,16,128]{3,2,1,0:T(8,128)(2,1)S(1)}, u32[]{:S(2)}, u32[]{:S(2)}) async-start(s16[32,17,16,128]{3,2,1,0:T(8,128)(2,1)} %following.1), calls=%async_computation.1 | async-start | bytes 4456448 | tf_op jit(solution)/shard_map/all_to_all | solution.py:1114
  199.4 1.4 copy-start.2
  221.3 54.7 %all-to-all-start.3 = ((s16[32,17,16,128]{3,2,1,0:T(8,128)(2,1)}), s16[32,17,16,128]{3,2,1,0:T(8,128)(2,1)S(1)}, u32[]{:S(2)}, u32[]{:S(2)}) async-start(s16[32,17,16,128]{3,2,1,0:T(8,128)(2,1)} %solve_group.3), calls=%async_computation.3 | async-start | bytes 4456448 | tf_op jit(solution)/shard_map/all_to_all | solution.py:1114
  276.0 4.0 %copy-start = (s16[32,17,16,128]{3,2,1,0:T(8,128)(2,1)}, s16[32,17,16,128]{3,2,1,0:T(8,128)(2,1)S(1)}, u32[]{:S(2)}) copy-start(s16[32,17,16,128]{3,2,1,0:T(8,128)(2,1)S(1)} %all-to-all-done.3.refs_1_.refs_3_) | copy-start | bytes 6684676
  276.0 54.8 %all-to-all-start.2 = ((s16[32,17,16,128]{3,2,1,0:T(8,128)(2,1)}), s16[32,17,16,128]{3,2,1,0:T(8,128)(2,1)}, u32[]{:S(2)}, u32[]{:S(2)}) async-start(s16[32,17,16,128]{3,2,1,0:T(8,128)(2,1)} %solve_group.2), calls=%async_computation.2 | async-start | bytes 4456448 | tf_op jit(solution)/shard_map/all_to_all | solution.py:1114

commit v3 on v2

--- a/solution.py
+++ b/solution.py
@@ -297,6 +297,7 @@
 
 CHUNK = 128
 BLOCK = 16
+SOLVED = ((0, 4), (8, 8), (4, 4))
 FLUX_SCALE = 32767.0 / 0.3
 F32 = jnp.float32
 BF16 = jnp.bfloat16
@@ -389,7 +390,8 @@
     step = pl.program_id(0)
     half = pl.num_programs(0) // 2
     span, layers, cells = planes_ref.shape
-    groups, group = code_send.shape[1], code.shape[2]
+    groups, group = code.shape[1:3]
+    per_group = group // span
     tiles = cells // 128
     neighbours = []
     for axis in ("azim", "axial"):
@@ -412,10 +414,14 @@
         remote(packs.at[s], packs_in.at[1 - s], row_send.at[s], row_recv.at[1 - s], neighbours[0][s])
         for s in range(2)
     ]
-    edge_copies = [
-        remote(edge.at[s], edge_in.at[1 - s], edge_send.at[s], edge_recv.at[1 - s], neighbours[1][s])
-        for s in range(2)
-    ]
+    def edge_copy(s, g):
+        return remote(
+            edge.at[s, g],
+            edge_in.at[1 - s, g],
+            edge_send.at[s, g],
+            edge_recv.at[1 - s, g],
+            neighbours[1][s],
+        )
 
     def code_copy(s, g):
         return remote(
@@ -453,17 +459,20 @@
 
     @pl.when(step < half)
     def _():
-        at = pl.ds(pl.multiple_of(step * span, span), span)
+        place = step // per_group
+        at = pl.ds(pl.multiple_of(lax.rem(step, per_group) * span, span), span)
         for tile in range(tiles):
             lanes = pl.ds(tile * 128, 128)
             work[tile] = courant_ref[0, :, :, lanes].astype(F32).reshape(span * layers, 128)
             for s, layer in ((0, 0), (1, layers - 1)):
-                edge[s, at, lanes] = layer_rows(tile, layer).astype(BF16)
-
-    @pl.when(step == half - 1)
-    def _():
-        for copy in edge_copies:
-            copy.start()
+                edge[s, place, at, lanes] = layer_rows(tile, layer).astype(BF16)
+
+    for g in range(groups):
+
+        @pl.when(step == (g + 1) * per_group - 1)
+        def _(g=g):
+            for s in range(2):
+                edge_copy(s, g).start()
 
     @pl.when(step >= half)
     def _():
@@ -479,18 +488,20 @@
                 for s, layer in ((0, 0), (1, layers - 1)):
                     fields[s, k, at, lanes] = layer_rows(tile, layer)
 
-    @pl.when(step == 2 * half - 1)
-    def _():
-        for copy in edge_copies:
-            copy.wait()
-        for g in range(groups):
+    for g in range(groups):
+
+        @pl.when(step == half + (g + 1) * per_group - 1)
+        def _(g=g):
             for s in range(2):
-
-                def donate(piece, _, g=g, s=s):
+                edge_copy(s, g).wait()
+            for s in range(2):
+
+                def donate(piece, _, s=s):
                     inside = pl.ds(pl.multiple_of(piece * 16, 16), 16)
                     at = pl.ds(pl.multiple_of(g * group + piece * 16, 16), 16)
                     normals = [fields[s, k, at, :] for k in range(3)]
-                    speed = 0.5 * (edge[s, at, :].astype(F32) + edge_in[s, at, :].astype(F32))
+                    own, beyond = edge[s, g, inside, :], edge_in[s, g, inside, :]
+                    speed = 0.5 * (own.astype(F32) + beyond.astype(F32))
                     inverse = inverse_of(*normals)
                     flux = slab_flux(
                         normals[1],
@@ -508,6 +519,9 @@
 
                 lax.fori_loop(0, group // 16, donate, 0)
                 code_copy(s, g).start()
+
+    @pl.when(step == 2 * half - 1)
+    def _():
         for copy in row_copies:
             copy.wait()
         ends_ref[...] = packs_in[...]
@@ -559,8 +573,8 @@
         ],
         scratch_shapes=[
             pltpu.VMEM((cells // 128, span * layers, 128), F32),
-            pltpu.VMEM((2, rows, cells), BF16),
-            pltpu.VMEM((2, rows, cells), BF16),
+            pltpu.VMEM(split_shape, BF16),
+            pltpu.VMEM(split_shape, BF16),
             pltpu.VMEM((2, 4, rows, cells), F32),
             pltpu.VMEM(split_shape, jnp.int16),
             pltpu.VMEM(split_shape, jnp.int16),
@@ -568,8 +582,8 @@
             pltpu.VMEM(ends, BF16),
             dma((2,)),
             dma((2,)),
-            dma((2,)),
-            dma((2,)),
+            dma((2, groups)),
+            dma((2, groups)),
             dma((2, groups)),
             dma((2, groups)),
         ],
@@ -883,7 +897,7 @@
     return jnp.exp2(decoded(codes) * (1.0 / 256.0)) * (1.0 / CODE_TOP)
 
 
-def solve_kernel(around, along, chunks, group, *refs):
+def solve_kernel(around, along, chunks, start, *refs):
     got = refs[:chunks]
     extra = refs[chunks : 2 * chunks]
     mix, unmix, forth_ref, back_ref, rates, weights, shifts = refs[2 * chunks : 2 * chunks + 7]
@@ -902,9 +916,11 @@
     share = (sent.shape[1] - 1) // chunks
     pairs = around // 4
     step = pl.program_id(0)
-    first = group * share + step * count
+    first = start + step * count
     for chunk in range(chunks):
         scale[chunk] = scale_of(extra[chunk][:, 0])
+    if chunks * share < layers:
+        exponents[...] = jnp.zeros_like(exponents)
 
     def spots():
         for pair in range(pairs):
@@ -979,13 +995,13 @@
         sent[:, chunks * share] = exponents[...].astype(jnp.int32).astype(jnp.int16)
 
 
-def solve_group(got, mix, unmix, tables, shifts, group, groups, around, along):
+def solve_group(got, mix, unmix, tables, shifts, start, share, around, along):
     chunks = len(got)
     devices, slots, layers, lanes = got[0].shape
     modes = slots - 1
-    share = modes // groups
     count = share
     steps = share // count
+    block = start // count
     rows = count * along * layers
     forth, back, rates, weights = tables
     width = forth.shape[-1]
@@ -994,18 +1010,20 @@
         return pl.BlockSpec(array.shape, lambda i: (0,) * array.ndim, pipeline_mode=pl.Buffered(1))
 
     return pl.pallas_call(
-        functools.partial(solve_kernel, around, along, chunks, group),
+        functools.partial(solve_kernel, around, along, chunks, start),
         grid=(steps,),
         in_specs=[
-            pl.BlockSpec((devices, count, layers, lanes), lambda i: (0, group * steps + i, 0, 0))
+            pl.BlockSpec((devices, count, layers, lanes), lambda i: (0, block + i, 0, 0))
         ]
         * chunks
         + [pl.BlockSpec((devices, 1, layers, lanes), lambda i: (0, modes, 0, 0))] * chunks
         + [fixed(mix), fixed(unmix)]
         + [pl.BlockSpec(memory_space=pl.ANY)] * 2
         + [fixed(rates), fixed(weights)]
-        + [pl.BlockSpec((rows, 1), lambda i: (group * steps + i, 0))],
-        out_specs=pl.BlockSpec((devices, slots, layers, lanes), lambda i: (0, 0, 0, 0)),
+        + [pl.BlockSpec((rows, 1), lambda i: (block + i, 0))],
+        out_specs=pl.BlockSpec(
+            (devices, chunks * share + 1, layers, lanes), lambda i: (0, 0, 0, 0)
+        ),
         out_shape=jax.ShapeDtypeStruct((devices, chunks * share + 1, layers, lanes), jnp.int16),
         scratch_shapes=[
             pltpu.VMEM((4, rows, width), BF16),
@@ -1028,8 +1046,10 @@
 def pressure_kernel(around, groups, *refs):
     got = refs[:groups]
     extra = refs[groups : 2 * groups]
-    basis, out, flat, wide, scale, high, low = refs[2 * groups :]
-    devices, share, layers, lanes = got[0].shape
+    basis = refs[2 * groups]
+    base = refs[2 * groups + 1 : -6]
+    out, flat, wide, scale, high, low = refs[-6:]
+    devices, _, layers, lanes = got[0].shape
     lane_tiles = out.shape[2] // 128
     chunk = pl.program_id(0)
     backwards = lax.rem(lax.axis_index("azim"), around // 2) >= around // 4
@@ -1037,28 +1057,32 @@
     j = lax.broadcasted_iota(jnp.int32, (lanes, lanes), 1)
     turned_place = jnp.where(backwards, lanes - 1, 0) + jnp.where(backwards, -1, 1) * i
     turn = jnp.where(j == turned_place, 1.0, 0.0).astype(BF16)
+    spans, filled = [], 0
     for group in range(groups):
+        share = got[group].shape[1]
+        spans.append((filled, devices * share))
         scale[group] = scale_of(extra[group][:, 0])
 
-        def unpack(device, _, group=group):
+        def unpack(device, _, group=group, share=share, filled=filled):
             for mode in range(share):
-                at = pl.multiple_of((device * share + mode) * layers, layers)
-                flat[group, pl.ds(at, layers), :] = (
+                at = pl.multiple_of((filled + device * share + mode) * layers, layers)
+                flat[pl.ds(at, layers), :] = (
                     decoded(got[group][device, mode])
                     * scale[group, device, pl.ds(chunk * share + mode, 1), :]
                 )
             return 0
 
         lax.fori_loop(0, devices, unpack, 0)
+        filled += devices * share
 
     together = high.shape[0] // lanes
 
     def radial(batch, _):
         for part in range(together):
-            for group in range(groups):
+            for offset, height in spans:
                 z = batch * together + part
-                values = split(flat[group, pl.ds(z, devices * share, stride=layers), :])
-                at = pl.ds(group * devices * share, devices * share)
+                values = split(flat[pl.ds(offset * layers + z, height, stride=layers), :])
+                at = pl.ds(offset, height)
                 for target, value in zip((high, low), values):
                     target[part * lanes : (part + 1) * lanes, at] = dot(
                         turn, value, ((1,), (1,))
@@ -1073,36 +1097,44 @@
 
     lax.fori_loop(0, layers // together, radial, 0)
     for tile in range(lane_tiles):
-        out[:, :, tile * 128 : (tile + 1) * 128] = wide[tile].reshape(lanes, layers, 128)
-
-
-def pressure_of(got, basis, around, chunks):
+        at = slice(tile * 128, (tile + 1) * 128)
+        result = wide[tile].reshape(lanes, layers, 128)
+        out[:, :, at] = result + base[0][:, :, at] if base else result
+
+
+def pressure_of(got, basis, around, chunks, base=None):
     groups = len(got)
-    devices, slots, layers, lanes = got[0].shape
-    share = (slots - 1) // chunks
-    cells = basis.shape[-1]
+    devices, _, layers, lanes = got[0].shape
+    shares = [(x.shape[1] - 1) // chunks for x in got]
+    inner, cells = basis.shape[1:]
+    whole = pl.BlockSpec((lanes, layers, cells), lambda i: (i, 0, 0))
     return pl.pallas_call(
         functools.partial(pressure_kernel, around, groups),
         grid=(chunks,),
-        in_specs=[pl.BlockSpec((devices, share, layers, lanes), lambda i: (0, i, 0, 0))] * groups
-        + [pl.BlockSpec((devices, 1, layers, lanes), lambda i: (0, chunks * share, 0, 0))] * groups
+        in_specs=[pl.BlockSpec((devices, share, layers, lanes), lambda i: (0, i, 0, 0)) for share in shares]
         + [
-            pl.BlockSpec(
-                basis.shape, lambda i: (0,) * basis.ndim, pipeline_mode=pl.Buffered(1)
-            )
-        ],
-        out_specs=pl.BlockSpec((lanes, layers, cells), lambda i: (i, 0, 0)),
+            pl.BlockSpec((devices, 1, layers, lanes), lambda i, share=share: (0, chunks * share, 0, 0))
+            for share in shares
+        ]
+        + [pl.BlockSpec(basis.shape, lambda i: (0, 0, 0), pipeline_mode=pl.Buffered(1))]
+        + ([] if base is None else [whole]),
+        out_specs=whole,
         out_shape=jax.ShapeDtypeStruct((lanes * chunks, layers, cells), F32),
         scratch_shapes=[
-            pltpu.VMEM((groups, devices * share * layers, lanes), F32),
+            pltpu.VMEM((inner * layers, lanes), F32),
             pltpu.VMEM((cells // 128, lanes * layers, 128), F32),
             pltpu.VMEM((groups, devices, layers, lanes), F32),
-            pltpu.VMEM((4 * lanes, groups * devices * share), BF16),
-            pltpu.VMEM((4 * lanes, groups * devices * share), BF16),
+            pltpu.VMEM((4 * lanes, inner), BF16),
+            pltpu.VMEM((4 * lanes, inner), BF16),
         ],
         compiler_params=pltpu.CompilerParams(vmem_limit_bytes=60 * 2**20),
+        cost_estimate=pl.CostEstimate(
+            flops=20 * lanes * chunks * layers * cells * inner,
+            bytes_accessed=20 * 2**20,
+            transcendentals=0,
+        ),
         name="pressure_of",
-    )(*got, *got, basis)
+    )(*got, *got, basis, *([] if base is None else [base]))
 
 
 def halves(values):
@@ -1145,7 +1177,7 @@
     around, along = lax.axis_size("azim"), lax.axis_size("axial")
     devices = around * along
     modes = cells // devices
-    chunks, groups = rows // CHUNK, 2
+    chunks = rows // CHUNK
     axial_flux, axial_speed, ends = halos(normals, planes, cell_flags, courant)
     forward_basis = halves(radial_basis.T)
     arrays = (fraction, normals, planes, cell_flags, courant)
@@ -1161,13 +1193,14 @@
     shifts = lax.dynamic_slice_in_dim(radial_rates, first, modes)[:, None] + axial_rates[None, :]
     shifts = shifts.reshape(modes * along * layers, 1)
     tables = [jnp.asarray(x) for x in folded_tables(rows * around)]
-    returned = []
-    for group in range(groups):
-        sent = solve_group(got, mix, unmix, tables, shifts, group, groups, around, along)
-        returned.append(exchanged(sent))
-    back_basis = radial_basis.T.reshape(devices, groups, modes // groups, cells)
-    back_basis = halves(back_basis.transpose(1, 0, 2, 3).reshape(-1, cells))
-    pressure = pressure_of(returned, back_basis, around, chunks)
+    returned, bases = [], []
+    for start, share in SOLVED:
+        sent = solve_group(got, mix, unmix, tables, shifts, start, share, around, along)
+        returned.append(exchanged(following(sent, returned[-1]) if returned else sent))
+        rows_of = radial_basis.T.reshape(devices, modes, cells)[:, start : start + share]
+        bases.append(rows_of.reshape(devices * share, cells))
+    pressure = pressure_of(returned[:-1], halves(jnp.concatenate(bases[:-1])), around, chunks)
+    pressure = pressure_of(returned[-1:], halves(bases[-1]), around, chunks, pressure)
     return (updated, pressure)
 
 

time: 355 us -> 349 us (0.983)
  waiting for transfers between devices: 128 us -> 94.9 us
  Pallas kernels: 193 us -> 210 us
  local copies, waits for them, and re-layouts: 9.93 us -> 17.2 us
    all_to_all x4 -> x5, waiting for transfers between devices: 128 us -> 94.9 us  [exchanged(): lax.all_to_all(sent, ('azim', 'axial'), split_axis=0, concat_axis=0, tile...]
    pallas_call x1 -> x2, Pallas kernels: 23.2 us -> 37 us  [pressure_of(): pl.pallas_call(functools.partial(pressure_kernel, around, groups), grid=(...]
    pallas_call x2 -> x3, Pallas kernels: 41 us -> 49.2 us  [solve_group(): pl.pallas_call(functools.partial(solve_kernel, around, along, chunks, sta...]
    pallas_call x1, Pallas kernels: 36.7 us -> 32.6 us  [halos(): pl.pallas_call(halo_kernel, grid=(2 * half,), in_specs=in_specs, out_spec...]
    unnamed x11 -> x17, local copies, waits for them, and re-layouts: 4.3 us -> 7.88 us
    all_to_all x4 -> x5, starting transfers between devices: 17.4 us -> 18.9 us  [exchanged(): lax.all_to_all(sent, ('azim', 'axial'), split_axis=0, concat_axis=0, tile...]
  transfers between devices with their start and end apart: 4 -> 5, of which waited for: 4 -> 5; matrix products, arithmetic and copies ran while one was open for 3% -> 4% of each run, Pallas kernels for 19% -> 29%
where the time goes in v3:
time: 349 us; the launch traced here: 348 us
  Pallas kernels  210 us (60%)
  waiting for transfers between devices  94.9 us (27%)
  starting transfers between devices  18.9 us (5%)
  local copies, waits for them, and re-layouts  17.2 us (5%)
  other arithmetic  6.22 us (2%)
    all_to_all x5, waiting for transfers between devices, exchanged(): lax.all_to_all(sent, ('azim', 'axial'), split_axis=0, concat_axis=0, tile...  94.9 us
    pallas_call x2, Pallas kernels, advect_chunk(): pl.pallas_call(functools.partial(chunk_kernel, around, chunk_index, rows...  91.7 us
    pallas_call x3, Pallas kernels, solve_group(): pl.pallas_call(functools.partial(solve_kernel, around, along, chunks, sta...  49.2 us
    pallas_call x2, Pallas kernels, pressure_of(): pl.pallas_call(functools.partial(pressure_kernel, around, groups), grid=(...  37 us
    pallas_call x1, Pallas kernels, halos(): pl.pallas_call(halo_kernel, grid=(2 * half,), in_specs=in_specs, out_spec...  32.6 us
    all_to_all x5, starting transfers between devices, exchanged(): lax.all_to_all(sent, ('azim', 'axial'), split_axis=0, concat_axis=0, tile...  18.9 us
    unnamed x17, local copies, waits for them, and re-layouts  7.88 us
  transfers between devices with their start and end apart: 5, of which 5 were waited for; matrix products, arithmetic and copies ran while one was open for 4% of the time, Pallas kernels for 29%

profile of v3, /device:TPU:1, one launch (start us, length us, event | category | flops | bytes accessed | tf_op | source)
XLA Modules:
  0.0 348.4 jit_solution(2310353111646234359)
XLA Ops:
  0.6 1.6 copy.21
  2.4 1.1 pad_maximum_fusion.basis_ref
  3.5 32.6 %halos.1 = (f32[2,256,512]{2,1,0:T(8,128)}, f32[2,256,512]{2,1,0:T(8,128)}, bf16[2,5,16,512]{3,2,1,0:T(8,128)(2,1)}) custom-call(bf16[3,256,16,512]{3,2,1,0:T(8,128)(2,1)} %last_courant_ref.5, bf16[3,256,16,512]{3,2,1,0:T(8,128)(2,1)} %last_normals_ref.5, bf16[256,16,512]{2,1,0:T(8,128)(2,1)} %last_planes_ref.5, s32[256,16,512]{2,1,0:T(8,128)} %last_flags_ref.5, ...), custom_call_target="tpu_custom_call" | custom-call | tf_op jit(solution)/shard_map/halos/pallas_call | solution.py:564
  36.1 45.9 %advect_chunk.2 = (f32[256,16,512]{2,1,0:T(8,128)}, s16[32,17,16,128]{3,2,1,0:T(8,128)(2,1)}) custom-call(f32[256,16,512]{2,1,0:T(8,128)} %fraction_ref.3, bf16[3,256,16,512]{3,2,1,0:T(8,128)(2,1)} %last_normals_ref.5, bf16[256,16,512]{2,1,0:T(8,128)(2,1)} %last_planes_ref.5, s32[256,16,512]{2,1,0:T(8,128)} %last_flags_ref.5, ...), custom_call_target="tpu_custom_call" | custom-call | flops 41943040000 | bytes 31457280 | tf_op jit(solution)/shard_map/advect_chunk/pallas_call | solution.py:838
  82.0 4.7 %all-to-all-start = ((s16[32,17,16,128]{3,2,1,0:T(8,128)(2,1)}), s16[32,17,16,128]{3,2,1,0:T(8,128)(2,1)S(1)}, u32[]{:S(2)}, u32[]{:S(2)}) async-start(s16[32,17,16,128]{3,2,1,0:T(8,128)(2,1)} %get-tuple-element.14), calls=%async_computation | async-start | bytes 4456448 | tf_op jit(solution)/shard_map/all_to_all | solution.py:1146
  86.7 45.8 %advect_chunk.3 = (f32[256,16,512]{2,1,0:T(8,128)}, s16[32,17,16,128]{3,2,1,0:T(8,128)(2,1)}) custom-call(f32[256,16,512]{2,1,0:T(8,128)} %fraction_ref.3, bf16[3,256,16,512]{3,2,1,0:T(8,128)(2,1)} %last_normals_ref.5, bf16[256,16,512]{2,1,0:T(8,128)(2,1)} %last_planes_ref.5, s32[256,16,512]{2,1,0:T(8,128)} %last_flags_ref.5, ...), custom_call_target="tpu_custom_call", output_to_operand_aliasing={{0}: (17, {})} | custom-call | flops 41943040000 | bytes 31457280 | tf_op jit(solution)/shard_map/advect_chunk/pallas_call | solution.py:838
  132.5 5.2 %all-to-all-done.earlier_ref.refs_0_.refs_2_ = s16[32,17,16,128]{3,2,1,0:T(8,128)(2,1)S(1)} async-done(((s16[32,17,16,128]{3,2,1,0:T(8,128)(2,1)}), s16[32,17,16,128]{3,2,1,0:T(8,128)(2,1)S(1)}, u32[]{:S(2)}, u32[]{:S(2)}) %all-to-all-start) | async-done | bytes 2228256 | tf_op jit(solution)/shard_map/all_to_all | solution.py:1146
  137.7 1.4 copy-done
  139.1 3.7 %all-to-all-start.1 = ((s16[32,17,16,128]{3,2,1,0:T(8,128)(2,1)}), s16[32,17,16,128]{3,2,1,0:T(8,128)(2,1)S(1)}, u32[]{:S(2)}, u32[]{:S(2)}) async-start(s16[32,17,16,128]{3,2,1,0:T(8,128)(2,1)} %following.3), calls=%async_computation.1 | async-start | bytes 4456448 | tf_op jit(solution)/shard_map/all_to_all | solution.py:1146
  142.9 1.2 broadcast_multiply_fusion
  144.1 2.1 mul.72
  146.1 1.4 mul.75
  148.3 1.3 add.35.refs_10_
  149.6 1.0 reduce-precision_convert_fusion.4
  151.5 42.3 %all-to-all-done.1.refs_1_.refs_3_ = s16[32,17,16,128]{3,2,1,0:T(8,128)(2,1)S(1)} async-done(((s16[32,17,16,128]{3,2,1,0:T(8,128)(2,1)}), s16[32,17,16,128]{3,2,1,0:T(8,128)(2,1)S(1)}, u32[]{:S(2)}, u32[]{:S(2)}) %all-to-all-start.1) | async-done | bytes 2228256 | tf_op jit(solution)/shard_map/all_to_all | solution.py:1146
  193.8 1.4 copy-done.1
  195.1 14.4 %solve_group.5 = s16[32,9,16,128]{3,2,1,0:T(8,128)(2,1)} custom-call(s16[32,17,16,128]{3,2,1,0:T(8,128)(2,1)} %copy-done, s16[32,17,16,128]{3,2,1,0:T(8,128)(2,1)} %copy-done.1, s16[32,17,16,128]{3,2,1,0:T(8,128)(2,1)} %copy-done, s16[32,17,16,128]{3,2,1,0:T(8,128)(2,1)} %copy-done.1, bf16[2,256,256]{2,1,0:T(8,128)(2,1)} %get-tuple-element.30.refs_4_, ...), custom_call_target="tpu_custom_call" | custom-call | flops 4026531840 | bytes 20971520 | tf_op jit(solution)/shard_map/solve_group/pallas_call | solution.py:1012
  209.5 3.7 %all-to-all-start.2 = ((s16[32,9,16,128]{3,2,1,0:T(8,128)(2,1)}), s16[32,9,16,128]{3,2,1,0:T(8,128)(2,1)S(1)}, u32[]{:S(2)}, u32[]{:S(2)}) async-start(s16[32,9,16,128]{3,2,1,0:T(8,128)(2,1)} %solve_group.5), calls=%async_computation.2 | async-start | bytes 2359296 | tf_op jit(solution)/shard_map/all_to_all | solution.py:1146
  213.2 20.5 %solve_group.4.values_ref = s16[32,17,16,128]{3,2,1,0:T(8,128)(2,1)} custom-call(s16[32,17,16,128]{3,2,1,0:T(8,128)(2,1)} %copy-done, s16[32,17,16,128]{3,2,1,0:T(8,128)(2,1)} %copy-done.1, s16[32,17,16,128]{3,2,1,0:T(8,128)(2,1)} %copy-done, s16[32,17,16,128]{3,2,1,0:T(8,128)(2,1)} %copy-done.1, bf16[2,256,256]{2,1,0:T(8,128)(2,1)} %get-tuple-element.30.refs_4_, ...), custom_call_target="tpu_custom_call" | custom-call | flops 8053063680 | bytes 20971520 | tf_op jit(solution)/shard_map/solve_group/pallas_call | solution.py:1012
  233.7 8.6 %all-to-all-done.2.earlier_ref.refs_0_.refs_2_ = s16[32,9,16,128]{3,2,1,0:T(8,128)(2,1)S(1)} async-done(((s16[32,9,16,128]{3,2,1,0:T(8,128)(2,1)}), s16[32,9,16,128]{3,2,1,0:T(8,128)(2,1)S(1)}, u32[]{:S(2)}, u32[]{:S(2)}) %all-to-all-start.2) | async-done | bytes 1179680 | tf_op jit(solution)/shard_map/all_to_all | solution.py:1146
  242.3 1.1 copy-done.3
  243.4 3.2 all-to-all-start.3
  247.5 1.0 reshape.242
  248.6 1.8 concatenate.24
  250.3 14.3 %solve_group.3.values_ref = s16[32,9,16,128]{3,2,1,0:T(8,128)(2,1)} custom-call(s16[32,17,16,128]{3,2,1,0:T(8,128)(2,1)} %copy-done, s16[32,17,16,128]{3,2,1,0:T(8,128)(2,1)} %copy-done.1, s16[32,17,16,128]{3,2,1,0:T(8,128)(2,1)} %copy-done, s16[32,17,16,128]{3,2,1,0:T(8,128)(2,1)} %copy-done.1, bf16[2,256,256]{2,1,0:T(8,128)(2,1)} %get-tuple-element.30.refs_4_, ...), custom_call_target="tpu_custom_call" | custom-call | flops 4026531840 | bytes 20971520 | tf_op jit(solution)/shard_map/solve_group/pallas_call | solution.py:1012
  264.7 33.0 %all-to-all-done.3.earlier_ref.refs_1_.refs_3_ = s16[32,17,16,128]{3,2,1,0:T(8,128)(2,1)S(1)} async-done(((s16[32,17,16,128]{3,2,1,0:T(8,128)(2,1)}), s16[32,17,16,128]{3,2,1,0:T(8,128)(2,1)S(1)}, u32[]{:S(2)}, u32[]{:S(2)}) %all-to-all-start.3) | async-done | bytes 2228256 | tf_op jit(solution)/shard_map/all_to_all | solution.py:1146
  297.6 1.4 copy-done.2
  299.0 3.7 %all-to-all-start.4 = ((s16[32,9,16,128]{3,2,1,0:T(8,128)(2,1)}), s16[32,9,16,128]{3,2,1,0:T(8,128)(2,1)S(1)}, u32[]{:S(2)}, u32[]{:S(2)}) async-start(s16[32,9,16,128]{3,2,1,0:T(8,128)(2,1)} %following.5), calls=%async_computation.4 | async-start | bytes 2359296 | tf_op jit(solution)/shard_map/all_to_all | solution.py:1146
  304.5 21.4 %pressure_of.2.refs_3_ = f32[256,16,512]{2,1,0:T(8,128)} custom-call(s16[32,9,16,128]{3,2,1,0:T(8,128)(2,1)} %copy-done.3, s16[32,17,16,128]{3,2,1,0:T(8,128)(2,1)} %copy-done.2, s16[32,9,16,128]{3,2,1,0:T(8,128)(2,1)} %copy-done.3, s16[32,17,16,128]{3,2,1,0:T(8,128)(2,1)} %copy-done.2, bf16[2,384,512]{2,1,0:T(8,128)(2,1)} %pad_maximum_fusion.2.refs_4_), custom_call_target="tpu_custom_call" | custom-call | flops 16106127360 | bytes 20971520 | tf_op jit(solution)/shard_map/pressure_of/pallas_call | solution.py:1111
  325.9 5.8 %all-to-all-done.4.refs_0_.refs_1_ = s16[32,9,16,128]{3,2,1,0:T(8,128)(2,1)S(1)} async-done(((s16[32,9,16,128]{3,2,1,0:T(8,128)(2,1)}), s16[32,9,16,128]{3,2,1,0:T(8,128)(2,1)S(1)}, u32[]{:S(2)}, u32[]{:S(2)}) %all-to-all-start.4) | async-done | bytes 1179680 | tf_op jit(solution)/shard_map/all_to_all | solution.py:1146
  331.8 1.1 copy-done.4
  332.9 15.6 %pressure_of.3 = f32[256,16,512]{2,1,0:T(8,128)} custom-call(s16[32,9,16,128]{3,2,1,0:T(8,128)(2,1)} %copy-done.4, s16[32,9,16,128]{3,2,1,0:T(8,128)(2,1)} %copy-done.4, bf16[2,128,512]{2,1,0:T(8,128)(2,1)} %pad_maximum_fusion.5.refs_2_, f32[256,16,512]{2,1,0:T(8,128)} %pressure_of.2.refs_3_), custom_call_target="tpu_custom_call" | custom-call | flops 5368709120 | bytes 20971520 | tf_op jit(solution)/shard_map/pressure_of/pallas_call | solution.py:1111
  (27 shorter events, 4.7 us)
Async XLA Ops:
  82.0 55.7 %all-to-all-start = ((s16[32,17,16,128]{3,2,1,0:T(8,128)(2,1)}), s16[32,17,16,128]{3,2,1,0:T(8,128)(2,1)S(1)}, u32[]{:S(2)}, u32[]{:S(2)}) async-start(s16[32,17,16,128]{3,2,1,0:T(8,128)(2,1)} %get-tuple-element.14), calls=%async_computation | async-start | bytes 4456448 | tf_op jit(solution)/shard_map/all_to_all | solution.py:1146
  137.7 1.4 copy-start
  139.1 3.7 %copy-start.6 = (f32[64,64]{1,0:T(8,128)S(1)}, f32[64,64]{1,0:T(8,128)}, u32[]{:S(2)}) copy-start(f32[64,64]{1,0:T(8,128)} %param.19) | copy-start | bytes 49156
  139.1 54.7 %all-to-all-start.1 = ((s16[32,17,16,128]{3,2,1,0:T(8,128)(2,1)}), s16[32,17,16,128]{3,2,1,0:T(8,128)(2,1)S(1)}, u32[]{:S(2)}, u32[]{:S(2)}) async-start(s16[32,17,16,128]{3,2,1,0:T(8,128)(2,1)} %following.3), calls=%async_computation.1 | async-start | bytes 4456448 | tf_op jit(solution)/shard_map/all_to_all | solution.py:1146
  142.7 5.5 %copy-start.7 = (f32[64]{0:T(128)S(1)}, f32[64]{0:T(128)}, u32[]{:S(2)}) copy-start(f32[64]{0:T(128)} %param.21) | copy-start | bytes 772
  193.8 1.4 copy-start.1
  209.5 32.8 %all-to-all-start.2 = ((s16[32,9,16,128]{3,2,1,0:T(8,128)(2,1)}), s16[32,9,16,128]{3,2,1,0:T(8,128)(2,1)S(1)}, u32[]{:S(2)}, u32[]{:S(2)}) async-start(s16[32,9,16,128]{3,2,1,0:T(8,128)(2,1)} %solve_group.5), calls=%async_computation.2 | async-start | bytes 2359296 | tf_op jit(solution)/shard_map/all_to_all | solution.py:1146
  242.3 1.1 copy-start.3
  243.4 54.2 %all-to-all-start.3 = ((s16[32,17,16,128]{3,2,1,0:T(8,128)(2,1)}), s16[32,17,16,128]{3,2,1,0:T(8,128)(2,1)S(1)}, u32[]{:S(2)}, u32[]{:S(2)}) async-start(s16[32,17,16,128]{3,2,1,0:T(8,128)(2,1)} %following.4), calls=%async_computation.3 | async-start | bytes 4456448 | tf_op jit(solution)/shard_map/all_to_all | solution.py:1146
  297.6 1.4 copy-start.2
  299.0 4.5 %copy-start.5 = (f32[1,128,512]{2,1,0:T(8,128)S(1)}, f32[1,128,512]{2,1,0:T(8,128)}, u32[]{:S(2)}) copy-start(f32[1,128,512]{2,1,0:T(8,128)} %concatenate.24) | copy-start | bytes 786436
  299.0 32.8 %all-to-all-start.4 = ((s16[32,9,16,128]{3,2,1,0:T(8,128)(2,1)}), s16[32,9,16,128]{3,2,1,0:T(8,128)(2,1)S(1)}, u32[]{:S(2)}, u32[]{:S(2)}) async-start(s16[32,9,16,128]{3,2,1,0:T(8,128)(2,1)} %following.5), calls=%async_computation.4 | async-start | bytes 2359296 | tf_op jit(solution)/shard_map/all_to_all | solution.py:1146
  331.8 1.1 copy-start.4

commit v4 on v3

--- a/solution.py
+++ b/solution.py
@@ -768,18 +768,21 @@
             return 0
 
         lax.fori_loop(0, layers // 2, radial, 0)
-        exponent = exponent_of(scales[...])
-        devices, _, height, lanes = sent_ref.shape
+        devices, slots, height, lanes = sent_ref.shape
         share = modes // devices
-        codes = exponent.astype(jnp.int32).astype(jnp.int16)
-        sent_ref[:, share] = codes.reshape(devices, share, lanes)
-        scales[...] = CODE_TOP / jnp.exp2(exponent * (1.0 / 256.0))
+        most = scales[...].reshape(devices, share // height, height, lanes)
+        exponent = exponent_of(jnp.max(most, axis=1))
+        sent_ref[:, slots - 1] = exponent.astype(jnp.int32).astype(jnp.int16)
+        factor = CODE_TOP / jnp.exp2(exponent * (1.0 / 256.0))
+        scales[pl.ds(0, devices * height), :] = factor.reshape(devices * height, lanes)
 
         def coding(device, _):
             for mode in range(share):
-                row = device * share + mode
-                values = wide[pl.ds(pl.multiple_of(row * layers, layers), layers), :]
-                sent_ref[device, mode] = to_codes(values * scales[pl.ds(row, 1), :])
+                factor = scales[pl.ds(device * height + mode % height, 1), :]
+                for part in range(layers // height):
+                    at = (device * share + mode) * layers + part * height
+                    values = wide[pl.ds(pl.multiple_of(at, height), height), :]
+                    sent_ref[device, mode * (layers // height) + part] = to_codes(values * factor)
             return 0
 
         lax.fori_loop(0, devices, coding, 0)
@@ -841,11 +844,11 @@
         in_specs=in_specs,
         out_specs=[
             whole,
-            pl.BlockSpec((devices, share + 1, layers, chunk), lambda i: (0, 0, 0, 0)),
+            pl.BlockSpec((devices, 2 * share + 1, layers // 2, chunk), lambda i: (0, 0, 0, 0)),
         ],
         out_shape=[
             jax.ShapeDtypeStruct(fraction.shape, F32),
-            jax.ShapeDtypeStruct((devices, share + 1, layers, chunk), jnp.int16),
+            jax.ShapeDtypeStruct((devices, 2 * share + 1, layers // 2, chunk), jnp.int16),
         ],
         scratch_shapes=[
             pltpu.VMEM((8, cells // 128, (block + 2) * layers, 128), F32),
@@ -912,16 +915,15 @@
         for copy in copies:
             copy.start()
 
-    devices, count, layers, lanes = got[0].shape
-    share = (sent.shape[1] - 1) // chunks
+    devices, count, height, lanes = got[0].shape
+    count, layers = count // 2, 2 * height
+    share = (sent.shape[1] - 1) // (2 * chunks)
+    together = chunks * share // height
     pairs = around // 4
     step = pl.program_id(0)
     first = start + step * count
     for chunk in range(chunks):
         scale[chunk] = scale_of(extra[chunk][:, 0])
-    if chunks * share < layers:
-        exponents[...] = jnp.zeros_like(exponents)
-
     def spots():
         for pair in range(pairs):
             for chunk in range(chunks):
@@ -937,11 +939,16 @@
     def fold(index, _):
         mode, axial = index // along, index % along
         rows = pl.ds(pl.multiple_of(index * layers, layers), layers)
-        row = pl.ds(first + mode, 1)
+        row = pl.ds(lax.rem(first + mode, height), 1)
         for at, places in spots():
             u0, u1, r0, r1 = [
-                decoded(got[chunk][azim * along + axial, mode])
-                * scale[chunk, azim * along + axial, row, :]
+                jnp.concatenate(
+                    [
+                        decoded(got[chunk][azim * along + axial, 2 * mode + part])
+                        * scale[chunk, azim * along + axial, row, :]
+                        for part in range(2)
+                    ]
+                )
                 for azim, chunk in places
             ]
             e0, o0, e1, o1 = u0 + u1, u0 - u1, r0 + r1, r0 - r1
@@ -956,8 +963,8 @@
         for copy in copies:
             copy.wait()
 
-    height = mix.shape[1]
-    parts = [pl.ds(at, height) for at in range(0, high.shape[1], height)]
+    deep = mix.shape[1]
+    parts = [pl.ds(at, deep) for at in range(0, high.shape[1], deep)]
 
     def waves(k, _):
         for at in parts:
@@ -973,32 +980,42 @@
 
     lax.fori_loop(0, 4, waves, 0)
 
+    apart = count // together
+
     def unfold(index, _):
         mode, axial = index // along, index % along
-        rows = pl.ds(pl.multiple_of(index * layers, layers), layers)
         for at, places in spots():
-            ec, es, oc, os = [result[k, rows, at] for k in range(4)]
-            e0, e1, o0, o1 = ec + es, ec - es, oc + os, os - oc
-            for (azim, chunk), values in zip(places, (e0 + o0, e0 - o0, e1 + o1, e1 - o1)):
+            found = []
+            for part in range(together):
+                row = ((mode + part * apart) * along + axial) * layers
+                rows = pl.ds(pl.multiple_of(row, layers), layers)
+                ec, es, oc, os = [result[k, rows, at] for k in range(4)]
+                e0, e1, o0, o1 = ec + es, ec - es, oc + os, os - oc
+                found.append((e0 + o0, e0 - o0, e1 + o1, e1 - o1))
+            for (azim, chunk), values in zip(places, zip(*found)):
                 device = azim * along + axial
-                slot = chunk * share + step * count + mode
-                exponent = exponent_of(jnp.max(jnp.abs(values), axis=0, keepdims=True))
-                exponents[device, pl.ds(slot, 1), :] = exponent
+                most = functools.reduce(jnp.maximum, [jnp.abs(x) for x in values])
+                exponent = exponent_of(jnp.max(most, axis=0, keepdims=True))
+                exponents[device, pl.ds(chunk * apart + mode, 1), :] = exponent
                 factor = CODE_TOP / jnp.exp2(exponent * (1.0 / 256.0))
-                sent[device, slot] = to_codes(values * factor)
+                for part, value in enumerate(values):
+                    slot = 2 * (chunk * share + mode + part * apart)
+                    for half in range(2):
+                        piece = value[half * height : (half + 1) * height]
+                        sent[device, slot + half] = to_codes(piece * factor)
         return 0
 
-    lax.fori_loop(0, count * along, unfold, 0)
+    lax.fori_loop(0, apart * along, unfold, 0)
 
     @pl.when(step == pl.num_programs(0) - 1)
     def _():
-        sent[:, chunks * share] = exponents[...].astype(jnp.int32).astype(jnp.int16)
+        sent[:, 2 * chunks * share] = exponents[...].astype(jnp.int32).astype(jnp.int16)
 
 
 def solve_group(got, mix, unmix, tables, shifts, start, share, around, along):
     chunks = len(got)
-    devices, slots, layers, lanes = got[0].shape
-    modes = slots - 1
+    devices, slots, height, lanes = got[0].shape
+    modes, layers = (slots - 1) // 2, 2 * height
     count = share
     steps = share // count
     block = start // count
@@ -1013,24 +1030,24 @@
         functools.partial(solve_kernel, around, along, chunks, start),
         grid=(steps,),
         in_specs=[
-            pl.BlockSpec((devices, count, layers, lanes), lambda i: (0, block + i, 0, 0))
+            pl.BlockSpec((devices, 2 * count, height, lanes), lambda i: (0, block + i, 0, 0))
         ]
         * chunks
-        + [pl.BlockSpec((devices, 1, layers, lanes), lambda i: (0, modes, 0, 0))] * chunks
+        + [pl.BlockSpec((devices, 1, height, lanes), lambda i: (0, 2 * modes, 0, 0))] * chunks
         + [fixed(mix), fixed(unmix)]
         + [pl.BlockSpec(memory_space=pl.ANY)] * 2
         + [fixed(rates), fixed(weights)]
         + [pl.BlockSpec((rows, 1), lambda i: (block + i, 0))],
         out_specs=pl.BlockSpec(
-            (devices, chunks * share + 1, layers, lanes), lambda i: (0, 0, 0, 0)
+            (devices, 2 * chunks * share + 1, height, lanes), lambda i: (0, 0, 0, 0)
         ),
-        out_shape=jax.ShapeDtypeStruct((devices, chunks * share + 1, layers, lanes), jnp.int16),
+        out_shape=jax.ShapeDtypeStruct((devices, 2 * chunks * share + 1, height, lanes), jnp.int16),
         scratch_shapes=[
             pltpu.VMEM((4, rows, width), BF16),
             pltpu.VMEM((4, rows, width), BF16),
             pltpu.VMEM((4, rows, width), F32),
-            pltpu.VMEM((chunks, devices, layers, lanes), F32),
-            pltpu.VMEM((devices, layers, lanes), F32),
+            pltpu.VMEM((chunks, devices, height, lanes), F32),
+            pltpu.VMEM((devices, height, lanes), F32),
             pltpu.VMEM(forth.shape, BF16),
             pltpu.VMEM(back.shape, BF16),
             pltpu.SemaphoreType.DMA((2,)),
@@ -1043,13 +1060,14 @@
     )(*got, *got, mix, unmix, forth, back, rates, weights, shifts)
 
 
-def pressure_kernel(around, groups, *refs):
+def pressure_kernel(around, groups, chunks, *refs):
     got = refs[:groups]
     extra = refs[groups : 2 * groups]
     basis = refs[2 * groups]
     base = refs[2 * groups + 1 : -6]
     out, flat, wide, scale, high, low = refs[-6:]
-    devices, _, layers, lanes = got[0].shape
+    devices, _, height, lanes = got[0].shape
+    layers = 2 * height
     lane_tiles = out.shape[2] // 128
     chunk = pl.program_id(0)
     backwards = lax.rem(lax.axis_index("azim"), around // 2) >= around // 4
@@ -1059,17 +1077,19 @@
     turn = jnp.where(j == turned_place, 1.0, 0.0).astype(BF16)
     spans, filled = [], 0
     for group in range(groups):
-        share = got[group].shape[1]
+        share = got[group].shape[1] // 2
+        apart = height // chunks
         spans.append((filled, devices * share))
         scale[group] = scale_of(extra[group][:, 0])
 
         def unpack(device, _, group=group, share=share, filled=filled):
             for mode in range(share):
-                at = pl.multiple_of((filled + device * share + mode) * layers, layers)
-                flat[pl.ds(at, layers), :] = (
-                    decoded(got[group][device, mode])
-                    * scale[group, device, pl.ds(chunk * share + mode, 1), :]
-                )
+                factor = scale[group, device, pl.ds(chunk * apart + mode % apart, 1), :]
+                for part in range(2):
+                    at = (filled + device * share + mode) * layers + part * height
+                    flat[pl.ds(pl.multiple_of(at, height), height), :] = (
+                        decoded(got[group][device, 2 * mode + part]) * factor
+                    )
             return 0
 
         lax.fori_loop(0, devices, unpack, 0)
@@ -1087,7 +1107,11 @@
                     target[part * lanes : (part + 1) * lanes, at] = dot(
                         turn, value, ((1,), (1,))
                     ).astype(BF16)
-        total = dot3((high[...], low[...]), (basis[0], basis[1]))
+        if filled > 128:
+            total = dot3((high[...], low[...]), (basis[0], basis[1]))
+        else:
+            lower = jnp.concatenate([high[...], low[...], high[...]], axis=1)
+            total = dot(lower, jnp.concatenate([basis[0], basis[0], basis[1]]), ((1,), (0,)))
         for part in range(together):
             for tile in range(lane_tiles):
                 wide[tile, pl.ds(batch * together + part, lanes, stride=layers), :] = total[
@@ -1104,16 +1128,17 @@
 
 def pressure_of(got, basis, around, chunks, base=None):
     groups = len(got)
-    devices, _, layers, lanes = got[0].shape
-    shares = [(x.shape[1] - 1) // chunks for x in got]
+    devices, _, height, lanes = got[0].shape
+    layers = 2 * height
+    shares = [(x.shape[1] - 1) // (2 * chunks) for x in got]
     inner, cells = basis.shape[1:]
     whole = pl.BlockSpec((lanes, layers, cells), lambda i: (i, 0, 0))
     return pl.pallas_call(
-        functools.partial(pressure_kernel, around, groups),
+        functools.partial(pressure_kernel, around, groups, chunks),
         grid=(chunks,),
-        in_specs=[pl.BlockSpec((devices, share, layers, lanes), lambda i: (0, i, 0, 0)) for share in shares]
+        in_specs=[pl.BlockSpec((devices, 2 * share, height, lanes), lambda i: (0, i, 0, 0)) for share in shares]
         + [
-            pl.BlockSpec((devices, 1, layers, lanes), lambda i, share=share: (0, chunks * share, 0, 0))
+            pl.BlockSpec((devices, 1, height, lanes), lambda i, share=share: (0, 2 * chunks * share, 0, 0))
             for share in shares
         ]
         + [pl.BlockSpec(basis.shape, lambda i: (0, 0, 0), pipeline_mode=pl.Buffered(1))]
@@ -1123,7 +1148,7 @@
         scratch_shapes=[
             pltpu.VMEM((inner * layers, lanes), F32),
             pltpu.VMEM((cells // 128, lanes * layers, 128), F32),
-            pltpu.VMEM((groups, devices, layers, lanes), F32),
+            pltpu.VMEM((groups, devices, height, lanes), F32),
             pltpu.VMEM((4 * lanes, inner), BF16),
             pltpu.VMEM((4 * lanes, inner), BF16),
         ],
@@ -1196,7 +1221,7 @@
     returned, bases = [], []
     for start, share in SOLVED:
         sent = solve_group(got, mix, unmix, tables, shifts, start, share, around, along)
-        returned.append(exchanged(following(sent, returned[-1]) if returned else sent))
+        returned.append(exchanged(sent))
         rows_of = radial_basis.T.reshape(devices, modes, cells)[:, start : start + share]
         bases.append(rows_of.reshape(devices * share, cells))
     pressure = pressure_of(returned[:-1], halves(jnp.concatenate(bases[:-1])), around, chunks)

time: 349 us -> 339 us (0.971)
  waiting for transfers between devices: 94.9 us -> 88 us
    all_to_all x5, waiting for transfers between devices: 94.9 us -> 88 us  [exchanged(): lax.all_to_all(sent, ('azim', 'axial'), split_axis=0, concat_axis=0, tile...]
    unnamed x17 -> x13, local copies, waits for them, and re-layouts: 7.88 us -> 5.35 us
  transfers between devices with their start and end apart: 5 -> 5, of which waited for: 5 -> 5; matrix products, arithmetic and copies ran while one was open for 4% -> 5% of each run, Pallas kernels for 29% -> 30%
where the time goes in v4:
time: 339 us; the launch traced here: 338 us
  Pallas kernels  209 us (62%)
  waiting for transfers between devices  88 us (26%)
  starting transfers between devices  18.7 us (6%)
  local copies, waits for them, and re-layouts  13.9 us (4%)
  other arithmetic  7.93 us (2%)
    pallas_call x2, Pallas kernels, advect_chunk(): pl.pallas_call(functools.partial(chunk_kernel, around, chunk_index, rows...  91.6 us
    all_to_all x5, waiting for transfers between devices, exchanged(): lax.all_to_all(sent, ('azim', 'axial'), split_axis=0, concat_axis=0, tile...  88 us
    pallas_call x3, Pallas kernels, solve_group(): pl.pallas_call(functools.partial(solve_kernel, around, along, chunks, sta...  48.3 us
    pallas_call x2, Pallas kernels, pressure_of(): pl.pallas_call(functools.partial(pressure_kernel, around, groups, chunks)...  36.1 us
    pallas_call x1, Pallas kernels, halos(): pl.pallas_call(halo_kernel, grid=(2 * half,), in_specs=in_specs, out_spec...  32.6 us
    all_to_all x5, starting transfers between devices, exchanged(): lax.all_to_all(sent, ('azim', 'axial'), split_axis=0, concat_axis=0, tile...  18.7 us
  transfers between devices with their start and end apart: 5, of which 5 were waited for; matrix products, arithmetic and copies ran while one was open for 5% of the time, Pallas kernels for 30%

profile of v4, /device:TPU:1, one launch (start us, length us, event | category | flops | bytes accessed | tf_op | source)
XLA Modules:
  0.0 338.0 jit_solution(15039627770099631427)
XLA Ops:
  0.6 1.6 copy.19
  2.4 1.1 pad_maximum_fusion.basis_ref
  3.5 32.6 %halos.1 = (f32[2,256,512]{2,1,0:T(8,128)}, f32[2,256,512]{2,1,0:T(8,128)}, bf16[2,5,16,512]{3,2,1,0:T(8,128)(2,1)}) custom-call(bf16[3,256,16,512]{3,2,1,0:T(8,128)(2,1)} %last_courant_ref.5, bf16[3,256,16,512]{3,2,1,0:T(8,128)(2,1)} %last_normals_ref.5, bf16[256,16,512]{2,1,0:T(8,128)(2,1)} %last_planes_ref.5, s32[256,16,512]{2,1,0:T(8,128)} %last_flags_ref.5, ...), custom_call_target="tpu_custom_call" | custom-call | tf_op jit(solution)/shard_map/halos/pallas_call | solution.py:564
  36.1 45.9 %advect_chunk.2 = (f32[256,16,512]{2,1,0:T(8,128)}, s16[32,33,8,128]{3,2,1,0:T(8,128)(2,1)}) custom-call(f32[256,16,512]{2,1,0:T(8,128)} %fraction_ref.3, bf16[3,256,16,512]{3,2,1,0:T(8,128)(2,1)} %last_normals_ref.5, bf16[256,16,512]{2,1,0:T(8,128)(2,1)} %last_planes_ref.5, s32[256,16,512]{2,1,0:T(8,128)} %last_flags_ref.5, ...), custom_call_target="tpu_custom_call" | custom-call | flops 41943040000 | bytes 31457280 | tf_op jit(solution)/shard_map/advect_chunk/pallas_call | solution.py:841
  81.9 4.7 %all-to-all-start = ((s16[32,33,8,128]{3,2,1,0:T(8,128)(2,1)}), s16[32,33,8,128]{3,2,1,0:T(8,128)(2,1)S(1)}, u32[]{:S(2)}, u32[]{:S(2)}) async-start(s16[32,33,8,128]{3,2,1,0:T(8,128)(2,1)} %get-tuple-element.14), calls=%async_computation | async-start | bytes 4325376 | tf_op jit(solution)/shard_map/all_to_all | solution.py:1171
  86.7 45.7 %advect_chunk.3 = (f32[256,16,512]{2,1,0:T(8,128)}, s16[32,33,8,128]{3,2,1,0:T(8,128)(2,1)}) custom-call(f32[256,16,512]{2,1,0:T(8,128)} %fraction_ref.3, bf16[3,256,16,512]{3,2,1,0:T(8,128)(2,1)} %last_normals_ref.5, bf16[256,16,512]{2,1,0:T(8,128)(2,1)} %last_planes_ref.5, s32[256,16,512]{2,1,0:T(8,128)} %last_flags_ref.5, ...), custom_call_target="tpu_custom_call", output_to_operand_aliasing={{0}: (17, {})} | custom-call | flops 41943040000 | bytes 31457280 | tf_op jit(solution)/shard_map/advect_chunk/pallas_call | solution.py:841
  132.4 3.9 %all-to-all-done.earlier_ref.refs_0_.refs_2_ = s16[32,33,8,128]{3,2,1,0:T(8,128)(2,1)S(1)} async-done(((s16[32,33,8,128]{3,2,1,0:T(8,128)(2,1)}), s16[32,33,8,128]{3,2,1,0:T(8,128)(2,1)S(1)}, u32[]{:S(2)}, u32[]{:S(2)}) %all-to-all-start) | async-done | bytes 2162720 | tf_op jit(solution)/shard_map/all_to_all | solution.py:1171
  136.3 1.3 copy-done
  137.6 3.6 %all-to-all-start.1 = ((s16[32,33,8,128]{3,2,1,0:T(8,128)(2,1)}), s16[32,33,8,128]{3,2,1,0:T(8,128)(2,1)S(1)}, u32[]{:S(2)}, u32[]{:S(2)}) async-start(s16[32,33,8,128]{3,2,1,0:T(8,128)(2,1)} %following.1), calls=%async_computation.1 | async-start | bytes 4325376 | tf_op jit(solution)/shard_map/all_to_all | solution.py:1171
  142.2 1.3 add.35.refs_10_
  143.4 1.2 broadcast_multiply_fusion
  144.6 2.1 mul.75
  146.7 1.4 mul.72
  148.1 1.0 reduce-precision_convert_fusion.3
  150.0 40.9 %all-to-all-done.1.refs_1_.refs_3_ = s16[32,33,8,128]{3,2,1,0:T(8,128)(2,1)S(1)} async-done(((s16[32,33,8,128]{3,2,1,0:T(8,128)(2,1)}), s16[32,33,8,128]{3,2,1,0:T(8,128)(2,1)S(1)}, u32[]{:S(2)}, u32[]{:S(2)}) %all-to-all-start.1) | async-done | bytes 2162720 | tf_op jit(solution)/shard_map/all_to_all | solution.py:1171
  190.9 1.4 copy-done.1
  192.2 14.4 %solve_group.4 = s16[32,17,8,128]{3,2,1,0:T(8,128)(2,1)} custom-call(s16[32,33,8,128]{3,2,1,0:T(8,128)(2,1)} %copy-done, s16[32,33,8,128]{3,2,1,0:T(8,128)(2,1)} %copy-done.1, s16[32,33,8,128]{3,2,1,0:T(8,128)(2,1)} %copy-done, s16[32,33,8,128]{3,2,1,0:T(8,128)(2,1)} %copy-done.1, bf16[2,256,256]{2,1,0:T(8,128)(2,1)} %get-tuple-element.30.refs_4_, ...), custom_call_target="tpu_custom_call" | custom-call | flops 4026531840 | bytes 20971520 | tf_op jit(solution)/shard_map/solve_group/pallas_call | solution.py:1029
  206.6 3.6 %all-to-all-start.3 = ((s16[32,17,8,128]{3,2,1,0:T(8,128)(2,1)}), s16[32,17,8,128]{3,2,1,0:T(8,128)(2,1)S(1)}, u32[]{:S(2)}, u32[]{:S(2)}) async-start(s16[32,17,8,128]{3,2,1,0:T(8,128)(2,1)} %solve_group.4), calls=%async_computation.3 | async-start | bytes 2228224 | tf_op jit(solution)/shard_map/all_to_all | solution.py:1171
  210.2 19.6 %solve_group.5 = s16[32,33,8,128]{3,2,1,0:T(8,128)(2,1)} custom-call(s16[32,33,8,128]{3,2,1,0:T(8,128)(2,1)} %copy-done, s16[32,33,8,128]{3,2,1,0:T(8,128)(2,1)} %copy-done.1, s16[32,33,8,128]{3,2,1,0:T(8,128)(2,1)} %copy-done, s16[32,33,8,128]{3,2,1,0:T(8,128)(2,1)} %copy-done.1, bf16[2,256,256]{2,1,0:T(8,128)(2,1)} %get-tuple-element.30.refs_4_, ...), custom_call_target="tpu_custom_call" | custom-call | flops 8053063680 | bytes 20971520 | tf_op jit(solution)/shard_map/solve_group/pallas_call | solution.py:1029
  229.8 8.2 %all-to-all-done.3.refs_0_.refs_2_ = s16[32,17,8,128]{3,2,1,0:T(8,128)(2,1)S(1)} async-done(((s16[32,17,8,128]{3,2,1,0:T(8,128)(2,1)}), s16[32,17,8,128]{3,2,1,0:T(8,128)(2,1)S(1)}, u32[]{:S(2)}, u32[]{:S(2)}) %all-to-all-start.3) | async-done | bytes 1114144 | tf_op jit(solution)/shard_map/all_to_all | solution.py:1171
  237.9 1.1 copy-done.3
  239.0 3.2 all-to-all-start.4
  243.1 1.0 reshape.242
  244.1 14.4 %solve_group.3 = s16[32,17,8,128]{3,2,1,0:T(8,128)(2,1)} custom-call(s16[32,33,8,128]{3,2,1,0:T(8,128)(2,1)} %copy-done, s16[32,33,8,128]{3,2,1,0:T(8,128)(2,1)} %copy-done.1, s16[32,33,8,128]{3,2,1,0:T(8,128)(2,1)} %copy-done, s16[32,33,8,128]{3,2,1,0:T(8,128)(2,1)} %copy-done.1, bf16[2,256,256]{2,1,0:T(8,128)(2,1)} %get-tuple-element.30.refs_4_, ...), custom_call_target="tpu_custom_call" | custom-call | flops 4026531840 | bytes 20971520 | tf_op jit(solution)/shard_map/solve_group/pallas_call | solution.py:1029
  258.5 33.3 %all-to-all-done.4.refs_1_.refs_3_ = s16[32,33,8,128]{3,2,1,0:T(8,128)(2,1)S(1)} async-done(((s16[32,33,8,128]{3,2,1,0:T(8,128)(2,1)}), s16[32,33,8,128]{3,2,1,0:T(8,128)(2,1)S(1)}, u32[]{:S(2)}, u32[]{:S(2)}) %all-to-all-start.4) | async-done | bytes 2162720 | tf_op jit(solution)/shard_map/all_to_all | solution.py:1171
  291.8 3.6 %all-to-all-start.2 = ((s16[32,17,8,128]{3,2,1,0:T(8,128)(2,1)}), s16[32,17,8,128]{3,2,1,0:T(8,128)(2,1)}, u32[]{:S(2)}, u32[]{:S(2)}) async-start(s16[32,17,8,128]{3,2,1,0:T(8,128)(2,1)} %solve_group.3), calls=%async_computation.2 | async-start | bytes 2228224 | tf_op jit(solution)/shard_map/all_to_all | solution.py:1171
  296.2 1.0 concatenate.24
  297.2 1.7 pad_maximum_fusion.5.refs_2_
  299.1 1.0 pad_maximum_fusion.2.refs_4_
  300.1 21.4 %pressure_of.2.refs_3_ = f32[256,16,512]{2,1,0:T(8,128)} custom-call(s16[32,17,8,128]{3,2,1,0:T(8,128)(2,1)} %copy-done.3, s16[32,33,8,128]{3,2,1,0:T(8,128)(2,1)} %copy-done.2, s16[32,17,8,128]{3,2,1,0:T(8,128)(2,1)} %copy-done.3, s16[32,33,8,128]{3,2,1,0:T(8,128)(2,1)} %copy-done.2, bf16[2,384,512]{2,1,0:T(8,128)(2,1)} %pad_maximum_fusion.2.refs_4_), custom_call_target="tpu_custom_call" | custom-call | flops 16106127360 | bytes 20971520 | tf_op jit(solution)/shard_map/pressure_of/pallas_call | solution.py:1136
  321.4 1.8 all-to-all-done.2.refs_0_.refs_1_
  323.2 14.8 %pressure_of.3 = f32[256,16,512]{2,1,0:T(8,128)} custom-call(s16[32,17,8,128]{3,2,1,0:T(8,128)(2,1)} %all-to-all-done.2.refs_0_.refs_1_, s16[32,17,8,128]{3,2,1,0:T(8,128)(2,1)} %all-to-all-done.2.refs_0_.refs_1_, bf16[2,128,512]{2,1,0:T(8,128)(2,1)} %pad_maximum_fusion.5.refs_2_, f32[256,16,512]{2,1,0:T(8,128)} %pressure_of.2.refs_3_), custom_call_target="tpu_custom_call" | custom-call | flops 5368709120 | bytes 20971520 | tf_op jit(solution)/shard_map/pressure_of/pallas_call | solution.py:1136
  (21 shorter events, 3.8 us)
Async XLA Ops:
  81.9 54.4 %all-to-all-start = ((s16[32,33,8,128]{3,2,1,0:T(8,128)(2,1)}), s16[32,33,8,128]{3,2,1,0:T(8,128)(2,1)S(1)}, u32[]{:S(2)}, u32[]{:S(2)}) async-start(s16[32,33,8,128]{3,2,1,0:T(8,128)(2,1)} %get-tuple-element.14), calls=%async_computation | async-start | bytes 4325376 | tf_op jit(solution)/shard_map/all_to_all | solution.py:1171
  136.3 1.3 copy-start
  137.6 3.6 %copy-start.4 = (f32[64,64]{1,0:T(8,128)S(1)}, f32[64,64]{1,0:T(8,128)}, u32[]{:S(2)}) copy-start(f32[64,64]{1,0:T(8,128)} %param.19) | copy-start | bytes 49156
  137.6 4.4 %copy-start.5 = (f32[64]{0:T(128)S(1)}, f32[64]{0:T(128)}, u32[]{:S(2)}) copy-start(f32[64]{0:T(128)} %param.21) | copy-start | bytes 772
  137.6 53.2 %all-to-all-start.1 = ((s16[32,33,8,128]{3,2,1,0:T(8,128)(2,1)}), s16[32,33,8,128]{3,2,1,0:T(8,128)(2,1)S(1)}, u32[]{:S(2)}, u32[]{:S(2)}) async-start(s16[32,33,8,128]{3,2,1,0:T(8,128)(2,1)} %following.1), calls=%async_computation.1 | async-start | bytes 4325376 | tf_op jit(solution)/shard_map/all_to_all | solution.py:1171
  190.8 1.4 copy-start.1
  206.6 31.3 %all-to-all-start.3 = ((s16[32,17,8,128]{3,2,1,0:T(8,128)(2,1)}), s16[32,17,8,128]{3,2,1,0:T(8,128)(2,1)S(1)}, u32[]{:S(2)}, u32[]{:S(2)}) async-start(s16[32,17,8,128]{3,2,1,0:T(8,128)(2,1)} %solve_group.4), calls=%async_computation.3 | async-start | bytes 2228224 | tf_op jit(solution)/shard_map/all_to_all | solution.py:1171
  237.9 1.1 copy-start.3
  239.0 52.8 %all-to-all-start.4 = ((s16[32,33,8,128]{3,2,1,0:T(8,128)(2,1)}), s16[32,33,8,128]{3,2,1,0:T(8,128)(2,1)S(1)}, u32[]{:S(2)}, u32[]{:S(2)}) async-start(s16[32,33,8,128]{3,2,1,0:T(8,128)(2,1)} %solve_group.5), calls=%async_computation.4 | async-start | bytes 4325376 | tf_op jit(solution)/shard_map/all_to_all | solution.py:1171
  291.8 8.3 %copy-start.2 = (s16[32,33,8,128]{3,2,1,0:T(8,128)(2,1)}, s16[32,33,8,128]{3,2,1,0:T(8,128)(2,1)S(1)}, u32[]{:S(2)}) copy-start(s16[32,33,8,128]{3,2,1,0:T(8,128)(2,1)S(1)} %all-to-all-done.4.refs_1_.refs_3_) | copy-start | bytes 6488068
  291.8 31.4 %all-to-all-start.2 = ((s16[32,17,8,128]{3,2,1,0:T(8,128)(2,1)}), s16[32,17,8,128]{3,2,1,0:T(8,128)(2,1)}, u32[]{:S(2)}, u32[]{:S(2)}) async-start(s16[32,17,8,128]{3,2,1,0:T(8,128)(2,1)} %solve_group.3), calls=%async_computation.2 | async-start | bytes 2228224 | tf_op jit(solution)/shard_map/all_to_all | solution.py:1171

commit v5 on v4

--- a/solution.py
+++ b/solution.py
@@ -902,28 +902,15 @@
 
 def solve_kernel(around, along, chunks, start, *refs):
     got = refs[:chunks]
-    extra = refs[chunks : 2 * chunks]
-    mix, unmix, forth_ref, back_ref, rates, weights, shifts = refs[2 * chunks : 2 * chunks + 7]
-    sent, high, low, result, scale, exponents, forth, back, arrived = refs[2 * chunks + 7 :]
-    copies = [
-        pltpu.make_async_copy(forth_ref, forth, arrived.at[0]),
-        pltpu.make_async_copy(back_ref, back, arrived.at[1]),
-    ]
-
-    @pl.when(pl.program_id(0) == 0)
-    def _():
-        for copy in copies:
-            copy.start()
-
-    devices, count, height, lanes = got[0].shape
-    count, layers = count // 2, 2 * height
+    mix, unmix, forth, back, rates, weights, shifts = refs[chunks : chunks + 7]
+    sent, high, low, result, scale, exponents = refs[chunks + 7 :]
+    devices, slots, height, lanes = got[0].shape
+    count, layers = (sent.shape[1] - 1) // (2 * chunks), 2 * height
     share = (sent.shape[1] - 1) // (2 * chunks)
     together = chunks * share // height
     pairs = around // 4
-    step = pl.program_id(0)
-    first = start + step * count
     for chunk in range(chunks):
-        scale[chunk] = scale_of(extra[chunk][:, 0])
+        scale[chunk] = scale_of(got[chunk][:, slots - 1])
     def spots():
         for pair in range(pairs):
             for chunk in range(chunks):
@@ -939,12 +926,12 @@
     def fold(index, _):
         mode, axial = index // along, index % along
         rows = pl.ds(pl.multiple_of(index * layers, layers), layers)
-        row = pl.ds(lax.rem(first + mode, height), 1)
+        row = pl.ds(lax.rem(start + mode, height), 1)
         for at, places in spots():
             u0, u1, r0, r1 = [
                 jnp.concatenate(
                     [
-                        decoded(got[chunk][azim * along + axial, 2 * mode + part])
+                        decoded(got[chunk][azim * along + axial, 2 * (start + mode) + part])
                         * scale[chunk, azim * along + axial, row, :]
                         for part in range(2)
                     ]
@@ -957,11 +944,6 @@
         return 0
 
     lax.fori_loop(0, count * along, fold, 0)
-
-    @pl.when(pl.program_id(0) == 0)
-    def _():
-        for copy in copies:
-            copy.wait()
 
     deep = mix.shape[1]
     parts = [pl.ds(at, deep) for at in range(0, high.shape[1], deep)]
@@ -1007,40 +989,21 @@
 
     lax.fori_loop(0, apart * along, unfold, 0)
 
-    @pl.when(step == pl.num_programs(0) - 1)
-    def _():
-        sent[:, 2 * chunks * share] = exponents[...].astype(jnp.int32).astype(jnp.int16)
+    sent[:, 2 * chunks * share] = exponents[...].astype(jnp.int32).astype(jnp.int16)
 
 
 def solve_group(got, mix, unmix, tables, shifts, start, share, around, along):
     chunks = len(got)
     devices, slots, height, lanes = got[0].shape
-    modes, layers = (slots - 1) // 2, 2 * height
-    count = share
-    steps = share // count
-    block = start // count
-    rows = count * along * layers
+    rows = share * along * 2 * height
     forth, back, rates, weights = tables
     width = forth.shape[-1]
-
-    def fixed(array):
-        return pl.BlockSpec(array.shape, lambda i: (0,) * array.ndim, pipeline_mode=pl.Buffered(1))
-
+    whole = pl.BlockSpec(memory_space=pltpu.VMEM)
+    shifts = lax.slice_in_dim(shifts, start * along * 2 * height, start * along * 2 * height + rows)
     return pl.pallas_call(
         functools.partial(solve_kernel, around, along, chunks, start),
-        grid=(steps,),
-        in_specs=[
-            pl.BlockSpec((devices, 2 * count, height, lanes), lambda i: (0, block + i, 0, 0))
-        ]
-        * chunks
-        + [pl.BlockSpec((devices, 1, height, lanes), lambda i: (0, 2 * modes, 0, 0))] * chunks
-        + [fixed(mix), fixed(unmix)]
-        + [pl.BlockSpec(memory_space=pl.ANY)] * 2
-        + [fixed(rates), fixed(weights)]
-        + [pl.BlockSpec((rows, 1), lambda i: (block + i, 0))],
-        out_specs=pl.BlockSpec(
-            (devices, 2 * chunks * share + 1, height, lanes), lambda i: (0, 0, 0, 0)
-        ),
+        in_specs=[whole] * (chunks + 7),
+        out_specs=whole,
         out_shape=jax.ShapeDtypeStruct((devices, 2 * chunks * share + 1, height, lanes), jnp.int16),
         scratch_shapes=[
             pltpu.VMEM((4, rows, width), BF16),
@@ -1048,23 +1011,19 @@
             pltpu.VMEM((4, rows, width), F32),
             pltpu.VMEM((chunks, devices, height, lanes), F32),
             pltpu.VMEM((devices, height, lanes), F32),
-            pltpu.VMEM(forth.shape, BF16),
-            pltpu.VMEM(back.shape, BF16),
-            pltpu.SemaphoreType.DMA((2,)),
         ],
-        compiler_params=pltpu.CompilerParams(vmem_limit_bytes=60 * 2**20),
+        compiler_params=pltpu.CompilerParams(vmem_limit_bytes=32 * 2**20),
         cost_estimate=pl.CostEstimate(
-            flops=60 * rows * width * width * steps, bytes_accessed=20 * 2**20, transcendentals=0
+            flops=60 * rows * width * width, bytes_accessed=20 * 2**20, transcendentals=0
         ),
         name="solve_group",
-    )(*got, *got, mix, unmix, forth, back, rates, weights, shifts)
+    )(*got, mix, unmix, forth, back, rates, weights, shifts)
 
 
 def pressure_kernel(around, groups, chunks, *refs):
     got = refs[:groups]
-    extra = refs[groups : 2 * groups]
-    basis = refs[2 * groups]
-    base = refs[2 * groups + 1 : -6]
+    basis = refs[groups]
+    base = refs[groups + 1 : -6]
     out, flat, wide, scale, high, low = refs[-6:]
     devices, _, height, lanes = got[0].shape
     layers = 2 * height
@@ -1077,10 +1036,10 @@
     turn = jnp.where(j == turned_place, 1.0, 0.0).astype(BF16)
     spans, filled = [], 0
     for group in range(groups):
-        share = got[group].shape[1] // 2
+        share = (got[group].shape[1] - 1) // (2 * chunks)
         apart = height // chunks
         spans.append((filled, devices * share))
-        scale[group] = scale_of(extra[group][:, 0])
+        scale[group] = scale_of(got[group][:, 2 * chunks * share])
 
         def unpack(device, _, group=group, share=share, filled=filled):
             for mode in range(share):
@@ -1088,7 +1047,7 @@
                 for part in range(2):
                     at = (filled + device * share + mode) * layers + part * height
                     flat[pl.ds(pl.multiple_of(at, height), height), :] = (
-                        decoded(got[group][device, 2 * mode + part]) * factor
+                        decoded(got[group][device, 2 * (chunk * share + mode) + part]) * factor
                     )
             return 0
 
@@ -1130,18 +1089,12 @@
     groups = len(got)
     devices, _, height, lanes = got[0].shape
     layers = 2 * height
-    shares = [(x.shape[1] - 1) // (2 * chunks) for x in got]
     inner, cells = basis.shape[1:]
     whole = pl.BlockSpec((lanes, layers, cells), lambda i: (i, 0, 0))
     return pl.pallas_call(
         functools.partial(pressure_kernel, around, groups, chunks),
         grid=(chunks,),
-        in_specs=[pl.BlockSpec((devices, 2 * share, height, lanes), lambda i: (0, i, 0, 0)) for share in shares]
-        + [
-            pl.BlockSpec((devices, 1, height, lanes), lambda i, share=share: (0, 2 * chunks * share, 0, 0))
-            for share in shares
-        ]
-        + [pl.BlockSpec(basis.shape, lambda i: (0, 0, 0), pipeline_mode=pl.Buffered(1))]
+        in_specs=[pl.BlockSpec(memory_space=pltpu.VMEM)] * (groups + 1)
         + ([] if base is None else [whole]),
         out_specs=whole,
         out_shape=jax.ShapeDtypeStruct((lanes * chunks, layers, cells), F32),
@@ -1152,14 +1105,14 @@
             pltpu.VMEM((4 * lanes, inner), BF16),
             pltpu.VMEM((4 * lanes, inner), BF16),
         ],
-        compiler_params=pltpu.CompilerParams(vmem_limit_bytes=60 * 2**20),
+        compiler_params=pltpu.CompilerParams(vmem_limit_bytes=40 * 2**20),
         cost_estimate=pl.CostEstimate(
             flops=20 * lanes * chunks * layers * cells * inner,
             bytes_accessed=20 * 2**20,
             transcendentals=0,
         ),
         name="pressure_of",
-    )(*got, *got, basis, *([] if base is None else [base]))
+    )(*got, basis, *([] if base is None else [base]))
 
 
 def halves(values):

time: 339 us -> 340 us (level)
  local copies, waits for them, and re-layouts: 13.9 us -> 41.8 us
  Pallas kernels: 209 us -> 194 us
  waiting for transfers between devices: 88 us -> 79.2 us
  other arithmetic: 7.93 us -> 3.88 us
    unnamed x13 -> x51, local copies, waits for them, and re-layouts: 5.35 us -> 29.9 us
    pallas_call x3, Pallas kernels: 48.3 us -> 38.1 us  [solve_group(): pl.pallas_call(functools.partial(solve_kernel, around, along, chunks, sta...]
    all_to_all x5, waiting for transfers between devices: 88 us -> 79.2 us  [exchanged(): lax.all_to_all(sent, ('azim', 'axial'), split_axis=0, concat_axis=0, tile...]
    pallas_call x2, Pallas kernels: 36.1 us -> 31.9 us  [pressure_of(): pl.pallas_call(functools.partial(pressure_kernel, around, groups, chunks)...]
    slice x0 -> x5, local copies, waits for them, and re-layouts: none -> 3.66 us  [solve_group(): lax.slice_in_dim(shifts, start * along * 2 * height, start * along * 2 *...]
  transfers between devices with their start and end apart: 5 -> 5, of which waited for: 5 -> 5; matrix products, arithmetic and copies ran while one was open for 5% -> 4% of each run, Pallas kernels for 30% -> 27%
where the time goes in v5:
time: 340 us; the launch traced here: 339 us
  Pallas kernels  194 us (57%)
  waiting for transfers between devices  79.2 us (23%)
  local copies, waits for them, and re-layouts  41.8 us (12%)
  starting transfers between devices  19 us (6%)
  other arithmetic  3.88 us (1%)
    pallas_call x2, Pallas kernels, advect_chunk(): pl.pallas_call(functools.partial(chunk_kernel, around, chunk_index, rows...  91.5 us
    all_to_all x5, waiting for transfers between devices, exchanged(): lax.all_to_all(sent, ('azim', 'axial'), split_axis=0, concat_axis=0, tile...  79.2 us
    pallas_call x3, Pallas kernels, solve_group(): pl.pallas_call(functools.partial(solve_kernel, around, along, chunks, sta...  38.1 us
    pallas_call x1, Pallas kernels, halos(): pl.pallas_call(halo_kernel, grid=(2 * half,), in_specs=in_specs, out_spec...  32.6 us
    pallas_call x2, Pallas kernels, pressure_of(): pl.pallas_call(functools.partial(pressure_kernel, around, groups, chunks)...  31.9 us
    unnamed x51, local copies, waits for them, and re-layouts  29.9 us
    all_to_all x5, starting transfers between devices, exchanged(): lax.all_to_all(sent, ('azim', 'axial'), split_axis=0, concat_axis=0, tile...  19 us
  transfers between devices with their start and end apart: 5, of which 5 were waited for; matrix products, arithmetic and copies ran while one was open for 4% of the time, Pallas kernels for 27%

profile of v5, /device:TPU:1, one launch (start us, length us, event | category | flops | bytes accessed | tf_op | source)
XLA Modules:
  0.0 339.0 jit_solution(657095654160697758)
XLA Ops:
  0.6 1.6 copy.19
  3.5 32.6 %halos.1 = (f32[2,256,512]{2,1,0:T(8,128)}, f32[2,256,512]{2,1,0:T(8,128)}, bf16[2,5,16,512]{3,2,1,0:T(8,128)(2,1)}) custom-call(bf16[3,256,16,512]{3,2,1,0:T(8,128)(2,1)} %last_courant_ref.5, bf16[3,256,16,512]{3,2,1,0:T(8,128)(2,1)} %last_normals_ref.5, bf16[256,16,512]{2,1,0:T(8,128)(2,1)} %last_planes_ref.5, s32[256,16,512]{2,1,0:T(8,128)} %last_flags_ref.5, ...), custom_call_target="tpu_custom_call" | custom-call | tf_op jit(solution)/shard_map/halos/pallas_call | solution.py:564
  36.2 45.8 %advect_chunk.2 = (f32[256,16,512]{2,1,0:T(8,128)}, s16[32,33,8,128]{3,2,1,0:T(8,128)(2,1)}) custom-call(f32[256,16,512]{2,1,0:T(8,128)} %fraction_ref.3, bf16[3,256,16,512]{3,2,1,0:T(8,128)(2,1)} %last_normals_ref.5, bf16[256,16,512]{2,1,0:T(8,128)(2,1)} %last_planes_ref.5, s32[256,16,512]{2,1,0:T(8,128)} %last_flags_ref.5, ...), custom_call_target="tpu_custom_call" | custom-call | flops 41943040000 | bytes 31457280 | tf_op jit(solution)/shard_map/advect_chunk/pallas_call | solution.py:841
  82.0 4.7 %all-to-all-start = ((s16[32,33,8,128]{3,2,1,0:T(8,128)(2,1)}), s16[32,33,8,128]{3,2,1,0:T(8,128)(2,1)S(1)}, u32[]{:S(2)}, u32[]{:S(2)}) async-start(s16[32,33,8,128]{3,2,1,0:T(8,128)(2,1)} %get-tuple-element.14), calls=%async_computation | async-start | bytes 4325376 | tf_op jit(solution)/shard_map/all_to_all | solution.py:1124
  86.7 45.7 %advect_chunk.3 = (f32[256,16,512]{2,1,0:T(8,128)}, s16[32,33,8,128]{3,2,1,0:T(8,128)(2,1)}) custom-call(f32[256,16,512]{2,1,0:T(8,128)} %fraction_ref.3, bf16[3,256,16,512]{3,2,1,0:T(8,128)(2,1)} %last_normals_ref.5, bf16[256,16,512]{2,1,0:T(8,128)(2,1)} %last_planes_ref.5, s32[256,16,512]{2,1,0:T(8,128)} %last_flags_ref.5, ...), custom_call_target="tpu_custom_call", output_to_operand_aliasing={{0}: (17, {})} | custom-call | flops 41943040000 | bytes 31457280 | tf_op jit(solution)/shard_map/advect_chunk/pallas_call | solution.py:841
  132.5 3.9 %all-to-all-done.earlier_ref.refs_0_ = s16[32,33,8,128]{3,2,1,0:T(8,128)(2,1)S(1)} async-done(((s16[32,33,8,128]{3,2,1,0:T(8,128)(2,1)}), s16[32,33,8,128]{3,2,1,0:T(8,128)(2,1)S(1)}, u32[]{:S(2)}, u32[]{:S(2)}) %all-to-all-start) | async-done | bytes 2162720 | tf_op jit(solution)/shard_map/all_to_all | solution.py:1124
  136.4 1.3 copy-done
  137.7 3.6 %all-to-all-start.1 = ((s16[32,33,8,128]{3,2,1,0:T(8,128)(2,1)}), s16[32,33,8,128]{3,2,1,0:T(8,128)(2,1)}, u32[]{:S(2)}, u32[]{:S(2)}) async-start(s16[32,33,8,128]{3,2,1,0:T(8,128)(2,1)} %following.1), calls=%async_computation.1 | async-start | bytes 4325376 | tf_op jit(solution)/shard_map/all_to_all | solution.py:1124
  145.7 45.3 %all-to-all-done.1.refs_1_ = s16[32,33,8,128]{3,2,1,0:T(8,128)(2,1)} async-done(((s16[32,33,8,128]{3,2,1,0:T(8,128)(2,1)}), s16[32,33,8,128]{3,2,1,0:T(8,128)(2,1)}, u32[]{:S(2)}, u32[]{:S(2)}) %all-to-all-start.1) | async-done | bytes 2162720 | tf_op jit(solution)/shard_map/all_to_all | solution.py:1124
  191.1 2.2 copy-done.12
  193.3 2.2 copy-done.15
  195.4 10.9 %solve_group.4 = s16[32,17,8,128]{3,2,1,0:T(8,128)(2,1)S(1)} custom-call(s16[32,33,8,128]{3,2,1,0:T(8,128)(2,1)S(1)} %copy-done.1, s16[32,33,8,128]{3,2,1,0:T(8,128)(2,1)} %all-to-all-done.1.refs_1_, bf16[2,256,256]{2,1,0:T(8,128)(2,1)S(1)} %get-tuple-element.32.refs_2_, bf16[2,256,256]{2,1,0:T(8,128)(2,1)S(1)} %get-tuple-element.33.refs_3_, ...), custom_call_target="tpu_custom_call" | custom-call | flops 4026531840 | bytes 20971520 | tf_op jit(solution)/shard_map/solve_group/pallas_call | solution.py:1003
  207.4 3.6 %all-to-all-start.3 = ((s16[32,17,8,128]{3,2,1,0:T(8,128)(2,1)}), s16[32,17,8,128]{3,2,1,0:T(8,128)(2,1)S(1)}, u32[]{:S(2)}, u32[]{:S(2)}) async-start(s16[32,17,8,128]{3,2,1,0:T(8,128)(2,1)} %copy-done.4), calls=%async_computation.3 | async-start | bytes 2228224 | tf_op jit(solution)/shard_map/all_to_all | solution.py:1124
  214.3 2.2 copy-done.13
  216.5 2.2 copy-done.16
  218.7 16.2 %solve_group.5 = s16[32,33,8,128]{3,2,1,0:T(8,128)(2,1)S(1)} custom-call(s16[32,33,8,128]{3,2,1,0:T(8,128)(2,1)S(1)} %copy-done.1, s16[32,33,8,128]{3,2,1,0:T(8,128)(2,1)} %all-to-all-done.1.refs_1_, bf16[2,256,256]{2,1,0:T(8,128)(2,1)S(1)} %copy-done.6, bf16[2,256,256]{2,1,0:T(8,128)(2,1)S(1)} %copy-done.9, bf16[4,2,512,512]{3,2,1,0:T(8,128)(2,1)S(1)} %copy-done.16, ...), custom_call_target="tpu_custom_call" | custom-call | flops 8053063680 | bytes 20971520 | tf_op jit(solution)/shard_map/solve_group/pallas_call | solution.py:1003
  234.9 1.3 copy-done.2
  236.3 2.4 all-to-all-done.3.refs_0_
  238.7 3.5 %all-to-all-start.4 = ((s16[32,33,8,128]{3,2,1,0:T(8,128)(2,1)}), s16[32,33,8,128]{3,2,1,0:T(8,128)(2,1)}, u32[]{:S(2)}, u32[]{:S(2)}) async-start(s16[32,33,8,128]{3,2,1,0:T(8,128)(2,1)} %copy-done.2), calls=%async_computation.4 | async-start | bytes 4325376 | tf_op jit(solution)/shard_map/all_to_all | solution.py:1124
  242.2 1.5 slice.36.refs_8_
  243.6 2.2 fusion.8
  245.8 1.7 reshape.223
  249.4 2.2 copy-done.14
  251.6 2.2 copy-done.17
  253.8 10.9 %solve_group.3 = s16[32,17,8,128]{3,2,1,0:T(8,128)(2,1)S(1)} custom-call(s16[32,33,8,128]{3,2,1,0:T(8,128)(2,1)S(1)} %copy-done.1, s16[32,33,8,128]{3,2,1,0:T(8,128)(2,1)} %all-to-all-done.1.refs_1_, bf16[2,256,256]{2,1,0:T(8,128)(2,1)S(1)} %copy-done.7, bf16[2,256,256]{2,1,0:T(8,128)(2,1)S(1)} %copy-done.10, bf16[4,2,512,512]{3,2,1,0:T(8,128)(2,1)S(1)} %copy-done.17, ...), custom_call_target="tpu_custom_call" | custom-call | flops 4026531840 | bytes 20971520 | tf_op jit(solution)/shard_map/solve_group/pallas_call | solution.py:1003
  265.7 26.1 %all-to-all-done.4.refs_1_ = s16[32,33,8,128]{3,2,1,0:T(8,128)(2,1)} async-done(((s16[32,33,8,128]{3,2,1,0:T(8,128)(2,1)}), s16[32,33,8,128]{3,2,1,0:T(8,128)(2,1)}, u32[]{:S(2)}, u32[]{:S(2)}) %all-to-all-start.4) | async-done | bytes 2162720 | tf_op jit(solution)/shard_map/all_to_all | solution.py:1124
  291.9 3.6 %all-to-all-start.2 = ((s16[32,17,8,128]{3,2,1,0:T(8,128)(2,1)}), s16[32,17,8,128]{3,2,1,0:T(8,128)(2,1)S(1)}, u32[]{:S(2)}, u32[]{:S(2)}) async-start(s16[32,17,8,128]{3,2,1,0:T(8,128)(2,1)} %copy-done.3), calls=%async_computation.2 | async-start | bytes 2228224 | tf_op jit(solution)/shard_map/all_to_all | solution.py:1124
  298.8 19.5 %pressure_of.2.refs_2_ = f32[256,16,512]{2,1,0:T(8,128)S(1)} custom-call(s16[32,17,8,128]{3,2,1,0:T(8,128)(2,1)S(1)} %all-to-all-done.3.refs_0_, s16[32,33,8,128]{3,2,1,0:T(8,128)(2,1)} %all-to-all-done.4.refs_1_, bf16[2,384,512]{2,1,0:T(8,128)(2,1)S(1)} %pad_maximum_fusion.2.refs_2_), custom_call_target="tpu_custom_call" | custom-call | flops 16106127360 | bytes 20971520 | tf_op jit(solution)/shard_map/pressure_of/pallas_call | solution.py:1094
  318.3 3.4 copy-done.20
  321.7 1.5 all-to-all-done.2.refs_0_
  323.2 3.4 copy-done.21
  326.6 12.4 %pressure_of.3 = f32[256,16,512]{2,1,0:T(8,128)} custom-call(s16[32,17,8,128]{3,2,1,0:T(8,128)(2,1)S(1)} %all-to-all-done.2.refs_0_, bf16[2,128,512]{2,1,0:T(8,128)(2,1)S(1)} %pad_maximum_fusion.5.refs_1_, f32[256,16,512]{2,1,0:T(8,128)S(1)} %copy-done.21), custom_call_target="tpu_custom_call" | custom-call | flops 5368709120 | bytes 20971520 | tf_op jit(solution)/shard_map/pressure_of/pallas_call | solution.py:1094
  (63 shorter events, 16.2 us)
Async XLA Ops:
  2.2 34.0 %copy-start.22 = (f32[512,512]{0,1:T(8,128)}, f32[512,512]{0,1:T(8,128)S(1)}, u32[]{:S(2)}) copy-start(f32[512,512]{0,1:T(8,128)S(1)} %copy.19) | copy-start | bytes 3145732
  82.0 54.4 %all-to-all-start = ((s16[32,33,8,128]{3,2,1,0:T(8,128)(2,1)}), s16[32,33,8,128]{3,2,1,0:T(8,128)(2,1)S(1)}, u32[]{:S(2)}, u32[]{:S(2)}) async-start(s16[32,33,8,128]{3,2,1,0:T(8,128)(2,1)} %get-tuple-element.14), calls=%async_computation | async-start | bytes 4325376 | tf_op jit(solution)/shard_map/all_to_all | solution.py:1124
  136.4 1.3 copy-start
  137.7 3.7 %copy-start.23 = (f32[64,64]{1,0:T(8,128)S(1)}, f32[64,64]{1,0:T(8,128)}, u32[]{:S(2)}) copy-start(f32[64,64]{1,0:T(8,128)} %param.19) | copy-start | bytes 49156
  137.7 4.5 %copy-start.24 = (f32[64]{0:T(128)S(1)}, f32[64]{0:T(128)}, u32[]{:S(2)}) copy-start(f32[64]{0:T(128)} %param.21) | copy-start | bytes 772
  137.7 53.3 %copy-start.1 = (s16[32,33,8,128]{3,2,1,0:T(8,128)(2,1)S(1)}, s16[32,33,8,128]{3,2,1,0:T(8,128)(2,1)}, u32[]{:S(2)}) copy-start(s16[32,33,8,128]{3,2,1,0:T(8,128)(2,1)} %copy-done) | copy-start | bytes 6488068
  137.7 53.3 %copy-start.18 = (f32[4,1,512]{2,1,0:T(1,128)S(1)}, f32[4,1,512]{2,1,0:T(1,128)}, u32[]{:S(2)}) copy-start(f32[4,1,512]{2,1,0:T(1,128)} %constant.28.clone.refs_7_) | copy-start | bytes 24580
  137.7 53.3 %copy-start.19 = (f32[4,1,512]{2,1,0:T(1,128)S(1)}, f32[4,1,512]{2,1,0:T(1,128)}, u32[]{:S(2)}) copy-start(f32[4,1,512]{2,1,0:T(1,128)} %constant.27.clone.refs_6_) | copy-start | bytes 24580
  137.7 53.3 %all-to-all-start.1 = ((s16[32,33,8,128]{3,2,1,0:T(8,128)(2,1)}), s16[32,33,8,128]{3,2,1,0:T(8,128)(2,1)}, u32[]{:S(2)}, u32[]{:S(2)}) async-start(s16[32,33,8,128]{3,2,1,0:T(8,128)(2,1)} %following.1), calls=%async_computation.1 | async-start | bytes 4325376 | tf_op jit(solution)/shard_map/all_to_all | solution.py:1124
  145.7 60.7 %copy-start.5 = (bf16[2,256,256]{2,1,0:T(8,128)(2,1)}, bf16[2,256,256]{2,1,0:T(8,128)(2,1)S(1)}, u32[]{:S(2)}) copy-start(bf16[2,256,256]{2,1,0:T(8,128)(2,1)S(1)} %get-tuple-element.32.refs_2_) | copy-start | bytes 786436
  145.7 60.7 %copy-start.8 = (bf16[2,256,256]{2,1,0:T(8,128)(2,1)}, bf16[2,256,256]{2,1,0:T(8,128)(2,1)S(1)}, u32[]{:S(2)}) copy-start(bf16[2,256,256]{2,1,0:T(8,128)(2,1)S(1)} %get-tuple-element.33.refs_3_) | copy-start | bytes 786436
  191.1 2.2 copy-start.12
  193.3 2.2 copy-start.15
  206.4 1.0 copy-start.4
  207.4 31.3 %all-to-all-start.3 = ((s16[32,17,8,128]{3,2,1,0:T(8,128)(2,1)}), s16[32,17,8,128]{3,2,1,0:T(8,128)(2,1)S(1)}, u32[]{:S(2)}, u32[]{:S(2)}) async-start(s16[32,17,8,128]{3,2,1,0:T(8,128)(2,1)} %copy-done.4), calls=%async_computation.3 | async-start | bytes 2228224 | tf_op jit(solution)/shard_map/all_to_all | solution.py:1124
  212.4 1.0 copy-start.6
  213.4 0.9 copy-start.9
  214.3 2.2 copy-start.13
  216.5 2.2 copy-start.16
  234.9 1.3 copy-start.2
  236.3 11.3 %copy-start.7 = (bf16[2,256,256]{2,1,0:T(8,128)(2,1)S(1)}, bf16[2,256,256]{2,1,0:T(8,128)(2,1)}, u32[]{:S(2)}) copy-start(bf16[2,256,256]{2,1,0:T(8,128)(2,1)} %copy-done.5) | copy-start | bytes 786436
  238.7 53.2 %all-to-all-start.4 = ((s16[32,33,8,128]{3,2,1,0:T(8,128)(2,1)}), s16[32,33,8,128]{3,2,1,0:T(8,128)(2,1)}, u32[]{:S(2)}, u32[]{:S(2)}) async-start(s16[32,33,8,128]{3,2,1,0:T(8,128)(2,1)} %copy-done.2), calls=%async_computation.4 | async-start | bytes 4325376 | tf_op jit(solution)/shard_map/all_to_all | solution.py:1124
  247.6 1.0 copy-start.10
  248.5 0.9 copy-start.11
  249.4 2.2 copy-start.14
  251.6 2.2 copy-start.17
  264.7 1.0 copy-start.3
  291.9 31.3 %all-to-all-start.2 = ((s16[32,17,8,128]{3,2,1,0:T(8,128)(2,1)}), s16[32,17,8,128]{3,2,1,0:T(8,128)(2,1)S(1)}, u32[]{:S(2)}, u32[]{:S(2)}) async-start(s16[32,17,8,128]{3,2,1,0:T(8,128)(2,1)} %copy-done.3), calls=%async_computation.2 | async-start | bytes 2228224 | tf_op jit(solution)/shard_map/all_to_all | solution.py:1124
  318.3 3.4 %copy-start.20 = (f32[256,16,512]{2,1,0:T(8,128)}, f32[256,16,512]{2,1,0:T(8,128)S(1)}, u32[]{:S(2)}) copy-start(f32[256,16,512]{2,1,0:T(8,128)S(1)} %pressure_of.2.refs_2_) | copy-start | bytes 25165828
  323.2 3.4 copy-start.21

commit v6 on v5

--- a/solution.py
+++ b/solution.py
@@ -297,6 +297,8 @@
 
 CHUNK = 128
 BLOCK = 16
+SOLVE_VMEM = 52
+PRESSURE_VMEM = 58
 SOLVED = ((0, 4), (8, 8), (4, 4))
 FLUX_SCALE = 32767.0 / 0.3
 F32 = jnp.float32
@@ -889,7 +891,7 @@
     tables = np.stack(tables)
     back = np.stack([halves(t) for t in tables])
     forth = np.stack([halves(t.T) for t in tables])
-    return forth, back, np.stack(rates)[:, None].astype(np.float32), np.stack(weights)[:, None].astype(np.float32)
+    return np.stack([forth, back]), np.stack(rates)[:, None].astype(np.float32), np.stack(weights)[:, None].astype(np.float32)
 
 
 def decoded(values):
@@ -902,8 +904,14 @@
 
 def solve_kernel(around, along, chunks, start, *refs):
     got = refs[:chunks]
-    mix, unmix, forth, back, rates, weights, shifts = refs[chunks : chunks + 7]
-    sent, high, low, result, scale, exponents = refs[chunks + 7 :]
+    mix, unmix, tables, rates, weights, shifts = refs[chunks : chunks + 6]
+    sent, high, low, result, scale, exponents, forth, back, arrived = refs[chunks + 6 :]
+    copies = [
+        pltpu.make_async_copy(tables.at[0], forth, arrived.at[0]),
+        pltpu.make_async_copy(tables.at[1], back, arrived.at[1]),
+    ]
+    for copy in copies:
+        copy.start()
     devices, slots, height, lanes = got[0].shape
     count, layers = (sent.shape[1] - 1) // (2 * chunks), 2 * height
     share = (sent.shape[1] - 1) // (2 * chunks)
@@ -945,6 +953,7 @@
 
     lax.fori_loop(0, count * along, fold, 0)
 
+    copies[0].wait()
     deep = mix.shape[1]
     parts = [pl.ds(at, deep) for at in range(0, high.shape[1], deep)]
 
@@ -955,6 +964,7 @@
             )
         spectrum = dot3((high[k], low[k]), (forth[k, 0], forth[k, 1]))
         high[k], low[k] = split(spectrum * weights[k] / (rates[k] + shifts[...]))
+        pl.when(k == 0)(copies[1].wait)
         high[k], low[k] = split(dot3((high[k], low[k]), (back[k, 0], back[k, 1])))
         for at in parts:
             result[k, at] = dot3((unmix[0], unmix[1]), (high[k, at], low[k, at]))
@@ -996,14 +1006,24 @@
     chunks = len(got)
     devices, slots, height, lanes = got[0].shape
     rows = share * along * 2 * height
-    forth, back, rates, weights = tables
-    width = forth.shape[-1]
+    tables, rates, weights = tables
+    width = tables.shape[-1]
     whole = pl.BlockSpec(memory_space=pltpu.VMEM)
+
+    def fixed(array):
+        return pl.BlockSpec(
+            array.shape, lambda i: (0,) * len(array.shape), pipeline_mode=pl.Buffered(1)
+        )
+
     shifts = lax.slice_in_dim(shifts, start * along * 2 * height, start * along * 2 * height + rows)
     return pl.pallas_call(
         functools.partial(solve_kernel, around, along, chunks, start),
-        in_specs=[whole] * (chunks + 7),
-        out_specs=whole,
+        grid=(1,),
+        in_specs=[whole] * chunks
+        + [fixed(mix), fixed(unmix)]
+        + [pl.BlockSpec(memory_space=pl.ANY)]
+        + [fixed(rates), fixed(weights), fixed(shifts)],
+        out_specs=fixed(jax.ShapeDtypeStruct((devices, 2 * chunks * share + 1, height, lanes), jnp.int16)),
         out_shape=jax.ShapeDtypeStruct((devices, 2 * chunks * share + 1, height, lanes), jnp.int16),
         scratch_shapes=[
             pltpu.VMEM((4, rows, width), BF16),
@@ -1011,23 +1031,25 @@
             pltpu.VMEM((4, rows, width), F32),
             pltpu.VMEM((chunks, devices, height, lanes), F32),
             pltpu.VMEM((devices, height, lanes), F32),
+            pltpu.VMEM(tables.shape[1:], BF16),
+            pltpu.VMEM(tables.shape[1:], BF16),
+            pltpu.SemaphoreType.DMA((2,)),
         ],
-        compiler_params=pltpu.CompilerParams(vmem_limit_bytes=32 * 2**20),
+        compiler_params=pltpu.CompilerParams(vmem_limit_bytes=SOLVE_VMEM * 2**20),
         cost_estimate=pl.CostEstimate(
             flops=60 * rows * width * width, bytes_accessed=20 * 2**20, transcendentals=0
         ),
         name="solve_group",
-    )(*got, mix, unmix, forth, back, rates, weights, shifts)
+    )(*got, mix, unmix, tables, rates, weights, shifts)
 
 
 def pressure_kernel(around, groups, chunks, *refs):
     got = refs[:groups]
     basis = refs[groups]
-    base = refs[groups + 1 : -6]
-    out, flat, wide, scale, high, low = refs[-6:]
+    base = refs[groups + 1 : -4]
+    out, flat, turned, scale = refs[-4:]
     devices, _, height, lanes = got[0].shape
     layers = 2 * height
-    lane_tiles = out.shape[2] // 128
     chunk = pl.program_id(0)
     backwards = lax.rem(lax.axis_index("azim"), around // 2) >= around // 4
     i = lax.broadcasted_iota(jnp.int32, (lanes, lanes), 0)
@@ -1054,35 +1076,35 @@
         lax.fori_loop(0, devices, unpack, 0)
         filled += devices * share
 
-    together = high.shape[0] // lanes
-
-    def radial(batch, _):
-        for part in range(together):
-            for offset, height in spans:
-                z = batch * together + part
-                values = split(flat[pl.ds(offset * layers + z, height, stride=layers), :])
-                at = pl.ds(offset, height)
-                for target, value in zip((high, low), values):
-                    target[part * lanes : (part + 1) * lanes, at] = dot(
-                        turn, value, ((1,), (1,))
-                    ).astype(BF16)
-        if filled > 128:
-            total = dot3((high[...], low[...]), (basis[0], basis[1]))
-        else:
-            lower = jnp.concatenate([high[...], low[...], high[...]], axis=1)
-            total = dot(lower, jnp.concatenate([basis[0], basis[0], basis[1]]), ((1,), (0,)))
-        for part in range(together):
-            for tile in range(lane_tiles):
-                wide[tile, pl.ds(batch * together + part, lanes, stride=layers), :] = total[
-                    part * lanes : (part + 1) * lanes, tile * 128 : (tile + 1) * 128
+    def turning(z, _):
+        for offset, height in spans:
+            high, low = split(flat[pl.ds(offset * layers + z, height, stride=layers), :])
+            rows = dot(turn, high, ((1,), (1,))) + dot(turn, low, ((1,), (1,)))
+            for at in range(0, height, 128):
+                turned[(offset + at) // 128, pl.ds(z, lanes, stride=layers), :] = rows[
+                    :, at : at + 128
                 ]
         return 0
 
-    lax.fori_loop(0, layers // together, radial, 0)
-    for tile in range(lane_tiles):
-        at = slice(tile * 128, (tile + 1) * 128)
-        result = wide[tile].reshape(lanes, layers, 128)
-        out[:, :, at] = result + base[0][:, :, at] if base else result
+    lax.fori_loop(0, layers, turning, 0, unroll=4)
+    azimuths = 32
+    height = azimuths * layers
+
+    def radial(batch, _):
+        at = pl.ds(pl.multiple_of(batch * height, height), height)
+        rows = jnp.concatenate([turned[tile, at, :] for tile in range(filled // 128)], axis=1)
+        high, low = split(rows)
+        if filled > 128:
+            total = dot3((high, low), (basis[0], basis[1]))
+        else:
+            rows = jnp.concatenate([high, low, high], axis=1)
+            total = dot(rows, jnp.concatenate([basis[0], basis[0], basis[1]]), ((1,), (0,)))
+        total = total.reshape(azimuths, layers, out.shape[2])
+        at = pl.ds(pl.multiple_of(batch * azimuths, azimuths), azimuths)
+        out[at] = total + base[0][at] if base else total
+        return 0
+
+    lax.fori_loop(0, lanes // azimuths, radial, 0)
 
 
 def pressure_of(got, basis, around, chunks, base=None):
@@ -1100,12 +1122,10 @@
         out_shape=jax.ShapeDtypeStruct((lanes * chunks, layers, cells), F32),
         scratch_shapes=[
             pltpu.VMEM((inner * layers, lanes), F32),
-            pltpu.VMEM((cells // 128, lanes * layers, 128), F32),
+            pltpu.VMEM((inner // 128, lanes * layers, 128), F32),
             pltpu.VMEM((groups, devices, height, lanes), F32),
-            pltpu.VMEM((4 * lanes, inner), BF16),
-            pltpu.VMEM((4 * lanes, inner), BF16),
         ],
-        compiler_params=pltpu.CompilerParams(vmem_limit_bytes=40 * 2**20),
+        compiler_params=pltpu.CompilerParams(vmem_limit_bytes=PRESSURE_VMEM * 2**20),
         cost_estimate=pl.CostEstimate(
             flops=20 * lanes * chunks * layers * cells * inner,
             bytes_accessed=20 * 2**20,
@@ -1132,7 +1152,7 @@
     anywhere = pl.BlockSpec(memory_space=pl.ANY)
     return pl.pallas_call(
         following_kernel,
-        in_specs=[anywhere, anywhere],
+        in_specs=[anywhere, pl.BlockSpec(memory_space=pltpu.VMEM)],
         out_specs=anywhere,
         out_shape=jax.ShapeDtypeStruct(values.shape, values.dtype),
         input_output_aliases={0: 0},

time: 340 us -> 336 us (0.988)
  local copies, waits for them, and re-layouts: 41.8 us -> 5.99 us
  waiting for transfers between devices: 79.2 us -> 99.8 us
  Pallas kernels: 194 us -> 206 us
    unnamed x51 -> x13, local copies, waits for them, and re-layouts: 29.9 us -> 3.69 us
    all_to_all x5, waiting for transfers between devices: 79.2 us -> 99.8 us  [exchanged(): lax.all_to_all(sent, ('azim', 'axial'), split_axis=0, concat_axis=0, tile...]
    pallas_call x3, Pallas kernels: 38.1 us -> 48.6 us  [solve_group(): pl.pallas_call(functools.partial(solve_kernel, around, along, chunks, sta...]
  transfers between devices with their start and end apart: 5 -> 5, of which waited for: 5 -> 5; matrix products, arithmetic and copies ran while one was open for 4% -> 1% of each run, Pallas kernels for 27% -> 30%
where the time goes in v6:
time: 336 us; the launch traced here: 335 us
  Pallas kernels  206 us (61%)
  waiting for transfers between devices  99.8 us (30%)
  starting transfers between devices  19 us (6%)
  local copies, waits for them, and re-layouts  5.99 us (2%)
  other arithmetic  3.46 us (1%)
    all_to_all x5, waiting for transfers between devices, exchanged(): lax.all_to_all(sent, ('azim', 'axial'), split_axis=0, concat_axis=0, tile...  99.8 us
    pallas_call x2, Pallas kernels, advect_chunk(): pl.pallas_call(functools.partial(chunk_kernel, around, chunk_index, rows...  91.6 us
    pallas_call x3, Pallas kernels, solve_group(): pl.pallas_call(functools.partial(solve_kernel, around, along, chunks, sta...  48.6 us
    pallas_call x1, Pallas kernels, halos(): pl.pallas_call(halo_kernel, grid=(2 * half,), in_specs=in_specs, out_spec...  32.6 us
    pallas_call x2, Pallas kernels, pressure_of(): pl.pallas_call(functools.partial(pressure_kernel, around, groups, chunks)...  31.6 us
    all_to_all x5, starting transfers between devices, exchanged(): lax.all_to_all(sent, ('azim', 'axial'), split_axis=0, concat_axis=0, tile...  19 us
  transfers between devices with their start and end apart: 5, of which 5 were waited for; matrix products, arithmetic and copies ran while one was open for 1% of the time, Pallas kernels for 30%

profile of v6, /device:TPU:1, one launch (start us, length us, event | category | flops | bytes accessed | tf_op | source)
XLA Modules:
  0.0 335.2 jit_solution(15567041925163258869)
XLA Ops:
  0.6 1.6 copy.18
  2.2 0.2 fusion.3
  2.4 1.1 pad_maximum_fusion.basis_ref
  3.4 32.6 %halos.1 = (f32[2,256,512]{2,1,0:T(8,128)}, f32[2,256,512]{2,1,0:T(8,128)}, bf16[2,5,16,512]{3,2,1,0:T(8,128)(2,1)}) custom-call(bf16[3,256,16,512]{3,2,1,0:T(8,128)(2,1)} %last_courant_ref.5, bf16[3,256,16,512]{3,2,1,0:T(8,128)(2,1)} %last_normals_ref.5, bf16[256,16,512]{2,1,0:T(8,128)(2,1)} %last_planes_ref.5, s32[256,16,512]{2,1,0:T(8,128)} %last_flags_ref.5, ...), custom_call_target="tpu_custom_call" | custom-call | tf_op jit(solution)/shard_map/halos/pallas_call | solution.py:566
  36.0 45.9 %advect_chunk.2 = (f32[256,16,512]{2,1,0:T(8,128)}, s16[32,33,8,128]{3,2,1,0:T(8,128)(2,1)}) custom-call(f32[256,16,512]{2,1,0:T(8,128)} %fraction_ref.3, bf16[3,256,16,512]{3,2,1,0:T(8,128)(2,1)} %last_normals_ref.5, bf16[256,16,512]{2,1,0:T(8,128)(2,1)} %last_planes_ref.5, s32[256,16,512]{2,1,0:T(8,128)} %last_flags_ref.5, ...), custom_call_target="tpu_custom_call" | custom-call | flops 41943040000 | bytes 31457280 | tf_op jit(solution)/shard_map/advect_chunk/pallas_call | solution.py:843
  81.9 4.8 %all-to-all-start = ((s16[32,33,8,128]{3,2,1,0:T(8,128)(2,1)}), s16[32,33,8,128]{3,2,1,0:T(8,128)(2,1)}, u32[]{:S(2)}, u32[]{:S(2)}) async-start(s16[32,33,8,128]{3,2,1,0:T(8,128)(2,1)} %get-tuple-element.14), calls=%async_computation | async-start | bytes 4325376 | tf_op jit(solution)/shard_map/all_to_all | solution.py:1144
  86.7 45.8 %advect_chunk.3 = (f32[256,16,512]{2,1,0:T(8,128)}, s16[32,33,8,128]{3,2,1,0:T(8,128)(2,1)}) custom-call(f32[256,16,512]{2,1,0:T(8,128)} %fraction_ref.3, bf16[3,256,16,512]{3,2,1,0:T(8,128)(2,1)} %last_normals_ref.5, bf16[256,16,512]{2,1,0:T(8,128)(2,1)} %last_planes_ref.5, s32[256,16,512]{2,1,0:T(8,128)} %last_flags_ref.5, ...), custom_call_target="tpu_custom_call", output_to_operand_aliasing={{0}: (17, {})} | custom-call | flops 41943040000 | bytes 31457280 | tf_op jit(solution)/shard_map/advect_chunk/pallas_call | solution.py:843
  132.5 4.0 %all-to-all-done.earlier_ref.refs_0_ = s16[32,33,8,128]{3,2,1,0:T(8,128)(2,1)} async-done(((s16[32,33,8,128]{3,2,1,0:T(8,128)(2,1)}), s16[32,33,8,128]{3,2,1,0:T(8,128)(2,1)}, u32[]{:S(2)}, u32[]{:S(2)}) %all-to-all-start) | async-done | bytes 2162720 | tf_op jit(solution)/shard_map/all_to_all | solution.py:1144
  136.5 1.6 following.1
  138.1 3.6 %all-to-all-start.1 = ((s16[32,33,8,128]{3,2,1,0:T(8,128)(2,1)}), s16[32,33,8,128]{3,2,1,0:T(8,128)(2,1)}, u32[]{:S(2)}, u32[]{:S(2)}) async-start(s16[32,33,8,128]{3,2,1,0:T(8,128)(2,1)} %following.1), calls=%async_computation.1 | async-start | bytes 4325376 | tf_op jit(solution)/shard_map/all_to_all | solution.py:1144
  141.8 0.8 dynamic_slice.3
  142.6 0.1 slice.37.refs_7_
  142.8 0.2 broadcast_multiply_fusion
  143.0 0.3 mul.75
  143.4 0.3 mul.72
  143.8 47.5 %all-to-all-done.1.refs_1_ = s16[32,33,8,128]{3,2,1,0:T(8,128)(2,1)} async-done(((s16[32,33,8,128]{3,2,1,0:T(8,128)(2,1)}), s16[32,33,8,128]{3,2,1,0:T(8,128)(2,1)}, u32[]{:S(2)}, u32[]{:S(2)}) %all-to-all-start.1) | async-done | bytes 2162720 | tf_op jit(solution)/shard_map/all_to_all | solution.py:1144
  191.4 14.6 %solve_group.4 = s16[32,17,8,128]{3,2,1,0:T(8,128)(2,1)} custom-call(s16[32,33,8,128]{3,2,1,0:T(8,128)(2,1)} %all-to-all-done.earlier_ref.refs_0_, s16[32,33,8,128]{3,2,1,0:T(8,128)(2,1)} %all-to-all-done.1.refs_1_, bf16[2,256,256]{2,1,0:T(8,128)(2,1)S(1)} %get-tuple-element.32.refs_2_, bf16[2,256,256]{2,1,0:T(8,128)(2,1)S(1)} %get-tuple-element.33.refs_3_, ...), custom_call_target="tpu_custom_call" | custom-call | flops 4026531840 | bytes 20971520 | tf_op jit(solution)/shard_map/solve_group/pallas_call | solution.py:1019
  206.0 3.6 %all-to-all-start.3 = ((s16[32,17,8,128]{3,2,1,0:T(8,128)(2,1)}), s16[32,17,8,128]{3,2,1,0:T(8,128)(2,1)S(1)}, u32[]{:S(2)}, u32[]{:S(2)}) async-start(s16[32,17,8,128]{3,2,1,0:T(8,128)(2,1)} %solve_group.4), calls=%async_computation.3 | async-start | bytes 2228224 | tf_op jit(solution)/shard_map/all_to_all | solution.py:1144
  209.6 0.2 slice.38.refs_7_
  209.8 19.5 %solve_group.5 = s16[32,33,8,128]{3,2,1,0:T(8,128)(2,1)} custom-call(s16[32,33,8,128]{3,2,1,0:T(8,128)(2,1)} %all-to-all-done.earlier_ref.refs_0_, s16[32,33,8,128]{3,2,1,0:T(8,128)(2,1)} %all-to-all-done.1.refs_1_, bf16[2,256,256]{2,1,0:T(8,128)(2,1)S(1)} %get-tuple-element.32.refs_2_, bf16[2,256,256]{2,1,0:T(8,128)(2,1)S(1)} %get-tuple-element.33.refs_3_, ...), custom_call_target="tpu_custom_call" | custom-call | flops 8053063680 | bytes 20971520 | tf_op jit(solution)/shard_map/solve_group/pallas_call | solution.py:1019
  229.2 8.0 %all-to-all-done.3.refs_0_ = s16[32,17,8,128]{3,2,1,0:T(8,128)(2,1)S(1)} async-done(((s16[32,17,8,128]{3,2,1,0:T(8,128)(2,1)}), s16[32,17,8,128]{3,2,1,0:T(8,128)(2,1)S(1)}, u32[]{:S(2)}, u32[]{:S(2)}) %all-to-all-start.3) | async-done | bytes 1114144 | tf_op jit(solution)/shard_map/all_to_all | solution.py:1144
  237.3 1.0 copy-done.2
  238.3 3.4 %all-to-all-start.4 = ((s16[32,33,8,128]{3,2,1,0:T(8,128)(2,1)}), s16[32,33,8,128]{3,2,1,0:T(8,128)(2,1)}, u32[]{:S(2)}, u32[]{:S(2)}) async-start(s16[32,33,8,128]{3,2,1,0:T(8,128)(2,1)} %solve_group.5), calls=%async_computation.4 | async-start | bytes 4325376 | tf_op jit(solution)/shard_map/all_to_all | solution.py:1144
  242.1 14.6 %solve_group.3 = s16[32,17,8,128]{3,2,1,0:T(8,128)(2,1)} custom-call(s16[32,33,8,128]{3,2,1,0:T(8,128)(2,1)} %all-to-all-done.earlier_ref.refs_0_, s16[32,33,8,128]{3,2,1,0:T(8,128)(2,1)} %all-to-all-done.1.refs_1_, bf16[2,256,256]{2,1,0:T(8,128)(2,1)S(1)} %get-tuple-element.32.refs_2_, bf16[2,256,256]{2,1,0:T(8,128)(2,1)S(1)} %get-tuple-element.33.refs_3_, ...), custom_call_target="tpu_custom_call" | custom-call | flops 4026531840 | bytes 20971520 | tf_op jit(solution)/shard_map/solve_group/pallas_call | solution.py:1019
  256.7 34.5 %all-to-all-done.4.refs_1_ = s16[32,33,8,128]{3,2,1,0:T(8,128)(2,1)} async-done(((s16[32,33,8,128]{3,2,1,0:T(8,128)(2,1)}), s16[32,33,8,128]{3,2,1,0:T(8,128)(2,1)}, u32[]{:S(2)}, u32[]{:S(2)}) %all-to-all-start.4) | async-done | bytes 2162720 | tf_op jit(solution)/shard_map/all_to_all | solution.py:1144
  291.2 3.6 %all-to-all-start.2 = ((s16[32,17,8,128]{3,2,1,0:T(8,128)(2,1)}), s16[32,17,8,128]{3,2,1,0:T(8,128)(2,1)S(1)}, u32[]{:S(2)}, u32[]{:S(2)}) async-start(s16[32,17,8,128]{3,2,1,0:T(8,128)(2,1)} %solve_group.3), calls=%async_computation.2 | async-start | bytes 2228224 | tf_op jit(solution)/shard_map/all_to_all | solution.py:1144
  295.0 0.7 pad_maximum_fusion.5.refs_1_
  295.9 0.9 pad_maximum_fusion.2.refs_2_
  296.8 20.1 %pressure_of.2.refs_2_ = f32[256,16,512]{2,1,0:T(8,128)} custom-call(s16[32,17,8,128]{3,2,1,0:T(8,128)(2,1)} %copy-done.2, s16[32,33,8,128]{3,2,1,0:T(8,128)(2,1)} %all-to-all-done.4.refs_1_, bf16[2,384,512]{2,1,0:T(8,128)(2,1)} %pad_maximum_fusion.2.refs_2_), custom_call_target="tpu_custom_call" | custom-call | flops 16106127360 | bytes 20971520 | tf_op jit(solution)/shard_map/pressure_of/pallas_call | solution.py:1116
  316.9 5.7 %all-to-all-done.2.refs_0_ = s16[32,17,8,128]{3,2,1,0:T(8,128)(2,1)S(1)} async-done(((s16[32,17,8,128]{3,2,1,0:T(8,128)(2,1)}), s16[32,17,8,128]{3,2,1,0:T(8,128)(2,1)S(1)}, u32[]{:S(2)}, u32[]{:S(2)}) %all-to-all-start.2) | async-done | bytes 1114144 | tf_op jit(solution)/shard_map/all_to_all | solution.py:1144
  322.6 1.1 copy-done.3
  323.6 11.6 %pressure_of.3 = f32[256,16,512]{2,1,0:T(8,128)} custom-call(s16[32,17,8,128]{3,2,1,0:T(8,128)(2,1)} %copy-done.3, bf16[2,128,512]{2,1,0:T(8,128)(2,1)} %pad_maximum_fusion.5.refs_1_, f32[256,16,512]{2,1,0:T(8,128)} %pressure_of.2.refs_2_), custom_call_target="tpu_custom_call" | custom-call | flops 5368709120 | bytes 20971520 | tf_op jit(solution)/shard_map/pressure_of/pallas_call | solution.py:1116
  (25 shorter events, 0.9 us)
Async XLA Ops:
  81.9 54.5 %all-to-all-start = ((s16[32,33,8,128]{3,2,1,0:T(8,128)(2,1)}), s16[32,33,8,128]{3,2,1,0:T(8,128)(2,1)}, u32[]{:S(2)}, u32[]{:S(2)}) async-start(s16[32,33,8,128]{3,2,1,0:T(8,128)(2,1)} %get-tuple-element.14), calls=%async_computation | async-start | bytes 4325376 | tf_op jit(solution)/shard_map/all_to_all | solution.py:1144
  138.1 3.6 %copy-start.4 = (f32[64,64]{1,0:T(8,128)S(1)}, f32[64,64]{1,0:T(8,128)}, u32[]{:S(2)}) copy-start(f32[64,64]{1,0:T(8,128)} %param.18) | copy-start | bytes 49156
  138.1 4.5 %copy-start.5 = (f32[64]{0:T(128)S(1)}, f32[64]{0:T(128)}, u32[]{:S(2)}) copy-start(f32[64]{0:T(128)} %param.20) | copy-start | bytes 772
  138.1 53.3 %all-to-all-start.1 = ((s16[32,33,8,128]{3,2,1,0:T(8,128)(2,1)}), s16[32,33,8,128]{3,2,1,0:T(8,128)(2,1)}, u32[]{:S(2)}, u32[]{:S(2)}) async-start(s16[32,33,8,128]{3,2,1,0:T(8,128)(2,1)} %following.1), calls=%async_computation.1 | async-start | bytes 4325376 | tf_op jit(solution)/shard_map/all_to_all | solution.py:1144
  142.8 48.6 %copy-start = (f32[4,1,512]{2,1,0:T(1,128)S(1)}, f32[4,1,512]{2,1,0:T(1,128)}, u32[]{:S(2)}) copy-start(f32[4,1,512]{2,1,0:T(1,128)} %constant.25.clone.refs_6_) | copy-start | bytes 24580
  142.8 48.6 %copy-start.1 = (f32[4,1,512]{2,1,0:T(1,128)S(1)}, f32[4,1,512]{2,1,0:T(1,128)}, u32[]{:S(2)}) copy-start(f32[4,1,512]{2,1,0:T(1,128)} %constant.24.clone.refs_5_) | copy-start | bytes 24580
  206.0 31.3 %all-to-all-start.3 = ((s16[32,17,8,128]{3,2,1,0:T(8,128)(2,1)}), s16[32,17,8,128]{3,2,1,0:T(8,128)(2,1)S(1)}, u32[]{:S(2)}, u32[]{:S(2)}) async-start(s16[32,17,8,128]{3,2,1,0:T(8,128)(2,1)} %solve_group.4), calls=%async_computation.3 | async-start | bytes 2228224 | tf_op jit(solution)/shard_map/all_to_all | solution.py:1144
  237.3 1.0 copy-start.2
  238.3 52.9 %all-to-all-start.4 = ((s16[32,33,8,128]{3,2,1,0:T(8,128)(2,1)}), s16[32,33,8,128]{3,2,1,0:T(8,128)(2,1)}, u32[]{:S(2)}, u32[]{:S(2)}) async-start(s16[32,33,8,128]{3,2,1,0:T(8,128)(2,1)} %solve_group.5), calls=%async_computation.4 | async-start | bytes 4325376 | tf_op jit(solution)/shard_map/all_to_all | solution.py:1144
  291.2 31.3 %all-to-all-start.2 = ((s16[32,17,8,128]{3,2,1,0:T(8,128)(2,1)}), s16[32,17,8,128]{3,2,1,0:T(8,128)(2,1)S(1)}, u32[]{:S(2)}, u32[]{:S(2)}) async-start(s16[32,17,8,128]{3,2,1,0:T(8,128)(2,1)} %solve_group.3), calls=%async_computation.2 | async-start | bytes 2228224 | tf_op jit(solution)/shard_map/all_to_all | solution.py:1144
  322.5 1.1 copy-start.3

commit v7 on v6

--- a/solution.py
+++ b/solution.py
@@ -297,8 +297,8 @@
 
 CHUNK = 128
 BLOCK = 16
-SOLVE_VMEM = 52
-PRESSURE_VMEM = 58
+SOLVE_VMEM = 62
+PRESSURE_VMEM = 62
 SOLVED = ((0, 4), (8, 8), (4, 4))
 FLUX_SCALE = 32767.0 / 0.3
 F32 = jnp.float32
@@ -590,7 +590,7 @@
             dma((2, groups)),
         ],
         compiler_params=pltpu.CompilerParams(
-            collective_id=0, has_side_effects=True, vmem_limit_bytes=60 * 2**20
+            collective_id=0, has_side_effects=True, vmem_limit_bytes=62 * 2**20
         ),
         name="halos",
     )(courant, normals, planes, flags, *(normals, planes, flags, courant) * 2)
@@ -629,7 +629,7 @@
 ):
     if chunk_index:
         rest = rest[1:]
-    updated_ref, sent_ref, parts, kept, source, wide, scales = rest
+    updated_ref, sent_ref, parts, kept, source, wide, scales, turned = rest
     block, layers, cells = fraction_ref.shape
     steps = pl.num_programs(0)
     step = pl.program_id(0)
@@ -698,6 +698,7 @@
             put_row(
                 block + 1, last_normals_ref, last_planes_ref, last_flags_ref, last_courant_ref
             )
+        turned[0], turned[1] = split(basis_ref[...].T)
         speed = get_field(block + 1, 6) + get_field(0, 6)
         kept[0] = upwind_flux(0, read_parts(block + 1), read_parts(0), speed)
         kept[1] = speed
@@ -762,7 +763,7 @@
         def radial(z, _):
             at = pl.ds(pl.multiple_of(z * 2 * chunk, 2 * chunk), 2 * chunk)
             rows = jnp.concatenate([source[tile, at, :] for tile in range(lane_tiles)], axis=1)
-            both = dot3((basis_ref[0], basis_ref[1]), split(rows), ((1,), (1,)))
+            both = dot3((turned[0], turned[1]), split(rows), ((1,), (1,)))
             for half in range(2):
                 got = both[:, half * chunk : (half + 1) * chunk]
                 scales[...] = jnp.maximum(scales[...], jnp.abs(got))
@@ -827,7 +828,7 @@
         pl.BlockSpec(ends.shape, lambda i: (0, 0, 0, 0)),
         edge,
         edge,
-        pl.BlockSpec((2, cells, cells), lambda i: (0, 0, 0)),
+        pl.BlockSpec((cells, cells), lambda i: (0, 0), pipeline_mode=pl.Buffered(1)),
     ]
     operands = [
         fraction, normals, planes, flags, courant,
@@ -858,9 +859,10 @@
             pltpu.VMEM((cells // 128, layers * chunk, 128), F32),
             pltpu.VMEM((cells * layers, chunk), F32),
             pltpu.VMEM((cells, chunk), F32),
+            pltpu.VMEM((2, cells, cells), BF16),
         ],
         input_output_aliases=aliases,
-        compiler_params=pltpu.CompilerParams(vmem_limit_bytes=60 * 2**20),
+        compiler_params=pltpu.CompilerParams(vmem_limit_bytes=62 * 2**20),
         cost_estimate=pl.CostEstimate(
             flops=40000 * chunk * layers * cells, bytes_accessed=30 * chunk * layers * cells, transcendentals=0
         ),
@@ -904,21 +906,23 @@
 
 def solve_kernel(around, along, chunks, start, *refs):
     got = refs[:chunks]
-    mix, unmix, tables, rates, weights, shifts = refs[chunks : chunks + 6]
-    sent, high, low, result, scale, exponents, forth, back, arrived = refs[chunks + 6 :]
+    extra = refs[chunks : 2 * chunks]
+    refs = refs[2 * chunks :]
+    mix, unmix, tables, rates, weights, shifts = refs[:6]
+    sent, high, low, result, scale, exponents, forth, back, arrived = refs[6:]
     copies = [
         pltpu.make_async_copy(tables.at[0], forth, arrived.at[0]),
         pltpu.make_async_copy(tables.at[1], back, arrived.at[1]),
     ]
     for copy in copies:
         copy.start()
-    devices, slots, height, lanes = got[0].shape
+    devices, _, height, lanes = got[0].shape
     count, layers = (sent.shape[1] - 1) // (2 * chunks), 2 * height
     share = (sent.shape[1] - 1) // (2 * chunks)
     together = chunks * share // height
     pairs = around // 4
     for chunk in range(chunks):
-        scale[chunk] = scale_of(got[chunk][:, slots - 1])
+        scale[chunk] = scale_of(extra[chunk][:, 0])
     def spots():
         for pair in range(pairs):
             for chunk in range(chunks):
@@ -939,7 +943,7 @@
             u0, u1, r0, r1 = [
                 jnp.concatenate(
                     [
-                        decoded(got[chunk][azim * along + axial, 2 * (start + mode) + part])
+                        decoded(got[chunk][azim * along + axial, 2 * mode + part])
                         * scale[chunk, azim * along + axial, row, :]
                         for part in range(2)
                     ]
@@ -1008,7 +1012,6 @@
     rows = share * along * 2 * height
     tables, rates, weights = tables
     width = tables.shape[-1]
-    whole = pl.BlockSpec(memory_space=pltpu.VMEM)
 
     def fixed(array):
         return pl.BlockSpec(
@@ -1019,7 +1022,22 @@
     return pl.pallas_call(
         functools.partial(solve_kernel, around, along, chunks, start),
         grid=(1,),
-        in_specs=[whole] * chunks
+        in_specs=[
+            pl.BlockSpec(
+                (devices, 2 * share, height, lanes),
+                lambda i: (0, start // share, 0, 0),
+                pipeline_mode=pl.Buffered(1),
+            )
+        ]
+        * chunks
+        + [
+            pl.BlockSpec(
+                (devices, 1, height, lanes),
+                lambda i: (0, slots - 1, 0, 0),
+                pipeline_mode=pl.Buffered(1),
+            )
+        ]
+        * chunks
         + [fixed(mix), fixed(unmix)]
         + [pl.BlockSpec(memory_space=pl.ANY)]
         + [fixed(rates), fixed(weights), fixed(shifts)],
@@ -1040,7 +1058,7 @@
             flops=60 * rows * width * width, bytes_accessed=20 * 2**20, transcendentals=0
         ),
         name="solve_group",
-    )(*got, mix, unmix, tables, rates, weights, shifts)
+    )(*got, *got, mix, unmix, tables, rates, weights, shifts)
 
 
 def pressure_kernel(around, groups, chunks, *refs):
@@ -1152,7 +1170,11 @@
     anywhere = pl.BlockSpec(memory_space=pl.ANY)
     return pl.pallas_call(
         following_kernel,
-        in_specs=[anywhere, pl.BlockSpec(memory_space=pltpu.VMEM)],
+        grid=(1,),
+        in_specs=[
+            anywhere,
+            pl.BlockSpec((1, 1) + earlier.shape[2:], lambda i: (0, 0, 0, 0)),
+        ],
         out_specs=anywhere,
         out_shape=jax.ShapeDtypeStruct(values.shape, values.dtype),
         input_output_aliases={0: 0},
@@ -1177,12 +1199,11 @@
     modes = cells // devices
     chunks = rows // CHUNK
     axial_flux, axial_speed, ends = halos(normals, planes, cell_flags, courant)
-    forward_basis = halves(radial_basis.T)
     arrays = (fraction, normals, planes, cell_flags, courant)
     updated, got = None, []
     for chunk in range(chunks):
         updated, sent = advect_chunk(
-            arrays, ends, axial_flux, axial_speed, forward_basis, chunk, CHUNK, around, devices, updated
+            arrays, ends, axial_flux, axial_speed, radial_basis, chunk, CHUNK, around, devices, updated
         )
         got.append(exchanged(following(sent, got[-1]) if got else sent))
     count = jnp.eye(4, dtype=F32)

time: 336 us -> 331 us (0.985)
  transfers between devices with their start and end apart: 5 -> 5, of which waited for: 5 -> 5; matrix products, arithmetic and copies ran while one was open for 1% -> 2% of each run, Pallas kernels for 30% -> 30%
where the time goes in v7:
time: 331 us; the launch traced here: 330 us
  Pallas kernels  204 us (62%)
  waiting for transfers between devices  97.7 us (30%)
  starting transfers between devices  19 us (6%)
  local copies, waits for them, and re-layouts  5.67 us (2%)
    all_to_all x5, waiting for transfers between devices, exchanged(): lax.all_to_all(sent, ('azim', 'axial'), split_axis=0, concat_axis=0, tile...  97.7 us
    pallas_call x2, Pallas kernels, advect_chunk(): pl.pallas_call(functools.partial(chunk_kernel, around, chunk_index, rows...  92.2 us
    pallas_call x3, Pallas kernels, solve_group(): pl.pallas_call(functools.partial(solve_kernel, around, along, chunks, sta...  46.6 us
    pallas_call x1, Pallas kernels, halos(): pl.pallas_call(halo_kernel, grid=(2 * half,), in_specs=in_specs, out_spec...  32.6 us
    pallas_call x2, Pallas kernels, pressure_of(): pl.pallas_call(functools.partial(pressure_kernel, around, groups, chunks)...  31.6 us
    all_to_all x5, starting transfers between devices, exchanged(): lax.all_to_all(sent, ('azim', 'axial'), split_axis=0, concat_axis=0, tile...  19 us
  transfers between devices with their start and end apart: 5, of which 5 were waited for; matrix products, arithmetic and copies ran while one was open for 2% of the time, Pallas kernels for 30%

profile of v7, /device:TPU:1, one launch (start us, length us, event | category | flops | bytes accessed | tf_op | source)
XLA Modules:
  0.0 329.9 jit_solution(16993182939687797633)
XLA Ops:
  0.6 32.6 %halos.1 = (f32[2,256,512]{2,1,0:T(8,128)}, f32[2,256,512]{2,1,0:T(8,128)}, bf16[2,5,16,512]{3,2,1,0:T(8,128)(2,1)}) custom-call(bf16[3,256,16,512]{3,2,1,0:T(8,128)(2,1)} %last_courant_ref.5, bf16[3,256,16,512]{3,2,1,0:T(8,128)(2,1)} %last_normals_ref.5, bf16[256,16,512]{2,1,0:T(8,128)(2,1)} %last_planes_ref.5, s32[256,16,512]{2,1,0:T(8,128)} %last_flags_ref.5, ...), custom_call_target="tpu_custom_call" | custom-call | tf_op jit(solution)/shard_map/halos/pallas_call | solution.py:566
  33.3 46.1 %advect_chunk.2 = (f32[256,16,512]{2,1,0:T(8,128)}, s16[32,33,8,128]{3,2,1,0:T(8,128)(2,1)}) custom-call(f32[256,16,512]{2,1,0:T(8,128)} %fraction_ref.3, bf16[3,256,16,512]{3,2,1,0:T(8,128)(2,1)} %last_normals_ref.5, bf16[256,16,512]{2,1,0:T(8,128)(2,1)} %last_planes_ref.5, s32[256,16,512]{2,1,0:T(8,128)} %last_flags_ref.5, ...), custom_call_target="tpu_custom_call" | custom-call | flops 41943040000 | bytes 31457280 | tf_op jit(solution)/shard_map/advect_chunk/pallas_call | solution.py:844
  79.4 4.8 %all-to-all-start = ((s16[32,33,8,128]{3,2,1,0:T(8,128)(2,1)}), s16[32,33,8,128]{3,2,1,0:T(8,128)(2,1)}, u32[]{:S(2)}, u32[]{:S(2)}) async-start(s16[32,33,8,128]{3,2,1,0:T(8,128)(2,1)} %get-tuple-element.14), calls=%async_computation | async-start | bytes 4325376 | tf_op jit(solution)/shard_map/all_to_all | solution.py:1162
  84.2 46.1 %advect_chunk.3 = (f32[256,16,512]{2,1,0:T(8,128)}, s16[32,33,8,128]{3,2,1,0:T(8,128)(2,1)}) custom-call(f32[256,16,512]{2,1,0:T(8,128)} %fraction_ref.3, bf16[3,256,16,512]{3,2,1,0:T(8,128)(2,1)} %last_normals_ref.5, bf16[256,16,512]{2,1,0:T(8,128)(2,1)} %last_planes_ref.5, s32[256,16,512]{2,1,0:T(8,128)} %last_flags_ref.5, ...), custom_call_target="tpu_custom_call", output_to_operand_aliasing={{0}: (17, {})} | custom-call | flops 41943040000 | bytes 31457280 | tf_op jit(solution)/shard_map/advect_chunk/pallas_call | solution.py:844
  130.2 3.7 %all-to-all-done.earlier_ref.refs_0_.refs_2_ = s16[32,33,8,128]{3,2,1,0:T(8,128)(2,1)} async-done(((s16[32,33,8,128]{3,2,1,0:T(8,128)(2,1)}), s16[32,33,8,128]{3,2,1,0:T(8,128)(2,1)}, u32[]{:S(2)}, u32[]{:S(2)}) %all-to-all-start) | async-done | bytes 2162720 | tf_op jit(solution)/shard_map/all_to_all | solution.py:1162
  133.9 0.7 following.1
  134.6 3.6 %all-to-all-start.1 = ((s16[32,33,8,128]{3,2,1,0:T(8,128)(2,1)}), s16[32,33,8,128]{3,2,1,0:T(8,128)(2,1)}, u32[]{:S(2)}, u32[]{:S(2)}) async-start(s16[32,33,8,128]{3,2,1,0:T(8,128)(2,1)} %following.1), calls=%async_computation.1 | async-start | bytes 4325376 | tf_op jit(solution)/shard_map/all_to_all | solution.py:1162
  138.3 0.8 dynamic_slice.3
  139.1 0.8 slice.37.refs_9_
  139.9 0.2 broadcast_multiply_fusion
  140.2 0.3 mul.75
  140.5 0.3 mul.72
  140.9 0.9 pad_maximum_fusion.2
  141.8 46.1 %all-to-all-done.1.refs_1_.refs_3_ = s16[32,33,8,128]{3,2,1,0:T(8,128)(2,1)} async-done(((s16[32,33,8,128]{3,2,1,0:T(8,128)(2,1)}), s16[32,33,8,128]{3,2,1,0:T(8,128)(2,1)}, u32[]{:S(2)}, u32[]{:S(2)}) %all-to-all-start.1) | async-done | bytes 2162720 | tf_op jit(solution)/shard_map/all_to_all | solution.py:1162
  187.9 13.8 %solve_group.4 = s16[32,17,8,128]{3,2,1,0:T(8,128)(2,1)} custom-call(s16[32,33,8,128]{3,2,1,0:T(8,128)(2,1)} %all-to-all-done.earlier_ref.refs_0_.refs_2_, s16[32,33,8,128]{3,2,1,0:T(8,128)(2,1)} %all-to-all-done.1.refs_1_.refs_3_, s16[32,33,8,128]{3,2,1,0:T(8,128)(2,1)} %all-to-all-done.earlier_ref.refs_0_.refs_2_, ...), custom_call_target="tpu_custom_call" | custom-call | flops 4026531840 | bytes 20971520 | tf_op jit(solution)/shard_map/solve_group/pallas_call | solution.py:1022
  201.7 3.6 %all-to-all-start.3 = ((s16[32,17,8,128]{3,2,1,0:T(8,128)(2,1)}), s16[32,17,8,128]{3,2,1,0:T(8,128)(2,1)S(1)}, u32[]{:S(2)}, u32[]{:S(2)}) async-start(s16[32,17,8,128]{3,2,1,0:T(8,128)(2,1)} %solve_group.4), calls=%async_computation.3 | async-start | bytes 2228224 | tf_op jit(solution)/shard_map/all_to_all | solution.py:1162
  205.3 0.9 slice.38.refs_9_
  206.2 19.0 %solve_group.5 = s16[32,33,8,128]{3,2,1,0:T(8,128)(2,1)} custom-call(s16[32,33,8,128]{3,2,1,0:T(8,128)(2,1)} %all-to-all-done.earlier_ref.refs_0_.refs_2_, s16[32,33,8,128]{3,2,1,0:T(8,128)(2,1)} %all-to-all-done.1.refs_1_.refs_3_, s16[32,33,8,128]{3,2,1,0:T(8,128)(2,1)} %all-to-all-done.earlier_ref.refs_0_.refs_2_, ...), custom_call_target="tpu_custom_call" | custom-call | flops 8053063680 | bytes 20971520 | tf_op jit(solution)/shard_map/solve_group/pallas_call | solution.py:1022
  225.2 7.8 %all-to-all-done.3.refs_0_ = s16[32,17,8,128]{3,2,1,0:T(8,128)(2,1)S(1)} async-done(((s16[32,17,8,128]{3,2,1,0:T(8,128)(2,1)}), s16[32,17,8,128]{3,2,1,0:T(8,128)(2,1)S(1)}, u32[]{:S(2)}, u32[]{:S(2)}) %all-to-all-start.3) | async-done | bytes 1114144 | tf_op jit(solution)/shard_map/all_to_all | solution.py:1162
  233.0 1.0 copy-done
  234.0 3.4 %all-to-all-start.4 = ((s16[32,33,8,128]{3,2,1,0:T(8,128)(2,1)}), s16[32,33,8,128]{3,2,1,0:T(8,128)(2,1)}, u32[]{:S(2)}, u32[]{:S(2)}) async-start(s16[32,33,8,128]{3,2,1,0:T(8,128)(2,1)} %solve_group.5), calls=%async_computation.4 | async-start | bytes 4325376 | tf_op jit(solution)/shard_map/all_to_all | solution.py:1162
  237.5 0.3 copy.22
  237.8 0.8 slice.36.refs_9_
  238.8 13.8 %solve_group.3 = s16[32,17,8,128]{3,2,1,0:T(8,128)(2,1)} custom-call(s16[32,33,8,128]{3,2,1,0:T(8,128)(2,1)} %all-to-all-done.earlier_ref.refs_0_.refs_2_, s16[32,33,8,128]{3,2,1,0:T(8,128)(2,1)} %all-to-all-done.1.refs_1_.refs_3_, s16[32,33,8,128]{3,2,1,0:T(8,128)(2,1)} %all-to-all-done.earlier_ref.refs_0_.refs_2_, ...), custom_call_target="tpu_custom_call" | custom-call | flops 4026531840 | bytes 20971520 | tf_op jit(solution)/shard_map/solve_group/pallas_call | solution.py:1022
  252.6 34.3 %all-to-all-done.4.refs_1_ = s16[32,33,8,128]{3,2,1,0:T(8,128)(2,1)} async-done(((s16[32,33,8,128]{3,2,1,0:T(8,128)(2,1)}), s16[32,33,8,128]{3,2,1,0:T(8,128)(2,1)}, u32[]{:S(2)}, u32[]{:S(2)}) %all-to-all-start.4) | async-done | bytes 2162720 | tf_op jit(solution)/shard_map/all_to_all | solution.py:1162
  286.9 3.6 %all-to-all-start.2 = ((s16[32,17,8,128]{3,2,1,0:T(8,128)(2,1)}), s16[32,17,8,128]{3,2,1,0:T(8,128)(2,1)}, u32[]{:S(2)}, u32[]{:S(2)}) async-start(s16[32,17,8,128]{3,2,1,0:T(8,128)(2,1)} %solve_group.3), calls=%async_computation.2 | async-start | bytes 2228224 | tf_op jit(solution)/shard_map/all_to_all | solution.py:1162
  290.7 0.7 pad_maximum_fusion.4.refs_1_
  291.5 0.1 reduce-precision_convert_fusion
  291.6 0.9 pad_maximum_fusion.1.refs_2_
  292.5 20.0 %pressure_of.2.refs_2_ = f32[256,16,512]{2,1,0:T(8,128)} custom-call(s16[32,17,8,128]{3,2,1,0:T(8,128)(2,1)} %copy-done, s16[32,33,8,128]{3,2,1,0:T(8,128)(2,1)} %all-to-all-done.4.refs_1_, bf16[2,384,512]{2,1,0:T(8,128)(2,1)} %pad_maximum_fusion.1.refs_2_), custom_call_target="tpu_custom_call" | custom-call | flops 16106127360 | bytes 20971520 | tf_op jit(solution)/shard_map/pressure_of/pallas_call | solution.py:1134
  312.6 5.8 %all-to-all-done.2.refs_0_ = s16[32,17,8,128]{3,2,1,0:T(8,128)(2,1)} async-done(((s16[32,17,8,128]{3,2,1,0:T(8,128)(2,1)}), s16[32,17,8,128]{3,2,1,0:T(8,128)(2,1)}, u32[]{:S(2)}, u32[]{:S(2)}) %all-to-all-start.2) | async-done | bytes 1114144 | tf_op jit(solution)/shard_map/all_to_all | solution.py:1162
  318.3 11.6 %pressure_of.3 = f32[256,16,512]{2,1,0:T(8,128)} custom-call(s16[32,17,8,128]{3,2,1,0:T(8,128)(2,1)} %all-to-all-done.2.refs_0_, bf16[2,128,512]{2,1,0:T(8,128)(2,1)} %pad_maximum_fusion.4.refs_1_, f32[256,16,512]{2,1,0:T(8,128)} %pressure_of.2.refs_2_), custom_call_target="tpu_custom_call" | custom-call | flops 5368709120 | bytes 20971520 | tf_op jit(solution)/shard_map/pressure_of/pallas_call | solution.py:1134
  (19 shorter events, 0.6 us)
Async XLA Ops:
  79.4 54.5 %all-to-all-start = ((s16[32,33,8,128]{3,2,1,0:T(8,128)(2,1)}), s16[32,33,8,128]{3,2,1,0:T(8,128)(2,1)}, u32[]{:S(2)}, u32[]{:S(2)}) async-start(s16[32,33,8,128]{3,2,1,0:T(8,128)(2,1)} %get-tuple-element.14), calls=%async_computation | async-start | bytes 4325376 | tf_op jit(solution)/shard_map/all_to_all | solution.py:1162
  134.6 3.6 %copy-start.2 = (f32[64,64]{1,0:T(8,128)S(1)}, f32[64,64]{1,0:T(8,128)}, u32[]{:S(2)}) copy-start(f32[64,64]{1,0:T(8,128)} %param.18) | copy-start | bytes 49156
  134.6 4.5 %copy-start.3 = (f32[64]{0:T(128)S(1)}, f32[64]{0:T(128)}, u32[]{:S(2)}) copy-start(f32[64]{0:T(128)} %param.20) | copy-start | bytes 772
  134.6 53.3 %all-to-all-start.1 = ((s16[32,33,8,128]{3,2,1,0:T(8,128)(2,1)}), s16[32,33,8,128]{3,2,1,0:T(8,128)(2,1)}, u32[]{:S(2)}, u32[]{:S(2)}) async-start(s16[32,33,8,128]{3,2,1,0:T(8,128)(2,1)} %following.1), calls=%async_computation.1 | async-start | bytes 4325376 | tf_op jit(solution)/shard_map/all_to_all | solution.py:1162
  201.7 31.3 %all-to-all-start.3 = ((s16[32,17,8,128]{3,2,1,0:T(8,128)(2,1)}), s16[32,17,8,128]{3,2,1,0:T(8,128)(2,1)S(1)}, u32[]{:S(2)}, u32[]{:S(2)}) async-start(s16[32,17,8,128]{3,2,1,0:T(8,128)(2,1)} %solve_group.4), calls=%async_computation.3 | async-start | bytes 2228224 | tf_op jit(solution)/shard_map/all_to_all | solution.py:1162
  225.2 12.2 %copy-start.1 = (f32[512,512]{1,0:T(8,128)S(1)}, f32[512,512]{1,0:T(8,128)}, u32[]{:S(2)}) copy-start(f32[512,512]{1,0:T(8,128)} %basis_ref.3) | copy-start | bytes 3145732
  233.0 1.0 copy-start
  234.0 52.9 %all-to-all-start.4 = ((s16[32,33,8,128]{3,2,1,0:T(8,128)(2,1)}), s16[32,33,8,128]{3,2,1,0:T(8,128)(2,1)}, u32[]{:S(2)}, u32[]{:S(2)}) async-start(s16[32,33,8,128]{3,2,1,0:T(8,128)(2,1)} %solve_group.5), calls=%async_computation.4 | async-start | bytes 4325376 | tf_op jit(solution)/shard_map/all_to_all | solution.py:1162
  286.9 31.4 %all-to-all-start.2 = ((s16[32,17,8,128]{3,2,1,0:T(8,128)(2,1)}), s16[32,17,8,128]{3,2,1,0:T(8,128)(2,1)}, u32[]{:S(2)}, u32[]{:S(2)}) async-start(s16[32,17,8,128]{3,2,1,0:T(8,128)(2,1)} %solve_group.3), calls=%async_computation.2 | async-start | bytes 2228224 | tf_op jit(solution)/shard_map/all_to_all | solution.py:1162

commit v8 on v7

--- a/solution.py
+++ b/solution.py
@@ -770,7 +770,7 @@
                 wide[pl.ds(z * 2 + half, modes, stride=layers), :] = got
             return 0
 
-        lax.fori_loop(0, layers // 2, radial, 0)
+        lax.fori_loop(0, layers // 2, radial, 0, unroll=2)
         devices, slots, height, lanes = sent_ref.shape
         share = modes // devices
         most = scales[...].reshape(devices, share // height, height, lanes)
@@ -974,7 +974,7 @@
             result[k, at] = dot3((unmix[0], unmix[1]), (high[k, at], low[k, at]))
         return 0
 
-    lax.fori_loop(0, 4, waves, 0)
+    lax.fori_loop(0, 4, waves, 0, unroll=2)
 
     apart = count // together
 
@@ -1122,7 +1122,7 @@
         out[at] = total + base[0][at] if base else total
         return 0
 
-    lax.fori_loop(0, lanes // azimuths, radial, 0)
+    lax.fori_loop(0, lanes // azimuths, radial, 0, unroll=2)
 
 
 def pressure_of(got, basis, around, chunks, base=None):

time: 331 us -> 329 us (level)
  Pallas kernels: 204 us -> 200 us
where the time goes in v8:
time: 329 us; the launch traced here: 328 us
  Pallas kernels  200 us (61%)
  waiting for transfers between devices  99.9 us (30%)
  starting transfers between devices  18.8 us (6%)
  local copies, waits for them, and re-layouts  5.67 us (2%)
    all_to_all x5, waiting for transfers between devices, exchanged(): lax.all_to_all(sent, ('azim', 'axial'), split_axis=0, concat_axis=0, tile...  99.9 us
    pallas_call x2, Pallas kernels, advect_chunk(): pl.pallas_call(functools.partial(chunk_kernel, around, chunk_index, rows...  90.8 us
    pallas_call x3, Pallas kernels, solve_group(): pl.pallas_call(functools.partial(solve_kernel, around, along, chunks, sta...  45.6 us
    pallas_call x1, Pallas kernels, halos(): pl.pallas_call(halo_kernel, grid=(2 * half,), in_specs=in_specs, out_spec...  32.6 us
    pallas_call x2, Pallas kernels, pressure_of(): pl.pallas_call(functools.partial(pressure_kernel, around, groups, chunks)...  30.2 us
    all_to_all x5, starting transfers between devices, exchanged(): lax.all_to_all(sent, ('azim', 'axial'), split_axis=0, concat_axis=0, tile...  18.8 us
  transfers between devices with their start and end apart: 5, of which 5 were waited for; matrix products, arithmetic and copies ran while one was open for 2% of the time, Pallas kernels for 30%

profile of v8, /device:TPU:1, one launch (start us, length us, event | category | flops | bytes accessed | tf_op | source)
XLA Modules:
  0.0 328.2 jit_solution(3518506846404710691)
XLA Ops:
  0.6 32.6 %halos.1 = (f32[2,256,512]{2,1,0:T(8,128)}, f32[2,256,512]{2,1,0:T(8,128)}, bf16[2,5,16,512]{3,2,1,0:T(8,128)(2,1)}) custom-call(bf16[3,256,16,512]{3,2,1,0:T(8,128)(2,1)} %last_courant_ref.5, bf16[3,256,16,512]{3,2,1,0:T(8,128)(2,1)} %last_normals_ref.5, bf16[256,16,512]{2,1,0:T(8,128)(2,1)} %last_planes_ref.5, s32[256,16,512]{2,1,0:T(8,128)} %last_flags_ref.5, ...), custom_call_target="tpu_custom_call" | custom-call | tf_op jit(solution)/shard_map/halos/pallas_call | solution.py:566
  33.3 45.4 %advect_chunk.2 = (f32[256,16,512]{2,1,0:T(8,128)}, s16[32,33,8,128]{3,2,1,0:T(8,128)(2,1)}) custom-call(f32[256,16,512]{2,1,0:T(8,128)} %fraction_ref.3, bf16[3,256,16,512]{3,2,1,0:T(8,128)(2,1)} %last_normals_ref.5, bf16[256,16,512]{2,1,0:T(8,128)(2,1)} %last_planes_ref.5, s32[256,16,512]{2,1,0:T(8,128)} %last_flags_ref.5, ...), custom_call_target="tpu_custom_call" | custom-call | flops 41943040000 | bytes 31457280 | tf_op jit(solution)/shard_map/advect_chunk/pallas_call | solution.py:844
  78.7 4.8 %all-to-all-start = ((s16[32,33,8,128]{3,2,1,0:T(8,128)(2,1)}), s16[32,33,8,128]{3,2,1,0:T(8,128)(2,1)}, u32[]{:S(2)}, u32[]{:S(2)}) async-start(s16[32,33,8,128]{3,2,1,0:T(8,128)(2,1)} %get-tuple-element.14), calls=%async_computation | async-start | bytes 4325376 | tf_op jit(solution)/shard_map/all_to_all | solution.py:1162
  83.5 45.4 %advect_chunk.3 = (f32[256,16,512]{2,1,0:T(8,128)}, s16[32,33,8,128]{3,2,1,0:T(8,128)(2,1)}) custom-call(f32[256,16,512]{2,1,0:T(8,128)} %fraction_ref.3, bf16[3,256,16,512]{3,2,1,0:T(8,128)(2,1)} %last_normals_ref.5, bf16[256,16,512]{2,1,0:T(8,128)(2,1)} %last_planes_ref.5, s32[256,16,512]{2,1,0:T(8,128)} %last_flags_ref.5, ...), custom_call_target="tpu_custom_call", output_to_operand_aliasing={{0}: (17, {})} | custom-call | flops 41943040000 | bytes 31457280 | tf_op jit(solution)/shard_map/advect_chunk/pallas_call | solution.py:844
  128.9 4.3 %all-to-all-done.earlier_ref.refs_0_.refs_2_ = s16[32,33,8,128]{3,2,1,0:T(8,128)(2,1)} async-done(((s16[32,33,8,128]{3,2,1,0:T(8,128)(2,1)}), s16[32,33,8,128]{3,2,1,0:T(8,128)(2,1)}, u32[]{:S(2)}, u32[]{:S(2)}) %all-to-all-start) | async-done | bytes 2162720 | tf_op jit(solution)/shard_map/all_to_all | solution.py:1162
  133.2 0.7 following.1
  133.9 3.6 %all-to-all-start.1 = ((s16[32,33,8,128]{3,2,1,0:T(8,128)(2,1)}), s16[32,33,8,128]{3,2,1,0:T(8,128)(2,1)}, u32[]{:S(2)}, u32[]{:S(2)}) async-start(s16[32,33,8,128]{3,2,1,0:T(8,128)(2,1)} %following.1), calls=%async_computation.1 | async-start | bytes 4325376 | tf_op jit(solution)/shard_map/all_to_all | solution.py:1162
  137.6 0.8 dynamic_slice.3
  138.4 0.8 slice.37.refs_9_
  139.2 0.2 broadcast_multiply_fusion
  139.5 0.3 mul.75
  139.8 0.3 mul.72
  140.2 0.9 pad_maximum_fusion.2
  141.1 46.1 %all-to-all-done.1.refs_1_.refs_3_ = s16[32,33,8,128]{3,2,1,0:T(8,128)(2,1)} async-done(((s16[32,33,8,128]{3,2,1,0:T(8,128)(2,1)}), s16[32,33,8,128]{3,2,1,0:T(8,128)(2,1)}, u32[]{:S(2)}, u32[]{:S(2)}) %all-to-all-start.1) | async-done | bytes 2162720 | tf_op jit(solution)/shard_map/all_to_all | solution.py:1162
  187.2 13.5 %solve_group.4 = s16[32,17,8,128]{3,2,1,0:T(8,128)(2,1)} custom-call(s16[32,33,8,128]{3,2,1,0:T(8,128)(2,1)} %all-to-all-done.earlier_ref.refs_0_.refs_2_, s16[32,33,8,128]{3,2,1,0:T(8,128)(2,1)} %all-to-all-done.1.refs_1_.refs_3_, s16[32,33,8,128]{3,2,1,0:T(8,128)(2,1)} %all-to-all-done.earlier_ref.refs_0_.refs_2_, ...), custom_call_target="tpu_custom_call" | custom-call | flops 4026531840 | bytes 20971520 | tf_op jit(solution)/shard_map/solve_group/pallas_call | solution.py:1022
  200.7 3.6 %all-to-all-start.3 = ((s16[32,17,8,128]{3,2,1,0:T(8,128)(2,1)}), s16[32,17,8,128]{3,2,1,0:T(8,128)(2,1)S(1)}, u32[]{:S(2)}, u32[]{:S(2)}) async-start(s16[32,17,8,128]{3,2,1,0:T(8,128)(2,1)} %solve_group.4), calls=%async_computation.3 | async-start | bytes 2228224 | tf_op jit(solution)/shard_map/all_to_all | solution.py:1162
  204.3 0.9 slice.38.refs_9_
  205.2 18.7 %solve_group.5 = s16[32,33,8,128]{3,2,1,0:T(8,128)(2,1)} custom-call(s16[32,33,8,128]{3,2,1,0:T(8,128)(2,1)} %all-to-all-done.earlier_ref.refs_0_.refs_2_, s16[32,33,8,128]{3,2,1,0:T(8,128)(2,1)} %all-to-all-done.1.refs_1_.refs_3_, s16[32,33,8,128]{3,2,1,0:T(8,128)(2,1)} %all-to-all-done.earlier_ref.refs_0_.refs_2_, ...), custom_call_target="tpu_custom_call" | custom-call | flops 8053063680 | bytes 20971520 | tf_op jit(solution)/shard_map/solve_group/pallas_call | solution.py:1022
  223.9 8.1 %all-to-all-done.3.refs_0_ = s16[32,17,8,128]{3,2,1,0:T(8,128)(2,1)S(1)} async-done(((s16[32,17,8,128]{3,2,1,0:T(8,128)(2,1)}), s16[32,17,8,128]{3,2,1,0:T(8,128)(2,1)S(1)}, u32[]{:S(2)}, u32[]{:S(2)}) %all-to-all-start.3) | async-done | bytes 1114144 | tf_op jit(solution)/shard_map/all_to_all | solution.py:1162
  232.0 1.0 copy-done
  233.0 3.3 all-to-all-start.4
  236.3 0.3 copy.22
  236.6 0.8 slice.36.refs_9_
  237.6 13.5 %solve_group.3 = s16[32,17,8,128]{3,2,1,0:T(8,128)(2,1)} custom-call(s16[32,33,8,128]{3,2,1,0:T(8,128)(2,1)} %all-to-all-done.earlier_ref.refs_0_.refs_2_, s16[32,33,8,128]{3,2,1,0:T(8,128)(2,1)} %all-to-all-done.1.refs_1_.refs_3_, s16[32,33,8,128]{3,2,1,0:T(8,128)(2,1)} %all-to-all-done.earlier_ref.refs_0_.refs_2_, ...), custom_call_target="tpu_custom_call" | custom-call | flops 4026531840 | bytes 20971520 | tf_op jit(solution)/shard_map/solve_group/pallas_call | solution.py:1022
  251.1 34.8 %all-to-all-done.4.refs_1_ = s16[32,33,8,128]{3,2,1,0:T(8,128)(2,1)} async-done(((s16[32,33,8,128]{3,2,1,0:T(8,128)(2,1)}), s16[32,33,8,128]{3,2,1,0:T(8,128)(2,1)}, u32[]{:S(2)}, u32[]{:S(2)}) %all-to-all-start.4) | async-done | bytes 2162720 | tf_op jit(solution)/shard_map/all_to_all | solution.py:1162
  285.9 3.6 %all-to-all-start.2 = ((s16[32,17,8,128]{3,2,1,0:T(8,128)(2,1)}), s16[32,17,8,128]{3,2,1,0:T(8,128)(2,1)}, u32[]{:S(2)}, u32[]{:S(2)}) async-start(s16[32,17,8,128]{3,2,1,0:T(8,128)(2,1)} %solve_group.3), calls=%async_computation.2 | async-start | bytes 2228224 | tf_op jit(solution)/shard_map/all_to_all | solution.py:1162
  289.7 0.7 pad_maximum_fusion.4.refs_1_
  290.4 0.1 reduce-precision_convert_fusion
  290.5 0.9 pad_maximum_fusion.1.refs_2_
  291.5 19.3 %pressure_of.2.refs_2_ = f32[256,16,512]{2,1,0:T(8,128)} custom-call(s16[32,17,8,128]{3,2,1,0:T(8,128)(2,1)} %copy-done, s16[32,33,8,128]{3,2,1,0:T(8,128)(2,1)} %all-to-all-done.4.refs_1_, bf16[2,384,512]{2,1,0:T(8,128)(2,1)} %pad_maximum_fusion.1.refs_2_), custom_call_target="tpu_custom_call" | custom-call | flops 16106127360 | bytes 20971520 | tf_op jit(solution)/shard_map/pressure_of/pallas_call | solution.py:1134
  310.8 6.5 %all-to-all-done.2.refs_0_ = s16[32,17,8,128]{3,2,1,0:T(8,128)(2,1)} async-done(((s16[32,17,8,128]{3,2,1,0:T(8,128)(2,1)}), s16[32,17,8,128]{3,2,1,0:T(8,128)(2,1)}, u32[]{:S(2)}, u32[]{:S(2)}) %all-to-all-start.2) | async-done | bytes 1114144 | tf_op jit(solution)/shard_map/all_to_all | solution.py:1162
  317.3 10.9 %pressure_of.3 = f32[256,16,512]{2,1,0:T(8,128)} custom-call(s16[32,17,8,128]{3,2,1,0:T(8,128)(2,1)} %all-to-all-done.2.refs_0_, bf16[2,128,512]{2,1,0:T(8,128)(2,1)} %pad_maximum_fusion.4.refs_1_, f32[256,16,512]{2,1,0:T(8,128)} %pressure_of.2.refs_2_), custom_call_target="tpu_custom_call" | custom-call | flops 5368709120 | bytes 20971520 | tf_op jit(solution)/shard_map/pressure_of/pallas_call | solution.py:1134
  (19 shorter events, 0.6 us)
Async XLA Ops:
  78.7 54.5 %all-to-all-start = ((s16[32,33,8,128]{3,2,1,0:T(8,128)(2,1)}), s16[32,33,8,128]{3,2,1,0:T(8,128)(2,1)}, u32[]{:S(2)}, u32[]{:S(2)}) async-start(s16[32,33,8,128]{3,2,1,0:T(8,128)(2,1)} %get-tuple-element.14), calls=%async_computation | async-start | bytes 4325376 | tf_op jit(solution)/shard_map/all_to_all | solution.py:1162
  133.9 3.6 %copy-start.2 = (f32[64,64]{1,0:T(8,128)S(1)}, f32[64,64]{1,0:T(8,128)}, u32[]{:S(2)}) copy-start(f32[64,64]{1,0:T(8,128)} %param.18) | copy-start | bytes 49156
  133.9 4.5 %copy-start.3 = (f32[64]{0:T(128)S(1)}, f32[64]{0:T(128)}, u32[]{:S(2)}) copy-start(f32[64]{0:T(128)} %param.20) | copy-start | bytes 772
  133.9 53.3 %all-to-all-start.1 = ((s16[32,33,8,128]{3,2,1,0:T(8,128)(2,1)}), s16[32,33,8,128]{3,2,1,0:T(8,128)(2,1)}, u32[]{:S(2)}, u32[]{:S(2)}) async-start(s16[32,33,8,128]{3,2,1,0:T(8,128)(2,1)} %following.1), calls=%async_computation.1 | async-start | bytes 4325376 | tf_op jit(solution)/shard_map/all_to_all | solution.py:1162
  200.7 31.3 %all-to-all-start.3 = ((s16[32,17,8,128]{3,2,1,0:T(8,128)(2,1)}), s16[32,17,8,128]{3,2,1,0:T(8,128)(2,1)S(1)}, u32[]{:S(2)}, u32[]{:S(2)}) async-start(s16[32,17,8,128]{3,2,1,0:T(8,128)(2,1)} %solve_group.4), calls=%async_computation.3 | async-start | bytes 2228224 | tf_op jit(solution)/shard_map/all_to_all | solution.py:1162
  223.9 12.4 %copy-start.1 = (f32[512,512]{1,0:T(8,128)S(1)}, f32[512,512]{1,0:T(8,128)}, u32[]{:S(2)}) copy-start(f32[512,512]{1,0:T(8,128)} %basis_ref.3) | copy-start | bytes 3145732
  232.0 1.0 copy-start
  233.0 52.9 %all-to-all-start.4 = ((s16[32,33,8,128]{3,2,1,0:T(8,128)(2,1)}), s16[32,33,8,128]{3,2,1,0:T(8,128)(2,1)}, u32[]{:S(2)}, u32[]{:S(2)}) async-start(s16[32,33,8,128]{3,2,1,0:T(8,128)(2,1)} %solve_group.5), calls=%async_computation.4 | async-start | bytes 4325376 | tf_op jit(solution)/shard_map/all_to_all | solution.py:1162
  285.9 31.4 %all-to-all-start.2 = ((s16[32,17,8,128]{3,2,1,0:T(8,128)(2,1)}), s16[32,17,8,128]{3,2,1,0:T(8,128)(2,1)}, u32[]{:S(2)}, u32[]{:S(2)}) async-start(s16[32,17,8,128]{3,2,1,0:T(8,128)(2,1)} %solve_group.3), calls=%async_computation.2 | async-start | bytes 2228224 | tf_op jit(solution)/shard_map/all_to_all | solution.py:1162
